TPU v7x, 32 devices: a whole 2x2x4 slice. The times are simulated.
32 devices in a mesh: grp: 2 (over x), len: 16 (over z, y, core).
Axes of the slice: x: 2, y: 2, z: 4, core: 2. Of those that a mesh axis runs over, the one named last changes fastest.
Arguments:
- tin_temp: float32 [64, 512, 1024], P(None, ('grp', 'len')), parts along dimension 1, may hold values from -6 to 6
- flow_code: int32 [64, 512, 1024], P(None, ('grp', 'len')), parts along dimension 1, may hold values from 0 to 3
- speeds: float32 [2, 64], replicated, may hold values from 0.02 to 0.12
- floor_temp: float32 [32, 48, 64, 256], P(('grp', 'len')), parts along dimension 0, may hold values from -6 to 6
- material: int32 [32, 48, 64, 256], P(('grp', 'len')), parts along dimension 0, may hold values from 0 to 2
- conductivity: float32 [3], replicated, may hold values from 0.03 to 0.15
Outputs:
- tin_out: float32 [64, 512, 1024], P(None, ('grp', 'len')), parts along dimension 1
- floor_out: float32 [32, 48, 64, 256], P(('grp', 'len')), parts along dimension 0
There are 2 independent parts, one for each index of `grp`. A program takes and returns all parts, laid end to end along the dimension named above; an argument that names none is the same for every part. Nothing has to cross between parts.
Inputs may be any that keep to these rules, and one draw needn't show every extreme that they name: flow_code % 2 is 0 where the tin cell takes its length upwind value from the lower length index and 1 from the higher; flow_code // 2 likewise across the width. material ids index conductivity.
All inputs are finite; a program needn't handle non-finite values.
Results may differ from a plain program's by a relative error of at most 0.0003.
Values sent between devices are 32-bit elements; how exact they have to be, the bound alone decides.
No kernel may reach another device: no remote copies, remote signals or barrier semaphores. Data moves between devices by JAX's collectives and lax.ppermute only.
A program may use at most 128 MiB of HBM per device.

v0:
```python
import functools

import jax
import jax.numpy as jnp
from jax import lax
from jax.experimental import pallas as pl
from jax.experimental.pallas import tpu as pltpu
from jax.sharding import PartitionSpec as P

TILE_Y = 4
KT = 0.1
HT = 0.2
HR = 0.2
LANES = 128
SUBL = 8
F32 = jnp.float32
ANY = pl.BlockSpec(memory_space=pl.ANY)
VMEM = pl.BlockSpec(memory_space=pltpu.VMEM)
SMEM = pl.BlockSpec(memory_space=pltpu.SMEM)


def params(mib):
    return pltpu.CompilerParams(vmem_limit_bytes=mib * 1024 * 1024)


def shape(dims, dtype=F32):
    return pltpu.VMEM(dims, dtype)


def far(dims, dtype=F32):
    return pltpu.HBM(dims, dtype)


def in_hbm(*arrays):
    return [pltpu.with_memory_space_constraint(a, pltpu.HBM) for a in arrays]


def in_vmem(*arrays):
    return [pltpu.with_memory_space_constraint(a, pltpu.VMEM) for a in arrays]


def cost(flops, nbytes):
    return pl.CostEstimate(flops=flops, bytes_accessed=nbytes, transcendentals=0)


def place():
    pos = lax.axis_index("len")
    group, column = pos // TILE_Y, pos % TILE_Y
    return group, column, pos % 2 == 1, group % 2 == 1


def iotas():
    rows = lax.broadcasted_iota(jnp.int32, (SUBL, LANES), 0)
    lanes = lax.broadcasted_iota(jnp.int32, (SUBL, LANES), 1)
    return rows, lanes


def swaps(kind):
    count = lax.axis_size("len")
    partner = {
        "e1": lambda i: i ^ 1,
        "e2": lambda i: i + 1 if i % 2 else i - 1,
        "x2": lambda i: i ^ 2,
        "x3": lambda i: i ^ 3,
        "z1": lambda i: i ^ TILE_Y,
        "z2": lambda i: i + TILE_Y if (i // TILE_Y) % 2 else i - TILE_Y,
    }[kind]
    return [(i, partner(i)) for i in range(count) if 0 <= partner(i) < count]


def swap(value, kind):
    return lax.ppermute(value, "len", swaps(kind))


def select_copy(cond, first, second, sem):
    @pl.when(cond)
    def _():
        pltpu.make_async_copy(*first, sem).start()

    @pl.when(jnp.logical_not(cond))
    def _():
        pltpu.make_async_copy(*second, sem).start()


def half_lookup(ids, cond):
    value = jnp.full(ids.shape, 0.5 * cond[0], F32)
    for i in range(1, cond.shape[0]):
        value = jnp.where(ids == i, 0.5 * cond[i], value)
    return value


def wait_bytes(src, dst, sem):
    pltpu.make_async_copy(src, dst, sem).wait()


def pack_rows_kernel(u, floor, ids, cond, e2, x2, z1, z2, mrow, sem):
    g, m = floor.at[0], ids.at[0]
    group, column, odd, godd = place()
    nx, cx = u.shape[1], g.shape[1]
    nr, width = g.shape[0], g.shape[2]
    select_copy(odd, (u.at[:, nx - 1, :], e2), (u.at[:, 0, :], e2), sem.at[0])
    low, high = g.at[:, 0, :], g.at[:, cx - 1, :]
    select_copy(godd, (low, z1.at[:nr]), (high, z1.at[:nr]), sem.at[1])
    select_copy(godd, (high, z2.at[:nr]), (low, z2.at[:nr]), sem.at[2])
    rows = [(m.at[:, r, :], mrow.at[s]) for r, s in ((0, 0), (cx - 1, 1))]
    for i, (src, dst) in enumerate(rows):
        pltpu.make_async_copy(src, dst, sem.at[3 + i]).start()
    other = column ^ 2
    lane = pl.multiple_of(other * width, LANES)
    row = pl.multiple_of(other * nx, SUBL)
    planes = (
        pltpu.make_async_copy(u.at[0, :, pl.ds(lane, width)], x2.at[:nx], sem.at[5]),
        pltpu.make_async_copy(g.at[0, pl.ds(row, nx), :], x2.at[nx:], sem.at[6]),
    )
    for copy in planes:
        copy.start()
    for i, (src, dst) in enumerate(rows):
        wait_bytes(src, dst, sem.at[3 + i])
    k_low, k_high = half_lookup(mrow[0], cond), half_lookup(mrow[1], cond)
    z1[nr:, :] = jnp.where(godd, k_low, k_high)
    z2[nr:, :] = jnp.where(godd, k_high, k_low)
    wait_bytes(u.at[:, 0, :], e2, sem.at[0])
    wait_bytes(low, z1.at[:nr], sem.at[1])
    wait_bytes(low, z2.at[:nr], sem.at[2])
    for copy in planes:
        copy.wait()


def put_columns(aux, cols):
    half = cols.shape[0] // 2
    aux[half:, :LANES] = cols[:half]
    aux[half:, LANES:] = cols[half:]


def get_columns(aux):
    half = aux.shape[0] // 2
    return jnp.concatenate([aux[half:, :LANES], aux[half:, LANES:]], 0)


def put_planes(dst, b_plane, p_plane, other):
    nx, width = b_plane.shape[0], p_plane.shape[1]
    lane = pl.multiple_of(other * width, LANES)
    row = pl.multiple_of(other * nx, SUBL)
    dst[:nx, :] = b_plane[:, pl.ds(lane, width)]
    dst[nx : 2 * nx, :] = p_plane[pl.ds(row, nx), :]


def keep_columns(own, z, at_z, at_y, rs, left, right, shift):
    lanes = lax.broadcasted_iota(jnp.int32, (SUBL, LANES), 1)
    both = pltpu.roll(jnp.where(lanes == 0, left, right), z + shift, 1)
    own[0, rs, :] = jnp.where(at_z, both, own[0, rs, :])
    own[1, rs, :] = jnp.where(at_y, both, own[1, rs, :])


def prepare_kernel(
    u, floor, ids, cond, _, e1, x3, own, gv, ce, cw, cn, cz, mv, kv, b_plane, sem
):
    g, m = floor.at[0], ids.at[0]
    group, column, odd, godd = place()
    zt, nx, ny = u.shape
    nr, cx, width = g.shape
    chunks = 6
    step = nr // chunks

    def load(c):
        at = pl.ds(c * step, step)
        return (
            pltpu.make_async_copy(m.at[at], mv.at[at], sem.at[2 * c]),
            pltpu.make_async_copy(g.at[at], gv.at[at], sem.at[2 * c + 1]),
        )

    base = 2 * chunks
    plane = pltpu.make_async_copy(u.at[0], b_plane, sem.at[base])
    for copy in load(0):
        copy.start()
    rows_out = e1.at[:, :ny]
    select_copy(odd, (u.at[:, 0, :], rows_out), (u.at[:, nx - 1, :], rows_out), sem.at[base + 1])
    plane.start()
    for c in range(1, chunks):
        for copy in load(c):
            copy.start()
    rows, lanes = iotas()
    r_last, l_first, l_last = rows == SUBL - 1, lanes == 0, lanes == LANES - 1
    tiles, wide = cx // SUBL, width // LANES
    shift = LANES // 2
    scal = [0.5 * cond[i] for i in range(cond.shape[0])]
    own[...] = jnp.zeros_like(own)

    def lookup(ids):
        value = jnp.full(ids.shape, scal[0], F32)
        for i in range(1, len(scal)):
            value = jnp.where(ids == i, scal[i], value)
        return value

    def layer(z):
        at_z, at_y = lanes == z, lanes == lax.rem(z + LANES - 1, LANES)
        at_kz, at_ky = lanes == z + shift, lanes == z + shift - 1
        before = jnp.maximum(z - 1, 0)
        spans = [slice(j * LANES, (j + 1) * LANES) for j in range(wide)]

        def tile(t):
            rs = slice(t * SUBL, (t + 1) * SUBL)
            ks = [lookup(mv[z, rs, at]) for at in spans]
            return ks, [pltpu.roll(k, SUBL - 1, 0) for k in ks]

        ks, ups = tile(0)
        for t in range(tiles):
            rs = slice(t * SUBL, (t + 1) * SUBL)
            if t + 1 < tiles:
                kn, un = tile(t + 1)
            east = [pltpu.roll(k, LANES - 1, 1) for k in ks]
            west = [pltpu.roll(k, 1, 1) for k in ks]
            for j, at in enumerate(spans):
                k = ks[j]
                kv[z, rs, at] = k
                cz[before, rs, at] = kv[before, rs, at] + k
                if t + 1 < tiles:
                    cn[z, rs, at] = k + jnp.where(r_last, un[j], ups[j])
                else:
                    cn[z, rs, at] = jnp.where(r_last, 0.0, k + ups[j])
                if j + 1 < wide:
                    ce[z, rs, at] = k + jnp.where(l_last, east[j + 1], east[j])
                else:
                    ce[z, rs, at] = jnp.where(l_last, 0.0, k + east[j])
                if j > 0:
                    cw[z, rs, at] = k + jnp.where(l_first, west[j - 1], west[j])
                else:
                    cw[z, rs, at] = jnp.where(l_first, 0.0, k + west[j])
            keep_columns(own, z, at_z, at_y, rs, gv[z, rs, spans[0]], gv[z, rs, spans[-1]], 0)
            keep_columns(own, z, at_kz, at_ky, rs, ks[0], ks[-1], shift)
            if t + 1 < tiles:
                ks, ups = kn, un

    def chunk(c, _):
        for copy in load(c):
            copy.wait()
        start = c * step

        def body(i, _):
            layer(start + 2 * i)
            layer(start + 2 * i + 1)
            return 0

        return lax.fori_loop(0, step // 2, body, 0)

    lax.fori_loop(0, chunks, chunk, 0)
    cz[nr - 1, :, :] = kv[nr - 1]
    own[1, :, :] = pltpu.roll(own[1], 1, 1)
    left, right = own[0], own[1]
    aux = e1.at[:, ny:]
    put_columns(aux, jnp.where(odd, left, right))
    inner = (column > 0) & (column < TILE_Y - 1)
    put_columns(x3, jnp.where(inner, jnp.where(odd, right, left), 0.0))
    plane.wait()
    put_planes(aux, b_plane, gv.at[0], column ^ 1)
    put_planes(x3, b_plane, gv.at[0], column ^ 3)
    wait_bytes(u.at[:, 0, :], rows_out, sem.at[base + 1])


def floor_kernel(
    emit, g, ce, cw, cn, cz, u, x1, x2, x3, z1, z2, y1, y2, own, *rest
):
    nr, cx, width = g.shape
    nx, ny = u.shape[1], u.shape[2]
    if emit:
        out, own_new, o1, o2, kc, kr = rest[:6]
        ov, rest = out, rest[6:]
    else:
        kc, kr, out, ov = rest[:4]
        rest = rest[4:]
    fzv, tcol, trow, bv, sem = rest
    group, column, odd, godd = place()
    tiles, wide = cx // SUBL, width // LANES
    step = SUBL
    chunks = nr // step
    shift = LANES // 2
    aux = x1.at[:, ny:]
    one, three = get_columns(aux), get_columns(x3)
    for s, halo in ((0, jnp.where(odd, one, three)), (1, jnp.where(odd, three, one))):
        if emit:
            kc[s, :, :] = pltpu.roll(own[s] + halo, shift, 1)
        tcol[s, :, :] = kc[s] * (halo - own[s])
    for s, (mine, halo) in enumerate(((z1, y1), (z2, y2))):
        if emit:
            kr[s, :, :] = mine[nr:, :] + halo[nr:, :]
        side = kr[s] * (halo[:nr, :] - mine[:nr, :])
        trow[jnp.where(godd, s, 1 - s), :, :] = side
    row = lambda other: pl.ds(pl.multiple_of(other * nx, SUBL), nx)
    bv[row(column), :] = u[0, :, pl.ds(pl.multiple_of(column * width, LANES), width)]
    for k, ref in ((1, aux), (2, x2), (3, x3)):
        bv[row(column ^ k), :] = ref[:nx, :]
    rows, lanes = iotas()
    r_first, r_last = rows == 0, rows == SUBL - 1
    l_first, l_last = lanes == 0, lanes == LANES - 1
    fzv[...] = jnp.zeros_like(fzv)
    if emit:
        own_new[...] = jnp.zeros_like(own_new)
    spans = [slice(j * LANES, (j + 1) * LANES) for j in range(wide)]

    def layer(start, offset):
        z = start + offset
        back = lax.rem(LANES - z, LANES)
        if emit:
            at_z, at_y = lanes == z, lanes == lax.rem(z + LANES - 1, LANES)
        above = z + 1
        if offset == step - 1:
            above = jnp.minimum(above, nr - 1)
            scale = jnp.where(z + 1 < nr, 1.0, 0.0)

        def tile(t):
            rs = slice(t * SUBL, (t + 1) * SUBL)
            gs = [g[z, rs, at] for at in spans]
            return gs, [pltpu.roll(v, SUBL - 1, 0) for v in gs]

        def row_of(s):
            block = trow[s, pl.ds(start, SUBL), :][offset : offset + 1]
            return [jnp.broadcast_to(block[:, at], (SUBL, LANES)) for at in spans]

        low, high = row_of(0), row_of(1)
        gs, ups = tile(0)
        prev = [-v for v in low]
        for t in range(tiles):
            rs = slice(t * SUBL, (t + 1) * SUBL)
            if t + 1 < tiles:
                gn, un = tile(t + 1)
            east = [pltpu.roll(v, LANES - 1, 1) for v in gs]
            west = [pltpu.roll(v, 1, 1) for v in gs]
            t_west = pltpu.roll(tcol[0, rs, :], back, 1)
            t_east = pltpu.roll(tcol[1, rs, :], LANES - 1 - z, 1)
            for j, at in enumerate(spans):
                v = gs[j]
                if t + 1 < tiles:
                    fx = cn[z, rs, at] * (jnp.where(r_last, un[j], ups[j]) - v)
                else:
                    fx = jnp.where(r_last, high[j], cn[z, rs, at] * (ups[j] - v))
                turned = pltpu.roll(fx, 1, 0)
                fxm = jnp.where(r_first, prev[j], turned)
                prev[j] = turned
                yp = jnp.where(l_last, east[j + 1], east[j]) if j + 1 < wide else east[j]
                ym = jnp.where(l_first, west[j - 1], west[j]) if j > 0 else west[j]
                side = ce[z, rs, at] * (yp - v) + cw[z, rs, at] * (ym - v)
                if j == 0:
                    side = side + jnp.where(l_first, t_west, 0.0)
                if j + 1 == wide:
                    side = side + jnp.where(l_last, t_east, 0.0)
                nxt = g[above, rs, at]
                if offset == step - 1:
                    nxt = scale * nxt
                fz = cz[z, rs, at] * (nxt - v)
                total = v + ((fx - fxm) + side + (fz - fzv[rs, at]))
                fzv[rs, at] = fz
                ov[z, rs, at] = total
            if t + 1 < tiles:
                gs, ups = gn, un

    def columns(z):
        at_z, at_y = lanes == z, lanes == lax.rem(z + LANES - 1, LANES)
        for t in range(tiles):
            rs = slice(t * SUBL, (t + 1) * SUBL)
            keep_columns(own_new, z, at_z, at_y, rs, ov[z, rs, spans[0]], ov[z, rs, spans[-1]], 0)

    def store(c):
        at = pl.ds(c * step, step)
        return pltpu.make_async_copy(ov.at[at], out.at[at], sem.at[c])

    def store_rows(c):
        at = pl.ds(pl.multiple_of(c * step, SUBL), step)
        low, high = ov.at[at, 0, :], ov.at[at, cx - 1, :]
        select_copy(godd, (low, o1.at[at]), (high, o1.at[at]), sem.at[chunks + c])
        select_copy(godd, (high, o2.at[at]), (low, o2.at[at]), sem.at[2 * chunks + c])

    def chunk(c, _):
        start = pl.multiple_of(c * step, SUBL)
        for offset in range(step):
            layer(start, offset)

        @pl.when(c == 0)
        def _():
            ov[0, :, :] = ov[0] + HR * (bv[...] - g[0])

        if emit:
            store_rows(c)
            for offset in range(step):
                columns(start + offset)
        else:
            store(c).start()
        return 0

    lax.fori_loop(0, chunks, chunk, 0)
    if emit:
        own_new[1, :, :] = pltpu.roll(own_new[1], 1, 1)
    for c in range(chunks):
        if emit:
            at = pl.ds(c * step, step)
            wait_bytes(ov.at[at, 0, :], o1.at[at], sem.at[chunks + c])
            wait_bytes(ov.at[at, 0, :], o2.at[at], sem.at[2 * chunks + c])
        else:
            store(c).wait()


def floor_sweep(emit, g, coefs, u, x1, x2, x3, z1, z2, y1, y2, own, halos=()):
    nr, cx, width = g.shape
    scratch = [
        pltpu.VMEM((cx, width), F32),
        pltpu.VMEM((2, cx, LANES), F32),
        pltpu.VMEM((2, nr, width), F32),
        pltpu.VMEM((cx, width), F32),
        pltpu.SemaphoreType.DMA((3 * nr // SUBL,)),
    ]
    if emit:
        outs = [
            shape(g.shape),
            shape(own.shape),
            shape((nr, width)),
            shape((nr, width)),
            shape(own.shape),
            shape((2, nr, width)),
        ]
        specs = [VMEM] * 6
    else:
        outs, specs = [far(g.shape)], [ANY]
        scratch = [pltpu.VMEM(g.shape, F32)] + scratch
    return pl.pallas_call(
        functools.partial(floor_kernel, emit),
        out_shape=outs,
        in_specs=[VMEM] * (14 + len(halos)),
        out_specs=specs,
        scratch_shapes=scratch,
        compiler_params=params(2 if emit else 6),
        cost_estimate=cost(30 * g.size, 12 * g.size),
        name="floor_sweep",
    )(*in_vmem(g, *coefs, u, x1, x2, x3, z1, z2, y1, y2, own, *halos))


def tin_kernel(emit, u, f, e1, e2, x2, x3, g, speeds, *rest):
    zt, nx, ny = u.shape
    width = x2.shape[1]
    if emit:
        g_new, own, out, o1, o2, ox2, ox3 = rest[:7]
        ov, rest = out, rest[7:]
    else:
        out, ov = rest[:2]
        rest = rest[2:]
    pv, sem = rest
    group, column, odd, godd = place()
    step = SUBL
    chunks = zt // step
    lanes_at = lambda other: pl.ds(pl.multiple_of(other * width, LANES), width)
    pv[:, lanes_at(column)] = g[0, pl.ds(pl.multiple_of(column * nx, SUBL), nx), :]
    for k, ref in ((1, e1.at[:, ny:]), (2, x2), (3, x3)):
        pv[:, lanes_at(column ^ k)] = ref[nx : 2 * nx, :]
    rows, lanes = iotas()
    r_first, r_last = rows == 0, rows == SUBL - 1
    l_first, l_last = lanes == 0, lanes == LANES - 1
    tiles, wide = nx // SUBL, ny // LANES
    zero = jnp.zeros((SUBL, LANES), F32)

    def layer(start, offset):
        z = start + offset
        sx, sy = speeds[0, z], speeds[1, z]
        centre = 1.0 - 6.0 * KT - sx - sy - jnp.where(z == 0, HT, 0.0)
        above, below = jnp.minimum(z + 1, zt - 1), jnp.maximum(z - 1, 0)

        def get(ref, z_, t, j):
            return ref[z_, t * SUBL : (t + 1) * SUBL, j * LANES : (j + 1) * LANES]

        left = [zero] * tiles
        now = [get(u, z, t, 0) for t in range(tiles)]
        turned = [pltpu.roll(v, LANES - 1, 1) for v in now]
        for j in range(wide):
            at = slice(j * LANES, (j + 1) * LANES)
            if j + 1 < wide:
                nxt = [get(u, z, t, j + 1) for t in range(tiles)]
                nxt_turned = [pltpu.roll(v, LANES - 1, 1) for v in nxt]
            else:
                nxt, nxt_turned = None, [zero] * tiles
            one = e1[pl.ds(start, SUBL), at][offset : offset + 1]
            two = e2[pl.ds(start, SUBL), at][offset : offset + 1]
            low = jnp.broadcast_to(jnp.where(odd, one, two), (SUBL, LANES))
            high = jnp.broadcast_to(jnp.where(odd, two, one), (SUBL, LANES))
            downs = [low] + [pltpu.roll(v, 1, 0) for v in now]
            ups = [pltpu.roll(v, SUBL - 1, 0) for v in now] + [high]
            for t in range(tiles):
                v = now[t]
                xm = jnp.where(r_first, downs[t], downs[t + 1])
                xp = jnp.where(r_last, ups[t + 1], ups[t])
                turn = pltpu.roll(v, 1, 1)
                ym = jnp.where(l_first, left[t], turn)
                yp = jnp.where(l_last, nxt_turned[t], turned[t])
                left[t] = turn
                code = get(f, z, t, j)
                xs = jnp.where((code & 1) == 0, xm, xp)
                ys = jnp.where(code < 2, ym, yp)
                spread = (xm + xp) + (ym + yp) + (get(u, above, t, j) + get(u, below, t, j))
                ov[z, t * SUBL : (t + 1) * SUBL, at] = (
                    (centre * v + KT * spread) + (sx * xs + sy * ys)
                )
            now, turned = nxt, nxt_turned

    def store(c):
        at = pl.ds(c * step, step)
        return pltpu.make_async_copy(ov.at[at], out.at[at], sem.at[c])

    def store_rows(c):
        at = pl.ds(pl.multiple_of(c * step, SUBL), step)
        low, high = ov.at[at, 0, :], ov.at[at, nx - 1, :]
        to1, to2 = o1.at[at, :ny], o2.at[at]
        select_copy(odd, (low, to1), (high, to1), sem.at[c])
        select_copy(odd, (high, to2), (low, to2), sem.at[chunks + c])

    def chunk(c, _):
        start = pl.multiple_of(c * step, SUBL)
        for offset in range(step):
            layer(start, offset)

        @pl.when(c == 0)
        def _():
            ov[0, :, :] = ov[0] + HT * pv[...]

        if emit:
            store_rows(c)
        else:
            store(c).start()
        return 0

    lax.fori_loop(0, chunks, chunk, 0)
    if emit:
        aux = o1.at[:, ny:]
        put_columns(aux, jnp.where(odd, own[0], own[1]))
        inner = (column > 0) & (column < TILE_Y - 1)
        put_columns(ox3, jnp.where(inner, jnp.where(odd, own[1], own[0]), 0.0))
        for k, ref in ((1, aux), (2, ox2), (3, ox3)):
            put_planes(ref, ov.at[0], g_new.at[0], column ^ k)
    for c in range(chunks):
        if emit:
            at = pl.ds(c * step, step)
            wait_bytes(ov.at[at, 0, :], o1.at[at, :ny], sem.at[c])
            wait_bytes(ov.at[at, 0, :], o2.at[at], sem.at[chunks + c])
        else:
            store(c).wait()


def tin_sweep(emit, u, f, e1, e2, x2, x3, g, speeds, own=()):
    zt, nx, ny = u.shape
    scratch = [pltpu.VMEM((nx, ny), F32), pltpu.SemaphoreType.DMA((2 * zt // SUBL,))]
    if emit:
        outs = [shape(v.shape) for v in (u, e1, e2, x2, x3)]
        specs = [VMEM] * 5
    else:
        outs, specs = [far(u.shape)], [ANY]
        scratch = [pltpu.VMEM(u.shape, F32)] + scratch
    return pl.pallas_call(
        functools.partial(tin_kernel, emit),
        out_shape=outs,
        in_specs=[VMEM] * 7 + [SMEM] + [VMEM] * len(own),
        out_specs=specs,
        scratch_shapes=scratch,
        compiler_params=params(2 if emit else 6),
        cost_estimate=cost(30 * u.size, 12 * u.size),
        name="tin_sweep",
    )(*in_vmem(u, f, e1, e2, x2, x3, g), speeds, *in_vmem(*own))


def local(tin_temp, flow_code, speeds, floor_temp, material, conductivity):
    u, f, g, m = tin_temp, flow_code, floor_temp[0], material[0]
    zt, nx, ny = u.shape
    nr, cx, width = g.shape
    e2, x2, z1, z2 = pl.pallas_call(
        pack_rows_kernel,
        out_shape=[
            shape((zt, ny)),
            shape((2 * nx, width)),
            shape((2 * nr, width)),
            shape((2 * nr, width)),
        ],
        in_specs=[ANY, ANY, ANY, SMEM],
        out_specs=[VMEM] * 4,
        scratch_shapes=[pltpu.VMEM((2, nr, width), jnp.int32), pltpu.SemaphoreType.DMA((7,))],
        compiler_params=params(2),
        cost_estimate=cost(0, 1 << 20),
        name="pack_rows",
    )(*in_hbm(u, floor_temp, material), conductivity)
    e2, x2 = swap(e2, "e2"), swap(x2, "x2")
    y1, y2 = swap(z1, "z1"), swap(z2, "z2")
    e1, x3, own, gv, *coefs = pl.pallas_call(
        prepare_kernel,
        out_shape=[
            shape((zt, ny + 2 * LANES)),
            shape((cx, 2 * LANES)),
            shape((2, cx, LANES)),
        ]
        + [shape(g.shape)] * 5,
        in_specs=[ANY, ANY, ANY, SMEM, ANY],
        out_specs=[VMEM] * 8,
        scratch_shapes=[
            pltpu.VMEM(g.shape, jnp.int32),
            pltpu.VMEM(g.shape, F32),
            pltpu.VMEM((nx, ny), F32),
            pltpu.SemaphoreType.DMA((14,)),
        ],
        compiler_params=params(10),
        cost_estimate=cost(0, 8 * g.size),
        name="prepare",
    )(*in_hbm(u, floor_temp, material), conductivity, z1)
    e1, x3 = swap(e1, "e1"), swap(x3, "x3")
    g1, own1, z1, z2, kc, kr = floor_sweep(
        True, gv, coefs, u, e1, x2, x3, z1, z2, y1, y2, own
    )
    y1, y2 = swap(z1, "z1"), swap(z2, "z2")
    u1, e1, e2, x2, x3 = tin_sweep(
        True, u, f, e1, e2, x2, x3, gv, speeds, (g1, own1)
    )
    e2 = swap(e2, "e2")
    e1, x2, x3 = swap(e1, "e1"), swap(x2, "x2"), swap(x3, "x3")
    (g2,) = floor_sweep(
        False, g1, coefs, u1, e1, x2, x3, z1, z2, y1, y2, own1, (kc, kr)
    )
    (u2,) = tin_sweep(False, u1, f, e1, e2, x2, x3, g1, speeds)
    return u2, g2[None]


def solution(mesh):
    placed = (
        P(None, ("grp", "len"), None),
        P(None, ("grp", "len"), None),
        P(),
        P(("grp", "len"), None, None, None),
        P(("grp", "len"), None, None, None),
        P(),
    )
    return jax.shard_map(
        local,
        mesh=mesh,
        in_specs=placed,
        out_specs=(P(None, ("grp", "len"), None), P(("grp", "len"), None, None, None)),
        check_vma=False,
    )
```

profile of v0, /device:TPU:8, one launch (start us, length us, event | category | flops | bytes accessed | tf_op | source)
XLA Modules:
  0.0 60.5 jit_solution(6454910432370439811)
XLA Ops:
  0.6 0.0 copy-start.3
  0.6 0.6 %copy-done.3 = f32[3]{0:T(128)S(1)} copy-done((f32[3]{0:T(128)S(1)}, f32[3]{0:T(128)}, u32[]{:S(2)}) %copy-start.3) | copy-done | bytes 36
  1.3 0.0 copy-start.4
  1.3 1.7 %pack_rows.1 = (f32[64,1024]{1,0:T(8,128)S(1)}, f32[32,256]{1,0:T(8,128)S(1)}, f32[96,256]{1,0:T(8,128)S(1)}, f32[96,256]{1,0:T(8,128)S(1)}) custom-call(f32[64,16,1024]{2,1,0:T(8,128)} %u.7, f32[1,48,64,256]{3,2,1,0:T(8,128)} %floor.3, s32[1,48,64,256]{3,2,1,0:T(8,128)} %ids.3, f32[3]{0:T(128)S(1)} %copy-done.3), custom_call_target="tpu_custom_call" | custom-call | bytes 1048576 | tf_op jit(solution)/shard_map/pack_rows/pallas_call | solution.py:568
  3.0 0.0 copy-done.4
  3.0 0.0 copy-start
  3.0 6.4 %prepare.1 = (f32[64,1280]{1,0:T(8,128)S(1)}, f32[64,256]{1,0:T(8,128)S(1)}, f32[2,64,128]{2,1,0:T(8,128)S(1)}, f32[48,64,256]{2,1,0:T(8,128)S(1)}, f32[48,64,25...) custom-call(f32[64,16,1024]{2,1,0:T(8,128)} %u.7, ...), custom_call_target="tpu_custom_call" | custom-call | bytes 6291456 | tf_op jit(solution)/shard_map/prepare/pallas_call | solution.py:585
  9.3 0.1 collective-permute-start
  9.4 3.4 %collective-permute-start.1 = (f32[64,1024]{1,0:T(8,128)S(1)}, f32[64,1024]{1,0:T(8,128)S(1)}, u32[]{:S(2)}, u32[]{:S(2)}) collective-permute-start(f32[64,1024]{1,0:T(8,128)S(1)} %get-tuple-element.27), channel_id=1, source_target_pairs={{1,2},{2,1},{3,4},{4,3},{5,6},{6,5},{7,8},{8,7},{9,10},{10,9},{11,... | collective-permute-start | bytes 786440 | tf_op jit(solution)/shard_map/ppermute | solution.py:72
  12.8 0.7 %collective-permute-start.2 = (f32[32,256]{1,0:T(8,128)S(1)}, f32[32,256]{1,0:T(8,128)S(1)}, u32[]{:S(2)}, u32[]{:S(2)}) collective-permute-start(f32[32,256]{1,0:T(8,128)S(1)} %get-tuple-element.28), channel_id=1, source_target_pairs={{0,2},{1,3},{2,0},{3,1},{4,6},{5,7},{6,4},{7,5},{8,10},{9,11},{10,... | collective-permute-start | bytes 98312 | tf_op jit(solution)/shard_map/ppermute | solution.py:72
  13.5 0.0 collective-permute-start.4
  13.5 5.0 %collective-permute-start.5 = (f32[96,256]{1,0:T(8,128)S(1)}, f32[96,256]{1,0:T(8,128)S(1)}, u32[]{:S(2)}, u32[]{:S(2)}) collective-permute-start(f32[96,256]{1,0:T(8,128)S(1)} %get-tuple-element.35.z2), channel_id=1, source_target_pairs={{4,8},{5,9},{6,10},{7,11},{8,4},{9,5},{10,6},{11,7},{20,24},{21,25... | collective-permute-start | bytes 294920 | tf_op jit(solution)/shard_map/ppermute | solution.py:72
  18.6 2.7 %collective-permute-done.2.x2 = f32[32,256]{1,0:T(8,128)S(1)} collective-permute-done((f32[32,256]{1,0:T(8,128)S(1)}, f32[32,256]{1,0:T(8,128)S(1)}, u32[]{:S(2)}, u32[]{:S(2)}) %collective-permute-start.2) | collective-permute-done | bytes 32800 | tf_op jit(solution)/shard_map/ppermute | solution.py:72
  21.3 0.6 collective-permute-start.3
  21.9 3.1 %collective-permute-done.3.x3 = f32[64,256]{1,0:T(8,128)S(1)} collective-permute-done((f32[64,256]{1,0:T(8,128)S(1)}, f32[64,256]{1,0:T(8,128)S(1)}, u32[]{:S(2)}, u32[]{:S(2)}) %collective-permute-start.3) | collective-permute-done | bytes 65568 | tf_op jit(solution)/shard_map/ppermute | solution.py:72
  25.0 0.0 collective-permute-done.4.y1
  25.0 0.0 collective-permute-done.5.y2
  25.0 0.0 collective-permute-done.x1.e1
  25.0 0.0 copy-done
  25.0 0.0 copy-start.1
  25.0 0.0 copy-start.2
  25.0 4.5 %floor_sweep.2 = (f32[48,64,256]{2,1,0:T(8,128)S(1)}, f32[2,64,128]{2,1,0:T(8,128)S(1)}, f32[48,256]{1,0:T(8,128)S(1)}, f32[48,256]{1,0:T(8,128)S(1)}, f32[2,64,...) custom-call(f32[48,64,256]{2,1,0:T(8,128)S(1)} %get-tuple-element.30.g, f32[48,64,256]{2,1,0:T(8,128)S(1)} %get-tuple-element.31.ce, ...), custom_call_target="tpu_custom_call" | custom-call | flops 23592960 | bytes 9437184 | tf_op jit(solution)/shard_map/floor_sweep/pallas_call | solution.py:423
  29.6 0.0 collective-permute-done.1.e2
  29.6 0.0 copy-done.1
  29.6 0.0 copy-done.2
  29.6 5.2 %tin_sweep.2 = (f32[64,16,1024]{2,1,0:T(8,128)S(1)}, f32[64,1280]{1,0:T(8,128)S(1)}, f32[64,1024]{1,0:T(8,128)S(1)}, f32[32,256]{1,0:T(8,128)S(1)}, f32[64,256]{1,0:T(8,128)S(1)}) custom-call(f32[64,16,1024]{2,1,0:T(8,128)S(1)} %copy-done, s32[64,16,1024]{2,1,0:T(8,128)S(1)} %copy-done.1, f32[64,1280]{1,0:T(8,128)S(1)} %collective-permute-done.x1.e1, ...), custom_call_target="tpu_custom_call" | custom-call | flops 31457280 | bytes 12582912 | tf_op jit(solution)/shard_map/tin_sweep/pallas_call | solution.py:552
  34.8 0.1 collective-permute-start.6
  34.9 2.1 %collective-permute-start.7 = (f32[64,1024]{1,0:T(8,128)S(1)}, f32[64,1024]{1,0:T(8,128)S(1)}, u32[]{:S(2)}, u32[]{:S(2)}) collective-permute-start(f32[64,1024]{1,0:T(8,128)S(1)} %get-tuple-element.41), channel_id=1, source_target_pairs={{1,2},{2,1},{3,4},{4,3},{5,6},{6,5},{7,8},{8,7},{9,10},{10,9},{11,... | collective-permute-start | bytes 786440 | tf_op jit(solution)/shard_map/ppermute | solution.py:72
  36.9 2.0 %collective-permute-start.8 = (f32[32,256]{1,0:T(8,128)S(1)}, f32[32,256]{1,0:T(8,128)S(1)}, u32[]{:S(2)}, u32[]{:S(2)}) collective-permute-start(f32[32,256]{1,0:T(8,128)S(1)} %get-tuple-element.42), channel_id=1, source_target_pairs={{0,2},{1,3},{2,0},{3,1},{4,6},{5,7},{6,4},{7,5},{8,10},{9,11},{10,... | collective-permute-start | bytes 98312 | tf_op jit(solution)/shard_map/ppermute | solution.py:72
  39.0 0.7 %collective-permute-start.9 = (f32[64,256]{1,0:T(8,128)S(1)}, f32[64,256]{1,0:T(8,128)S(1)}, u32[]{:S(2)}, u32[]{:S(2)}) collective-permute-start(f32[64,256]{1,0:T(8,128)S(1)} %get-tuple-element.43), channel_id=1, source_target_pairs={{0,3},{1,2},{2,1},{3,0},{4,7},{5,6},{6,5},{7,4},{8,11},{9,10},{10,... | collective-permute-start | bytes 196616 | tf_op jit(solution)/shard_map/ppermute | solution.py:72
  39.7 0.4 collective-permute-start.10
  40.1 7.3 %collective-permute-done.8.x2 = f32[32,256]{1,0:T(8,128)S(1)} collective-permute-done((f32[32,256]{1,0:T(8,128)S(1)}, f32[32,256]{1,0:T(8,128)S(1)}, u32[]{:S(2)}, u32[]{:S(2)}) %collective-permute-start.8) | collective-permute-done | bytes 32800 | tf_op jit(solution)/shard_map/ppermute | solution.py:72
  47.4 3.5 %collective-permute-start.11 = (f32[48,256]{1,0:T(8,128)S(1)}, f32[48,256]{1,0:T(8,128)S(1)}, u32[]{:S(2)}, u32[]{:S(2)}) collective-permute-start(f32[48,256]{1,0:T(8,128)S(1)} %get-tuple-element.45.z2), channel_id=1, source_target_pairs={{4,8},{5,9},{6,10},{7,11},{8,4},{9,5},{10,6},{11,7},{20,24},{21,25... | collective-permute-start | bytes 147464 | tf_op jit(solution)/shard_map/ppermute | solution.py:72
  50.9 0.0 collective-permute-done.9.x3
  50.9 0.0 collective-permute-done.7.e2
  50.9 0.0 collective-permute-done.6.e1.x1
  50.9 5.3 %tin_sweep.3 = f32[64,16,1024]{2,1,0:T(8,128)} custom-call(f32[64,16,1024]{2,1,0:T(8,128)S(1)} %get-tuple-element.39.u, s32[64,16,1024]{2,1,0:T(8,128)S(1)} %copy-done.1, f32[64,1280]{1,0:T(8,128)S(1)} %collective-permute-done.6.e1.x1, f32[64,1024]{1,0:T(8,128)S(1)} %collective-permute-done.7.e2, f32[32,256]{1,0:T(8,128)S(1)} %collective-permute-done.8.x2, ...), custom_call_target="tpu_custom_call" | custom-call | flops 31457280 | bytes 12582912 | tf_op jit(solution)/shard_map/tin_sweep/pallas_call | solution.py:552
  56.3 0.0 collective-permute-done.10.y1
  56.3 0.0 collective-permute-done.11.y2
  56.3 4.2 %floor_sweep.3 = f32[48,64,256]{2,1,0:T(8,128)} custom-call(f32[48,64,256]{2,1,0:T(8,128)S(1)} %get-tuple-element.37.rest_0_.g, f32[48,64,256]{2,1,0:T(8,128)S(1)} %get-tuple-element.31.ce, f32[48,64,256]{2,1,0:T(8,128)S(1)} %get-tuple-element.32.cw, f32[48,64,256]{2,1,0:T(8,128)S(1)} %get-tuple-element.33.cn, f32[48,64,256]{2,1,0:T(8,128)S(1)} %get-tuple-element.34.cz, ...), custom_call_target="tpu_custom_call" | custom-call | flops 23592960 | bytes 9437184 | tf_op jit(solution)/shard_map/floor_sweep/pallas_call | solution.py:423
Async XLA Ops:
  0.6 0.7 %copy-start.3 = (f32[3]{0:T(128)S(1)}, f32[3]{0:T(128)}, u32[]{:S(2)}) copy-start(f32[3]{0:T(128)} %cond.3) | copy-start | bytes 40
  1.3 1.7 %copy-start.4 = (f32[3]{0:T(128)S(1)}, f32[3]{0:T(128)}, u32[]{:S(2)}) copy-start(f32[3]{0:T(128)} %cond.3) | copy-start | bytes 40
  3.0 22.0 %copy-start = (f32[64,16,1024]{2,1,0:T(8,128)S(1)}, f32[64,16,1024]{2,1,0:T(8,128)}, u32[]{:S(2)}) copy-start(f32[64,16,1024]{2,1,0:T(8,128)} %u.7) | copy-start | bytes 12582916
  9.3 15.6 %collective-permute-start = (f32[64,1280]{1,0:T(8,128)S(1)}, f32[64,1280]{1,0:T(8,128)S(1)}, u32[]{:S(2)}, u32[]{:S(2)}) collective-permute-start(f32[64,1280]{1,0:T(8,128)S(1)} %get-tuple-element.26), channel_id=1, source_target_pairs={{0,1},{1,0},{2,3},{3,2},{4,5},{5,4},{6,7},{7,6},{8,9},{9,8},{10,11... | collective-permute-start | bytes 983048 | tf_op jit(solution)/shard_map/ppermute | solution.py:72
  9.4 20.1 %collective-permute-start.1 = (f32[64,1024]{1,0:T(8,128)S(1)}, f32[64,1024]{1,0:T(8,128)S(1)}, u32[]{:S(2)}, u32[]{:S(2)}) collective-permute-start(f32[64,1024]{1,0:T(8,128)S(1)} %get-tuple-element.27), channel_id=1, source_target_pairs={{1,2},{2,1},{3,4},{4,3},{5,6},{6,5},{7,8},{8,7},{9,10},{10,9},{11,... | collective-permute-start | bytes 786440 | tf_op jit(solution)/shard_map/ppermute | solution.py:72
  12.8 8.5 %collective-permute-start.2 = (f32[32,256]{1,0:T(8,128)S(1)}, f32[32,256]{1,0:T(8,128)S(1)}, u32[]{:S(2)}, u32[]{:S(2)}) collective-permute-start(f32[32,256]{1,0:T(8,128)S(1)} %get-tuple-element.28), channel_id=1, source_target_pairs={{0,2},{1,3},{2,0},{3,1},{4,6},{5,7},{6,4},{7,5},{8,10},{9,11},{10,... | collective-permute-start | bytes 98312 | tf_op jit(solution)/shard_map/ppermute | solution.py:72
  13.5 11.5 %collective-permute-start.4 = (f32[96,256]{1,0:T(8,128)S(1)}, f32[96,256]{1,0:T(8,128)S(1)}, u32[]{:S(2)}, u32[]{:S(2)}) collective-permute-start(f32[96,256]{1,0:T(8,128)S(1)} %get-tuple-element.25._.z1), channel_id=1, source_target_pairs={{0,4},{1,5},{2,6},{3,7},{4,0},{5,1},{6,2},{7,3},{8,12},{9,13},{10,... | collective-permute-start | bytes 294920 | tf_op jit(solution)/shard_map/ppermute | solution.py:72
  13.5 11.5 %collective-permute-start.5 = (f32[96,256]{1,0:T(8,128)S(1)}, f32[96,256]{1,0:T(8,128)S(1)}, u32[]{:S(2)}, u32[]{:S(2)}) collective-permute-start(f32[96,256]{1,0:T(8,128)S(1)} %get-tuple-element.35.z2), channel_id=1, source_target_pairs={{4,8},{5,9},{6,10},{7,11},{8,4},{9,5},{10,6},{11,7},{20,24},{21,25... | collective-permute-start | bytes 294920 | tf_op jit(solution)/shard_map/ppermute | solution.py:72
  21.3 3.7 %collective-permute-start.3 = (f32[64,256]{1,0:T(8,128)S(1)}, f32[64,256]{1,0:T(8,128)S(1)}, u32[]{:S(2)}, u32[]{:S(2)}) collective-permute-start(f32[64,256]{1,0:T(8,128)S(1)} %get-tuple-element.29), channel_id=1, source_target_pairs={{0,3},{1,2},{2,1},{3,0},{4,7},{5,6},{6,5},{7,4},{8,11},{9,10},{10,... | collective-permute-start | bytes 196616 | tf_op jit(solution)/shard_map/ppermute | solution.py:72
  25.0 4.6 %copy-start.1 = (s32[64,16,1024]{2,1,0:T(8,128)S(1)}, s32[64,16,1024]{2,1,0:T(8,128)}, u32[]{:S(2)}) copy-start(s32[64,16,1024]{2,1,0:T(8,128)} %f.3) | copy-start | bytes 12582916
  25.0 4.6 %copy-start.2 = (f32[2,64]{1,0:T(2,128)S(1)}, f32[2,64]{1,0:T(2,128)}, u32[]{:S(2)}) copy-start(f32[2,64]{1,0:T(2,128)} %speeds.3) | copy-start | bytes 1540
  34.8 16.2 %collective-permute-start.6 = (f32[64,1280]{1,0:T(8,128)S(1)}, f32[64,1280]{1,0:T(8,128)S(1)}, u32[]{:S(2)}, u32[]{:S(2)}) collective-permute-start(f32[64,1280]{1,0:T(8,128)S(1)} %get-tuple-element.40), channel_id=1, source_target_pairs={{0,1},{1,0},{2,3},{3,2},{4,5},{5,4},{6,7},{7,6},{8,9},{9,8},{10,11... | collective-permute-start | bytes 983048 | tf_op jit(solution)/shard_map/ppermute | solution.py:72
  34.9 16.1 %collective-permute-start.7 = (f32[64,1024]{1,0:T(8,128)S(1)}, f32[64,1024]{1,0:T(8,128)S(1)}, u32[]{:S(2)}, u32[]{:S(2)}) collective-permute-start(f32[64,1024]{1,0:T(8,128)S(1)} %get-tuple-element.41), channel_id=1, source_target_pairs={{1,2},{2,1},{3,4},{4,3},{5,6},{6,5},{7,8},{8,7},{9,10},{10,9},{11,... | collective-permute-start | bytes 786440 | tf_op jit(solution)/shard_map/ppermute | solution.py:72
  36.9 10.5 %collective-permute-start.8 = (f32[32,256]{1,0:T(8,128)S(1)}, f32[32,256]{1,0:T(8,128)S(1)}, u32[]{:S(2)}, u32[]{:S(2)}) collective-permute-start(f32[32,256]{1,0:T(8,128)S(1)} %get-tuple-element.42), channel_id=1, source_target_pairs={{0,2},{1,3},{2,0},{3,1},{4,6},{5,7},{6,4},{7,5},{8,10},{9,11},{10,... | collective-permute-start | bytes 98312 | tf_op jit(solution)/shard_map/ppermute | solution.py:72
  39.0 12.0 %collective-permute-start.9 = (f32[64,256]{1,0:T(8,128)S(1)}, f32[64,256]{1,0:T(8,128)S(1)}, u32[]{:S(2)}, u32[]{:S(2)}) collective-permute-start(f32[64,256]{1,0:T(8,128)S(1)} %get-tuple-element.43), channel_id=1, source_target_pairs={{0,3},{1,2},{2,1},{3,0},{4,7},{5,6},{6,5},{7,4},{8,11},{9,10},{10,... | collective-permute-start | bytes 196616 | tf_op jit(solution)/shard_map/ppermute | solution.py:72
  39.7 16.6 %collective-permute-start.10 = (f32[48,256]{1,0:T(8,128)S(1)}, f32[48,256]{1,0:T(8,128)S(1)}, u32[]{:S(2)}, u32[]{:S(2)}) collective-permute-start(f32[48,256]{1,0:T(8,128)S(1)} %get-tuple-element.44.z1), channel_id=1, source_target_pairs={{0,4},{1,5},{2,6},{3,7},{4,0},{5,1},{6,2},{7,3},{8,12},{9,13},{10,... | collective-permute-start | bytes 147464 | tf_op jit(solution)/shard_map/ppermute | solution.py:72
  47.4 8.9 %collective-permute-start.11 = (f32[48,256]{1,0:T(8,128)S(1)}, f32[48,256]{1,0:T(8,128)S(1)}, u32[]{:S(2)}, u32[]{:S(2)}) collective-permute-start(f32[48,256]{1,0:T(8,128)S(1)} %get-tuple-element.45.z2), channel_id=1, source_target_pairs={{4,8},{5,9},{6,10},{7,11},{8,4},{9,5},{10,6},{11,7},{20,24},{21,25... | collective-permute-start | bytes 147464 | tf_op jit(solution)/shard_map/ppermute | solution.py:72
where the time goes:
time: 60.8 us; the launch traced here: 60.5 us
  Pallas kernels  27.3 us (45%)
  starting transfers between devices  18.6 us (31%)
  waiting for transfers between devices  13.1 us (22%)
  between operations  0.84 us (1%)
  local copies, waits for them, and re-layouts  0.67 us (1%)
    ppermute x12, starting transfers between devices, swap(): return lax.ppermute(value, 'len', swaps(kind))  18.6 us
    ppermute x12, waiting for transfers between devices, swap(): return lax.ppermute(value, 'len', swaps(kind))  13.1 us
    pallas_call x2, Pallas kernels, tin_sweep(): pl.pallas_call(functools.partial(tin_kernel, emit), out_shape=outs, in_sp...  10.5 us
    pallas_call x2, Pallas kernels, floor_sweep(): pl.pallas_call(functools.partial(floor_kernel, emit), out_shape=outs, in_...  8.77 us
    pallas_call x1, Pallas kernels, local(): pl.pallas_call(prepare_kernel, out_shape=[shape((zt, ny + 2 * LANES)), sh...  6.37 us
    pallas_call x1, Pallas kernels, local(): pl.pallas_call(pack_rows_kernel, out_shape=[shape((zt, ny)), shape((2 * n...  1.66 us
  transfers between devices with their start and end apart: 12, of which 3 were waited for; matrix products, arithmetic and copies ran while one was open for 0% of the time, Pallas kernels for 16%

commit v1 on v0

v1 whole, which is shorter than its diff:
```python
import functools

import jax
import jax.numpy as jnp
from jax import lax
from jax.experimental import pallas as pl
from jax.experimental.pallas import tpu as pltpu
from jax.sharding import PartitionSpec as P

TILE_Y = 4
KT = 0.1
HT = 0.2
HR = 0.2
LANES = 128
SUBL = 8
F32 = jnp.float32
ANY = pl.BlockSpec(memory_space=pl.ANY)
VMEM = pl.BlockSpec(memory_space=pltpu.VMEM)
SMEM = pl.BlockSpec(memory_space=pltpu.SMEM)


def params(mib):
    return pltpu.CompilerParams(vmem_limit_bytes=mib * 1024 * 1024)


def shape(dims, dtype=F32):
    return pltpu.VMEM(dims, dtype)


def far(dims, dtype=F32):
    return pltpu.HBM(dims, dtype)


def in_hbm(*arrays):
    return [pltpu.with_memory_space_constraint(a, pltpu.HBM) for a in arrays]


def in_vmem(*arrays):
    return [pltpu.with_memory_space_constraint(a, pltpu.VMEM) for a in arrays]


def cost(flops, nbytes):
    return pl.CostEstimate(flops=flops, bytes_accessed=nbytes, transcendentals=0)


def place():
    pos = lax.axis_index("len")
    group, column = pos // TILE_Y, pos % TILE_Y
    return group, column, pos % 2 == 1, group % 2 == 1


def iotas():
    rows = lax.broadcasted_iota(jnp.int32, (SUBL, LANES), 0)
    lanes = lax.broadcasted_iota(jnp.int32, (SUBL, LANES), 1)
    return rows, lanes


def partner(kind, pos):
    return {
        "e1": lambda: pos ^ 1,
        "e2": lambda: pos + 1 if pos % 2 else pos - 1,
        "x2": lambda: pos ^ 2,
        "z1": lambda: pos ^ TILE_Y,
        "z2": lambda: pos + TILE_Y if (pos // TILE_Y) % 2 else pos - TILE_Y,
    }[kind]()


def swap(value, kind):
    count, parts = lax.axis_size("len"), lax.axis_size("grp")
    pairs = []
    for part in range(parts):
        for pos in range(count):
            to, other = part, partner(kind, pos)
            if not 0 <= other < count:
                to, other = (part ^ 1, pos) if kind == "e2" else (part, pos ^ 1)
            if 0 <= to < parts:
                pairs.append((part * count + pos, to * count + other))
    return lax.ppermute(value, ("grp", "len"), pairs)


def select_copy(cond, first, second, sem):
    @pl.when(cond)
    def _():
        pltpu.make_async_copy(*first, sem).start()

    @pl.when(jnp.logical_not(cond))
    def _():
        pltpu.make_async_copy(*second, sem).start()


def half_lookup(ids, cond):
    value = jnp.full(ids.shape, 0.5 * cond[0], F32)
    for i in range(1, cond.shape[0]):
        value = jnp.where(ids == i, 0.5 * cond[i], value)
    return value


def wait_bytes(src, dst, sem):
    pltpu.make_async_copy(src, dst, sem).wait()


def put_columns(aux, cols):
    half = cols.shape[0] // 2
    aux[half:, :LANES] = cols[:half]
    aux[half:, LANES:] = cols[half:]


def get_columns(aux):
    half = aux.shape[0] // 2
    return jnp.concatenate([aux[half:, :LANES], aux[half:, LANES:]], 0)


def put_planes(dst, b_plane, p_plane, other):
    nx, width = b_plane.shape[0], p_plane.shape[1]
    lane = pl.multiple_of(other * width, LANES)
    row = pl.multiple_of(other * nx, SUBL)
    dst[:nx, :] = b_plane[:, pl.ds(lane, width)]
    dst[nx : 2 * nx, :] = p_plane[pl.ds(row, nx), :]


def keep_columns(own, slots, start, step, rs, edges):
    lanes = lax.broadcasted_iota(jnp.int32, (SUBL, LANES), 1)
    left, right = own[0, rs, :], own[1, rs, :]
    for offset in range(step):
        z = start + offset + slots
        first, last = edges(offset)
        both = pltpu.roll(jnp.where(lanes == 0, first, last), z, 1)
        left = jnp.where(lanes == z, both, left)
        right = jnp.where(lanes == lax.rem(z + LANES - 1, LANES), both, right)
    own[0, rs, :] = left
    own[1, rs, :] = right


def put_parts(e1_aux, x2, own, b_plane, p_plane, column, odd):
    nx = b_plane.shape[0]
    left, right = own[0], own[1]
    put_columns(e1_aux, jnp.where(odd, left, right))
    put_planes(e1_aux, b_plane, p_plane, column ^ 1)
    put_planes(x2, b_plane, p_plane, column ^ 2)
    aux = x2.at[2 * nx :]
    inner = (column > 0) & (column < TILE_Y - 1)
    put_columns(aux, jnp.where(inner, jnp.where(odd, right, left), 0.0))
    put_planes(aux, b_plane, p_plane, column ^ 3)


def pack_kernel(
    u, floor, ids, cond, e1, e2, x2, z1, z2, own, gv, mv, own_m, b_plane, mrow, sem
):
    g, m = floor.at[0], ids.at[0]
    group, column, odd, godd = place()
    nx, ny = u.shape[1], u.shape[2]
    nr, cx, width = g.shape
    step = SUBL
    chunks = nr // step
    shift = LANES // 2

    def load(c):
        at = pl.ds(c * step, step)
        return (
            pltpu.make_async_copy(g.at[at], gv.at[at], sem.at[2 * c]),
            pltpu.make_async_copy(m.at[at], mv.at[at], sem.at[2 * c + 1]),
        )

    base = 2 * chunks
    for copy in load(0):
        copy.start()
    plane = pltpu.make_async_copy(u.at[0], b_plane, sem.at[base])
    plane.start()
    low, high = g.at[:, 0, :], g.at[:, cx - 1, :]
    mrows = [
        pltpu.make_async_copy(m.at[:, r, :], mrow.at[s], sem.at[base + 1 + s])
        for r, s in ((0, 0), (cx - 1, 1))
    ]
    for copy in mrows + [copy for c in range(1, chunks) for copy in load(c)]:
        copy.start()
    select_copy(godd, (low, z1.at[:nr]), (high, z1.at[:nr]), sem.at[base + 3])
    select_copy(godd, (high, z2.at[:nr]), (low, z2.at[:nr]), sem.at[base + 4])
    rows_out = e1.at[:, :ny]
    select_copy(odd, (u.at[:, nx - 1, :], e2), (u.at[:, 0, :], e2), sem.at[base + 5])
    select_copy(odd, (u.at[:, 0, :], rows_out), (u.at[:, nx - 1, :], rows_out), sem.at[base + 6])
    own[...] = jnp.zeros_like(own)
    own_m[...] = jnp.zeros_like(own_m)

    def chunk(c, _):
        for copy in load(c):
            copy.wait()
        start = c * step
        for t in range(cx // SUBL):
            rs = slice(t * SUBL, (t + 1) * SUBL)

            def edges(ref):
                return lambda offset: (
                    ref[start + offset, rs, :LANES],
                    ref[start + offset, rs, width - LANES :],
                )

            keep_columns(own, 0, start, step, rs, edges(gv))
            keep_columns(own_m, shift, start, step, rs, edges(mv))
        return 0

    lax.fori_loop(0, chunks, chunk, 0)
    is_k = lax.broadcasted_iota(jnp.int32, (cx, LANES), 1) >= shift
    for s in range(2):
        codes = pltpu.roll(own_m[s], s, 1)
        own[s, :, :] = jnp.where(is_k, half_lookup(codes, cond), pltpu.roll(own[s], s, 1))
    plane.wait()
    put_parts(e1.at[:, ny:], x2, own, b_plane, gv.at[0], column, odd)
    for copy in mrows:
        copy.wait()
    k_low, k_high = half_lookup(mrow[0], cond), half_lookup(mrow[1], cond)
    z1[nr:, :] = jnp.where(godd, k_low, k_high)
    z2[nr:, :] = jnp.where(godd, k_high, k_low)
    wait_bytes(low, z1.at[:nr], sem.at[base + 3])
    wait_bytes(low, z2.at[:nr], sem.at[base + 4])
    wait_bytes(u.at[:, 0, :], e2, sem.at[base + 5])
    wait_bytes(u.at[:, 0, :], rows_out, sem.at[base + 6])


def coefficients_kernel(m, cond, u, f, ce, cw, cn, cz, urows, frows, kv, sem):
    nr, cx, width = m.shape
    nx = u.shape[1]
    picks = [(u.at[:, r, :], urows.at[i]) for i, r in enumerate((0, 1, nx - 2, nx - 1))]
    picks += [(f.at[:, r, :], frows.at[i]) for i, r in enumerate((0, nx - 1))]
    picks = [pltpu.make_async_copy(a, b, sem.at[i]) for i, (a, b) in enumerate(picks)]
    for copy in picks:
        copy.start()
    rows, lanes = iotas()
    r_last, l_first, l_last = rows == SUBL - 1, lanes == 0, lanes == LANES - 1
    tiles, wide = cx // SUBL, width // LANES
    spans = [slice(j * LANES, (j + 1) * LANES) for j in range(wide)]
    step = SUBL

    def layer(z):
        before = jnp.maximum(z - 1, 0)

        def tile(t):
            rs = slice(t * SUBL, (t + 1) * SUBL)
            ks = [half_lookup(m[z, rs, at], cond) for at in spans]
            return ks, [pltpu.roll(k, SUBL - 1, 0) for k in ks]

        ks, ups = tile(0)
        for t in range(tiles):
            rs = slice(t * SUBL, (t + 1) * SUBL)
            if t + 1 < tiles:
                kn, un = tile(t + 1)
            east = [pltpu.roll(k, LANES - 1, 1) for k in ks]
            west = [pltpu.roll(k, 1, 1) for k in ks]
            for j, at in enumerate(spans):
                k = ks[j]
                kv[z, rs, at] = k
                cz[before, rs, at] = kv[before, rs, at] + k
                if t + 1 < tiles:
                    cn[z, rs, at] = k + jnp.where(r_last, un[j], ups[j])
                else:
                    cn[z, rs, at] = jnp.where(r_last, 0.0, k + ups[j])
                if j + 1 < wide:
                    ce[z, rs, at] = k + jnp.where(l_last, east[j + 1], east[j])
                else:
                    ce[z, rs, at] = jnp.where(l_last, 0.0, k + east[j])
                if j > 0:
                    cw[z, rs, at] = k + jnp.where(l_first, west[j - 1], west[j])
                else:
                    cw[z, rs, at] = jnp.where(l_first, 0.0, k + west[j])
            if t + 1 < tiles:
                ks, ups = kn, un

    def chunk(c, _):
        for offset in range(step):
            layer(c * step + offset)
        return 0

    lax.fori_loop(0, nr // step, chunk, 0)
    cz[nr - 1, :, :] = kv[nr - 1]
    for copy in picks:
        copy.wait()


def floor_kernel(
    emit, g, ce, cw, cn, cz, u, x1, x2, x3, z1, z2, y1, y2, own, *rest
):
    nr, cx, width = g.shape
    nx, ny = u.shape[1], u.shape[2]
    if emit:
        out, own_new, o1, o2, kc, kr = rest[:6]
        ov, rest = out, rest[6:]
    else:
        kc, kr, out, ov = rest[:4]
        rest = rest[4:]
    fzv, tcol, trow, bv, sem = rest
    group, column, odd, godd = place()
    tiles, wide = cx // SUBL, width // LANES
    step = SUBL
    chunks = nr // step
    shift = LANES // 2
    aux, x3 = x1.at[:, ny:], x3.at[2 * nx :]
    groups = lax.axis_size("len") // TILE_Y
    known = (group ^ 1) < groups, jnp.where(godd, group + 1 < groups, group > 0)
    one, three = get_columns(aux), get_columns(x3)
    for s, halo in ((0, jnp.where(odd, one, three)), (1, jnp.where(odd, three, one))):
        if emit:
            kc[s, :, :] = pltpu.roll(own[s] + halo, shift, 1)
        tcol[s, :, :] = kc[s] * (halo - own[s])
    for s, (mine, halo) in enumerate(((z1, y1), (z2, y2))):
        halo = jnp.where(known[s], halo[...], 0.0)
        if emit:
            kr[s, :, :] = mine[nr:, :] + halo[nr:, :]
        side = kr[s] * (halo[:nr, :] - mine[:nr, :])
        trow[jnp.where(godd, s, 1 - s), :, :] = side
    row = lambda other: pl.ds(pl.multiple_of(other * nx, SUBL), nx)
    bv[row(column), :] = u[0, :, pl.ds(pl.multiple_of(column * width, LANES), width)]
    for k, ref in ((1, aux), (2, x2), (3, x3)):
        bv[row(column ^ k), :] = ref[:nx, :]
    rows, lanes = iotas()
    r_first, r_last = rows == 0, rows == SUBL - 1
    l_first, l_last = lanes == 0, lanes == LANES - 1
    fzv[...] = jnp.zeros_like(fzv)
    if emit:
        own_new[...] = jnp.zeros_like(own_new)
    spans = [slice(j * LANES, (j + 1) * LANES) for j in range(wide)]

    def layer(start, offset):
        z = start + offset
        back = lax.rem(LANES - z, LANES)
        above = z + 1
        if offset == step - 1:
            above = jnp.minimum(above, nr - 1)
            scale = jnp.where(z + 1 < nr, 1.0, 0.0)

        def tile(t):
            rs = slice(t * SUBL, (t + 1) * SUBL)
            gs = [g[z, rs, at] for at in spans]
            return gs, [pltpu.roll(v, SUBL - 1, 0) for v in gs]

        def row_of(s):
            block = trow[s, pl.ds(start, SUBL), :][offset : offset + 1]
            return [jnp.broadcast_to(block[:, at], (SUBL, LANES)) for at in spans]

        low, high = row_of(0), row_of(1)
        gs, ups = tile(0)
        prev = [-v for v in low]
        for t in range(tiles):
            rs = slice(t * SUBL, (t + 1) * SUBL)
            if t + 1 < tiles:
                gn, un = tile(t + 1)
            east = [pltpu.roll(v, LANES - 1, 1) for v in gs]
            west = [pltpu.roll(v, 1, 1) for v in gs]
            t_west = pltpu.roll(tcol[0, rs, :], back, 1)
            t_east = pltpu.roll(tcol[1, rs, :], LANES - 1 - z, 1)
            for j, at in enumerate(spans):
                v = gs[j]
                if t + 1 < tiles:
                    fx = cn[z, rs, at] * (jnp.where(r_last, un[j], ups[j]) - v)
                else:
                    fx = jnp.where(r_last, high[j], cn[z, rs, at] * (ups[j] - v))
                turned = pltpu.roll(fx, 1, 0)
                fxm = jnp.where(r_first, prev[j], turned)
                prev[j] = turned
                yp = jnp.where(l_last, east[j + 1], east[j]) if j + 1 < wide else east[j]
                ym = jnp.where(l_first, west[j - 1], west[j]) if j > 0 else west[j]
                side = ce[z, rs, at] * (yp - v) + cw[z, rs, at] * (ym - v)
                if j == 0:
                    side = side + jnp.where(l_first, t_west, 0.0)
                if j + 1 == wide:
                    side = side + jnp.where(l_last, t_east, 0.0)
                nxt = g[above, rs, at]
                if offset == step - 1:
                    nxt = scale * nxt
                fz = cz[z, rs, at] * (nxt - v)
                total = v + ((fx - fxm) + side + (fz - fzv[rs, at]))
                fzv[rs, at] = fz
                ov[z, rs, at] = total
            if t + 1 < tiles:
                gs, ups = gn, un

    def columns(start):
        for t in range(tiles):
            rs = slice(t * SUBL, (t + 1) * SUBL)
            edges = lambda offset: (
                ov[start + offset, rs, spans[0]],
                ov[start + offset, rs, spans[-1]],
            )
            keep_columns(own_new, 0, start, step, rs, edges)

    def store(c):
        at = pl.ds(c * step, step)
        return pltpu.make_async_copy(ov.at[at], out.at[at], sem.at[c])

    def store_rows(c):
        at = pl.ds(pl.multiple_of(c * step, SUBL), step)
        low, high = ov.at[at, 0, :], ov.at[at, cx - 1, :]
        select_copy(godd, (low, o1.at[at]), (high, o1.at[at]), sem.at[chunks + c])
        select_copy(godd, (high, o2.at[at]), (low, o2.at[at]), sem.at[2 * chunks + c])

    def chunk(c, _):
        start = pl.multiple_of(c * step, SUBL)
        for offset in range(step):
            layer(start, offset)

        @pl.when(c == 0)
        def _():
            ov[0, :, :] = ov[0] + HR * (bv[...] - g[0])

        if emit:
            store_rows(c)
            columns(start)
        else:
            store(c).start()
        return 0

    lax.fori_loop(0, chunks, chunk, 0)
    if emit:
        own_new[1, :, :] = pltpu.roll(own_new[1], 1, 1)
    for c in range(chunks):
        if emit:
            at = pl.ds(c * step, step)
            wait_bytes(ov.at[at, 0, :], o1.at[at], sem.at[chunks + c])
            wait_bytes(ov.at[at, 0, :], o2.at[at], sem.at[2 * chunks + c])
        else:
            store(c).wait()


def floor_sweep(emit, g, coefs, u, x1, x2, x3, z1, z2, y1, y2, own, halos=()):
    nr, cx, width = g.shape
    scratch = [
        pltpu.VMEM((cx, width), F32),
        pltpu.VMEM((2, cx, LANES), F32),
        pltpu.VMEM((2, nr, width), F32),
        pltpu.VMEM((cx, width), F32),
        pltpu.SemaphoreType.DMA((3 * nr // SUBL,)),
    ]
    if emit:
        outs = [
            shape(g.shape),
            shape(own.shape),
            shape((nr, width)),
            shape((nr, width)),
            shape(own.shape),
            shape((2, nr, width)),
        ]
        specs = [VMEM] * 6
    else:
        outs, specs = [far(g.shape)], [ANY]
        scratch = [pltpu.VMEM(g.shape, F32)] + scratch
    return pl.pallas_call(
        functools.partial(floor_kernel, emit),
        out_shape=outs,
        in_specs=[VMEM] * (14 + len(halos)),
        out_specs=specs,
        scratch_shapes=scratch,
        compiler_params=params(2 if emit else 6),
        cost_estimate=cost(0, 16 << 20),
        name="floor_sweep",
    )(*in_vmem(g, *coefs, u, x1, x2, x3, z1, z2, y1, y2, own, *halos))


def tin_layer(u, f, e1, e2, speeds, start, offset, out):
    zt, nx, ny = u.shape
    _, _, odd, _ = place()
    pos = lax.axis_index("len")
    alone = (pos == 0) | (pos == lax.axis_size("len") - 1)
    rows, lanes = iotas()
    r_first, r_last = rows == 0, rows == SUBL - 1
    l_first, l_last = lanes == 0, lanes == LANES - 1
    tiles, wide = nx // SUBL, ny // LANES
    zero = jnp.zeros((SUBL, LANES), F32)
    z = start + offset
    sx, sy = speeds[0, z], speeds[1, z]
    centre = 1.0 - 6.0 * KT - sx - sy - jnp.where(z == 0, HT, 0.0)
    above, below = jnp.minimum(z + 1, zt - 1), jnp.maximum(z - 1, 0)

    def get(ref, z_, t, j):
        return ref[z_, t * SUBL : (t + 1) * SUBL, j * LANES : (j + 1) * LANES]

    left = [zero] * tiles
    now = [get(u, z, t, 0) for t in range(tiles)]
    turned = [pltpu.roll(v, LANES - 1, 1) for v in now]
    for j in range(wide):
        at = slice(j * LANES, (j + 1) * LANES)
        if j + 1 < wide:
            nxt = [get(u, z, t, j + 1) for t in range(tiles)]
            nxt_turned = [pltpu.roll(v, LANES - 1, 1) for v in nxt]
        else:
            nxt, nxt_turned = None, [zero] * tiles
        one = e1[pl.ds(start, SUBL), at][offset : offset + 1]
        two = jnp.where(alone, 0.0, e2[pl.ds(start, SUBL), at][offset : offset + 1])
        low = jnp.broadcast_to(jnp.where(odd, one, two), (SUBL, LANES))
        high = jnp.broadcast_to(jnp.where(odd, two, one), (SUBL, LANES))
        downs = [low] + [pltpu.roll(v, 1, 0) for v in now]
        ups = [pltpu.roll(v, SUBL - 1, 0) for v in now] + [high]
        for t in range(tiles):
            v = now[t]
            xm = jnp.where(r_first, downs[t], downs[t + 1])
            xp = jnp.where(r_last, ups[t + 1], ups[t])
            turn = pltpu.roll(v, 1, 1)
            ym = jnp.where(l_first, left[t], turn)
            yp = jnp.where(l_last, nxt_turned[t], turned[t])
            left[t] = turn
            code = get(f, z, t, j)
            xs = jnp.where((code & 1) == 0, xm, xp)
            ys = jnp.where(code < 2, ym, yp)
            spread = (xm + xp) + (ym + yp) + (get(u, above, t, j) + get(u, below, t, j))
            out[t * SUBL : (t + 1) * SUBL, at] = (centre * v + KT * spread) + (sx * xs + sy * ys)
        now, turned = nxt, nxt_turned


def gather_floor_top(pv, e1, x2, x3, g):
    nx, ny = pv.shape
    width = x2.shape[1]
    column = place()[1]
    lanes_at = lambda other: pl.ds(pl.multiple_of(other * width, LANES), width)
    pv[:, lanes_at(column)] = g[0, pl.ds(pl.multiple_of(column * nx, SUBL), nx), :]
    for k, ref in ((1, e1.at[:, ny:]), (2, x2), (3, x3.at[2 * nx :])):
        pv[:, lanes_at(column ^ k)] = ref[nx : 2 * nx, :]


def edge_kernel(u, f, urows, frows, x2, x3, e1, e2, g, g_new, own, speeds, ox2, o1, o2, pv, plane):
    zt, nx, ny = u.shape
    group, column, odd, _ = place()
    pos = lax.axis_index("len")
    alone = (pos == 0) | (pos == lax.axis_size("len") - 1)
    gather_floor_top(pv, e1, x2, x3, g)
    tin_layer(u, f, e1, e2, speeds, 0, 0, plane)
    plane[...] = plane[...] + HT * pv[...]
    put_parts(o1.at[:, ny:], ox2, own, plane, g_new.at[0], column, odd)
    rows, lanes = iotas()
    r_first, r_last = rows == 0, rows == SUBL - 1
    l_first, l_last = lanes == 0, lanes == LANES - 1
    wide, blocks = ny // LANES, zt // SUBL
    zero = jnp.zeros((SUBL, LANES), F32)

    def block(b, _):
        start = pl.multiple_of(b * SUBL, SUBL)
        here = pl.ds(start, SUBL)
        before = pl.ds(pl.multiple_of(jnp.maximum(start - SUBL, 0), SUBL), SUBL)
        after = pl.ds(pl.multiple_of(jnp.minimum(start + SUBL, zt - SUBL), SUBL), SUBL)
        bottom, top = b == 0, b == blocks - 1
        sx = sy = zero
        for i in range(SUBL):
            sx = jnp.where(rows == i, speeds[0, start + i], sx)
            sy = jnp.where(rows == i, speeds[1, start + i], sy)
        contact = jnp.where(r_first & bottom, HT, 0.0)
        centre = 1.0 - 6.0 * KT - sx - sy - contact
        outs = []
        for s, (edge, inner, side) in enumerate(((0, 1, 0), (3, 2, nx - 1))):
            vs = [urows[edge, here, j * LANES : (j + 1) * LANES] for j in range(wide)]
            east = [pltpu.roll(v, LANES - 1, 1) for v in vs] + [zero]
            west = [zero] + [pltpu.roll(v, 1, 1) for v in vs]
            for j in range(wide):
                at = slice(j * LANES, (j + 1) * LANES)
                v, code, inside = vs[j], frows[s, here, at], urows[inner, here, at]
                one, two = e1[here, at], jnp.where(alone, 0.0, e2[here, at])
                outside = jnp.where(odd, two, one) if s else jnp.where(odd, one, two)
                xm, xp = (inside, outside) if s else (outside, inside)
                ym = jnp.where(l_first, west[j], west[j + 1])
                yp = jnp.where(l_last, east[j + 1], east[j])
                above, below = urows[edge, after, at], urows[edge, before, at]
                above = jnp.where(top, pltpu.roll(v, 1, 0), above)
                below = jnp.where(bottom, pltpu.roll(v, SUBL - 1, 0), below)
                above = jnp.where(r_last, pltpu.roll(above, SUBL - 1, 0), pltpu.roll(v, SUBL - 1, 0))
                below = jnp.where(r_first, pltpu.roll(below, 1, 0), pltpu.roll(v, 1, 0))
                xs = jnp.where((code & 1) == 0, xm, xp)
                ys = jnp.where(code < 2, ym, yp)
                spread = (xm + xp) + (ym + yp) + (above + below)
                new = (centre * v + KT * spread) + (sx * xs + sy * ys)
                new = new + contact * jnp.broadcast_to(pv[side : side + 1, at], (SUBL, LANES))
                outs.append(new)
        for j in range(wide):
            at = slice(j * LANES, (j + 1) * LANES)
            low, high = outs[j], outs[wide + j]
            o1[here, at] = jnp.where(odd, low, high)
            o2[here, at] = jnp.where(odd, high, low)
        return 0

    lax.fori_loop(0, blocks, block, 0)


def edge_sweep(u, f, urows, frows, x2, x3, e1, e2, g, g_new, own, speeds):
    plane = pltpu.VMEM(u.shape[1:], F32)
    return pl.pallas_call(
        edge_kernel,
        out_shape=[shape(v.shape) for v in (x2, e1, e2)],
        in_specs=[VMEM] * 11 + [SMEM],
        out_specs=[VMEM] * 3,
        scratch_shapes=[plane, plane],
        compiler_params=params(2),
        cost_estimate=cost(0, 4 << 20),
        name="edge",
    )(*in_vmem(u, f, urows, frows, x2, x3, e1, e2, g, g_new, own), speeds)


def tin_kernel(final, u, f, x2, x3, e1, e2, g, speeds, out, *rest):
    zt, nx, ny = u.shape
    if final:
        ov, rest = rest[0], rest[1:]
    else:
        ov = out
    pv, sem = rest
    step = SUBL
    gather_floor_top(pv, e1, x2, x3, g)

    def store(c):
        at = pl.ds(c * step, step)
        return pltpu.make_async_copy(ov.at[at], out.at[at], sem.at[c])

    def chunk(c, _):
        start = pl.multiple_of(c * step, SUBL)
        for offset in range(step):
            tin_layer(u, f, e1, e2, speeds, start, offset, ov.at[start + offset])

        @pl.when(c == 0)
        def _():
            ov[0, :, :] = ov[0] + HT * pv[...]

        if final:
            store(c).start()
        return 0

    lax.fori_loop(0, zt // step, chunk, 0)
    if final:
        for c in range(zt // step):
            store(c).wait()


def tin_sweep(final, u, f, x2, x3, e1, e2, g, speeds):
    zt, nx, ny = u.shape
    scratch = [pltpu.VMEM((nx, ny), F32), pltpu.SemaphoreType.DMA((zt // SUBL,))]
    if final:
        out, spec, scratch = far(u.shape), ANY, [pltpu.VMEM(u.shape, F32)] + scratch
    else:
        out, spec = shape(u.shape), VMEM
    return pl.pallas_call(
        functools.partial(tin_kernel, final),
        out_shape=out,
        in_specs=[VMEM] * 7 + [SMEM],
        out_specs=spec,
        scratch_shapes=scratch,
        compiler_params=params(6 if final else 2),
        cost_estimate=cost(0, 20 << 20),
        name="tin_sweep",
    )(*in_vmem(u, f, x2, x3, e1, e2, g), speeds)


def local(tin_temp, flow_code, speeds, floor_temp, material, conductivity):
    u, f, g, m = tin_temp, flow_code, floor_temp[0], material[0]
    zt, nx, ny = u.shape
    nr, cx, width = g.shape
    e1, e2, x2, z1, z2, own, gv, mv = pl.pallas_call(
        pack_kernel,
        out_shape=[
            shape((zt, ny + 2 * LANES)),
            shape((zt, ny)),
            shape((2 * nx + cx, width)),
            shape((2 * nr, width)),
            shape((2 * nr, width)),
            shape((2, cx, LANES)),
            shape(g.shape),
            shape(g.shape, jnp.int32),
        ],
        in_specs=[ANY, ANY, ANY, SMEM],
        out_specs=[VMEM] * 8,
        scratch_shapes=[
            pltpu.VMEM((2, cx, LANES), jnp.int32),
            pltpu.VMEM((nx, ny), F32),
            pltpu.VMEM((2, nr, width), jnp.int32),
            pltpu.SemaphoreType.DMA((2 * nr // SUBL + 7,)),
        ],
        compiler_params=params(2),
        cost_estimate=cost(0, 12 << 20),
        name="pack",
    )(*in_hbm(u, floor_temp, material), conductivity)
    x2 = swap(x2, "x2")
    y1, y2 = swap(z1, "z1"), swap(z2, "z2")
    e1, e2 = swap(e1, "e1"), swap(e2, "e2")
    *coefs, urows, frows = pl.pallas_call(
        coefficients_kernel,
        out_shape=[shape(g.shape)] * 4
        + [shape((4, zt, ny)), shape((2, zt, ny), jnp.int32)],
        in_specs=[VMEM, SMEM, ANY, ANY],
        out_specs=[VMEM] * 6,
        scratch_shapes=[pltpu.VMEM(g.shape, F32), pltpu.SemaphoreType.DMA((6,))],
        compiler_params=params(6),
        cost_estimate=cost(0, 16 << 20),
        name="coefficients",
    )(*in_vmem(mv), conductivity, *in_hbm(u, f))
    x2, coefs[0] = lax.optimization_barrier((x2, coefs[0]))
    x3 = swap(x2, "e1")
    g1, own1, z1, z2, kc, kr = floor_sweep(
        True, gv, coefs, u, e1, x2, x3, z1, z2, y1, y2, own
    )
    w2, w1, d2 = edge_sweep(u, f, urows, frows, x2, x3, e1, e2, gv, g1, own1, speeds)
    w2 = swap(w2, "x2")
    y1, y2 = swap(z1, "z1"), swap(z2, "z2")
    w1, d2 = swap(w1, "e1"), swap(d2, "e2")
    u1 = tin_sweep(False, u, f, x2, x3, e1, e2, gv, speeds)
    w2, u1 = lax.optimization_barrier((w2, u1))
    w3 = swap(w2, "e1")
    (g2,) = floor_sweep(
        False, g1, coefs, u1, w1, w2, w3, z1, z2, y1, y2, own1, (kc, kr)
    )
    u2 = tin_sweep(True, u1, f, w2, w3, w1, d2, g1, speeds)
    return u2, g2[None]


def solution(mesh):
    placed = (
        P(None, ("grp", "len"), None),
        P(None, ("grp", "len"), None),
        P(),
        P(("grp", "len"), None, None, None),
        P(("grp", "len"), None, None, None),
        P(),
    )
    return jax.shard_map(
        local,
        mesh=mesh,
        in_specs=placed,
        out_specs=(P(None, ("grp", "len"), None), P(("grp", "len"), None, None, None)),
        check_vma=False,
    )
```

time: 60.8 us -> 48 us (0.79)
  starting transfers between devices: 18.6 us -> 10.2 us
  waiting for transfers between devices: 13.1 us -> 8.44 us
    ppermute x12, starting transfers between devices: 18.6 us -> 10.2 us  [swap(): return lax.ppermute(value, ('grp', 'len'), pairs)]
    ppermute x12, waiting for transfers between devices: 13.1 us -> 8.44 us  [swap(): return lax.ppermute(value, ('grp', 'len'), pairs)]
    pallas_call x4 -> x5, Pallas kernels: 18.5 us -> 18.9 us  [the longest x2 9.75 us: tin_sweep(): pl.pallas_call(functools.partial(tin_kernel, final), out_shape=out, in_sp...]
  transfers between devices with their start and end apart: 12 -> 12, of which waited for: 3 -> 3; matrix products, arithmetic and copies ran while one was open for 0% -> 0% of each run, Pallas kernels for 16% -> 38%
where the time goes in v1:
time: 48 us; the launch traced here: 47.2 us
  Pallas kernels  27.1 us (56%)
  starting transfers between devices  10.2 us (21%)
  waiting for transfers between devices  8.44 us (18%)
  between operations  0.76 us (2%)
  local copies, waits for them, and re-layouts  0.67 us (1%)
    ppermute x12, starting transfers between devices, swap(): return lax.ppermute(value, ('grp', 'len'), pairs)  10.2 us
    pallas_call x2, Pallas kernels, tin_sweep(): pl.pallas_call(functools.partial(tin_kernel, final), out_shape=out, in_sp...  9.75 us
    ppermute x12, waiting for transfers between devices, swap(): return lax.ppermute(value, ('grp', 'len'), pairs)  8.44 us
    pallas_call x2, Pallas kernels, floor_sweep(): pl.pallas_call(functools.partial(floor_kernel, emit), out_shape=outs, in_...  8.2 us
    pallas_call x1, Pallas kernels, local(): pl.pallas_call(pack_kernel, out_shape=[shape((zt, ny + 2 * LANES)), shape...  3.89 us
    pallas_call x1, Pallas kernels, local(): pl.pallas_call(coefficients_kernel, out_shape=[shape(g.shape)] * 4 + [sha...  3.72 us
    pallas_call x1, Pallas kernels, edge_sweep(): pl.pallas_call(edge_kernel, out_shape=[shape(v.shape) for v in (x2, e1, e...  1.59 us
  transfers between devices with their start and end apart: 12, of which 3 were waited for; matrix products, arithmetic and copies ran while one was open for 0% of the time, Pallas kernels for 38%

profile of v1, /device:TPU:8, one launch (start us, length us, event | category | flops | bytes accessed | tf_op | source)
XLA Modules:
  0.0 47.2 jit_solution(7240167911020445948)
XLA Ops:
  0.6 0.0 copy-start.3
  0.6 0.6 %copy-done.3 = f32[3]{0:T(128)S(1)} copy-done((f32[3]{0:T(128)S(1)}, f32[3]{0:T(128)}, u32[]{:S(2)}) %copy-start.3) | copy-done | bytes 36
  1.3 0.0 copy-start.4
  1.3 3.9 %pack.1 = (f32[64,1280]{1,0:T(8,128)S(1)}, f32[64,1024]{1,0:T(8,128)S(1)}, f32[96,256]{1,0:T(8,128)S(1)}, f32[96,256]{1,0:T(8,128)S(1)}, f32[96,256]{1,0:T(8,128...) custom-call(f32[64,16,1024]{2,1,0:T(8,128)} %u.9, ...), custom_call_target="tpu_custom_call" | custom-call | bytes 12582912 | tf_op jit(solution)/shard_map/pack/pallas_call | solution.py:647
  5.2 0.1 collective-permute-start.2
  5.3 1.5 %collective-permute-start.3 = (f32[64,1024]{1,0:T(8,128)S(1)}, f32[64,1024]{1,0:T(8,128)S(1)}, u32[]{:S(2)}, u32[]{:S(2)}) collective-permute-start(f32[64,1024]{1,0:T(8,128)S(1)} %get-tuple-element.36), channel_id=1, source_target_pairs={{0,16},{1,2},{2,1},{3,4},{4,3},{5,6},{6,5},{7,8},{8,7},{9,10},{10,... | collective-permute-start | bytes 786440 | tf_op jit(solution)/shard_map/ppermute | solution.py:78
  6.8 0.6 %collective-permute-start = (f32[96,256]{1,0:T(8,128)S(1)}, f32[96,256]{1,0:T(8,128)S(1)}, u32[]{:S(2)}, u32[]{:S(2)}) collective-permute-start(f32[96,256]{1,0:T(8,128)S(1)} %get-tuple-element.32), channel_id=1, source_target_pairs={{0,2},{1,3},{2,0},{3,1},{4,6},{5,7},{6,4},{7,5},{8,10},{9,11},{10,... | collective-permute-start | bytes 294920 | tf_op jit(solution)/shard_map/ppermute | solution.py:78
  7.4 0.0 collective-permute-start.4
  7.4 3.1 %collective-permute-start.5 = (f32[96,256]{1,0:T(8,128)S(1)}, f32[96,256]{1,0:T(8,128)S(1)}, u32[]{:S(2)}, u32[]{:S(2)}) collective-permute-start(f32[96,256]{1,0:T(8,128)S(1)} %get-tuple-element.43.z2), channel_id=1, source_target_pairs={{0,1},{1,0},{2,3},{3,2},{4,8},{5,9},{6,10},{7,11},{8,4},{9,5},{10,... | collective-permute-start | bytes 294920 | tf_op jit(solution)/shard_map/ppermute | solution.py:78
  10.5 0.0 copy-done.4
  10.6 0.0 copy-start
  10.6 3.7 %coefficients.1 = (f32[48,64,256]{2,1,0:T(8,128)S(1)}, f32[48,64,256]{2,1,0:T(8,128)S(1)}, f32[48,64,256]{2,1,0:T(8,128)S(1)}, f32[48,64,256]{2,1,0:T(8,128)S(1)...) custom-call(s32[48,64,256]{2,1,0:T(8,128)S(1)} %get-tuple-element.29.m, f32[3]{0:T(128)S(1)} %copy-done.4, ...), custom_call_target="tpu_custom_call" | custom-call | bytes 16777216 | tf_op jit(solution)/shard_map/coefficients/pallas_call | solution.py:674
  14.3 2.4 %collective-permute-done.x2 = f32[96,256]{1,0:T(8,128)S(1)} collective-permute-done((f32[96,256]{1,0:T(8,128)S(1)}, f32[96,256]{1,0:T(8,128)S(1)}, u32[]{:S(2)}, u32[]{:S(2)}) %collective-permute-start) | collective-permute-done | bytes 98336 | tf_op jit(solution)/shard_map/ppermute | solution.py:78
  16.7 0.0 collective-permute-start.1
  16.7 0.0 collective-permute-done.4.y1
  16.7 0.0 collective-permute-done.5.y2
  16.7 1.3 %collective-permute-done.1.x3 = f32[96,256]{1,0:T(8,128)S(1)} collective-permute-done((f32[96,256]{1,0:T(8,128)S(1)}, f32[96,256]{1,0:T(8,128)S(1)}, u32[]{:S(2)}, u32[]{:S(2)}) %collective-permute-start.1) | collective-permute-done | bytes 98336 | tf_op jit(solution)/shard_map/ppermute | solution.py:78
  18.0 0.0 collective-permute-done.2.x1.e1
  18.0 0.0 copy-done
  18.0 0.0 copy-start.1
  18.0 0.0 copy-start.2
  18.0 4.3 %floor_sweep.2 = (f32[48,64,256]{2,1,0:T(8,128)S(1)}, f32[2,64,128]{2,1,0:T(8,128)S(1)}, f32[48,256]{1,0:T(8,128)S(1)}, f32[48,256]{1,0:T(8,128)S(1)}, f32[2,64,...) custom-call(f32[48,64,256]{2,1,0:T(8,128)S(1)} %get-tuple-element.37.g, f32[48,64,256]{2,1,0:T(8,128)S(1)} %get-tuple-element.38.ce, ...), custom_call_target="tpu_custom_call" | custom-call | bytes 16777216 | tf_op jit(solution)/shard_map/floor_sweep/pallas_call | solution.py:444
  22.3 0.0 collective-permute-done.3.e2
  22.3 0.0 copy-done.1
  22.3 0.0 copy-done.2
  22.3 1.6 %edge.1 = (f32[96,256]{1,0:T(8,128)S(1)}, f32[64,1280]{1,0:T(8,128)S(1)}, f32[64,1024]{1,0:T(8,128)S(1)}) custom-call(f32[64,16,1024]{2,1,0:T(8,128)S(1)} %copy-done, s32[64,16,1024]{2,1,0:T(8,128)S(1)} %copy-done.1, f32[4,64,1024]{2,1,0:T(8,128)S(1)} %get-tuple-element.30.urows, s32[2,64,1024]{2,1,0:T(8,128)S(1)} %get-tuple-element.31.frows, ...), custom_call_target="tpu_custom_call" | custom-call | bytes 4194304 | tf_op jit(solution)/shard_map/edge/pallas_call | solution.py:579
  23.9 0.2 collective-permute-start.8
  24.1 0.2 collective-permute-start.9
  24.3 1.8 %collective-permute-start.6 = (f32[96,256]{1,0:T(8,128)S(1)}, f32[96,256]{1,0:T(8,128)S(1)}, u32[]{:S(2)}, u32[]{:S(2)}) collective-permute-start(f32[96,256]{1,0:T(8,128)S(1)} %get-tuple-element.47), channel_id=1, source_target_pairs={{0,2},{1,3},{2,0},{3,1},{4,6},{5,7},{6,4},{7,5},{8,10},{9,11},{10,... | collective-permute-start | bytes 294920 | tf_op jit(solution)/shard_map/ppermute | solution.py:78
  26.1 4.5 %tin_sweep.2.u = f32[64,16,1024]{2,1,0:T(8,128)S(1)} custom-call(f32[64,16,1024]{2,1,0:T(8,128)S(1)} %copy-done, s32[64,16,1024]{2,1,0:T(8,128)S(1)} %copy-done.1, f32[96,256]{1,0:T(8,128)S(1)} %collective-permute-done.x2, f32[96,256]{1,0:T(8,128)S(1)} %collective-permute-done.1.x3, f32[64,1280]{1,0:T(8,128)S(1)} %collective-permute-done.2.x1.e1, ...), custom_call_target="tpu_custom_call" | custom-call | bytes 20971520 | tf_op jit(solution)/shard_map/tin_sweep/pallas_call | solution.py:631
  30.6 4.7 %collective-permute-done.6.x2 = f32[96,256]{1,0:T(8,128)S(1)} collective-permute-done((f32[96,256]{1,0:T(8,128)S(1)}, f32[96,256]{1,0:T(8,128)S(1)}, u32[]{:S(2)}, u32[]{:S(2)}) %collective-permute-start.6) | collective-permute-done | bytes 98336 | tf_op jit(solution)/shard_map/ppermute | solution.py:78
  35.4 0.0 collective-permute-start.7
  35.4 0.0 collective-permute-start.10
  35.4 2.6 %collective-permute-start.11 = (f32[48,256]{1,0:T(8,128)S(1)}, f32[48,256]{1,0:T(8,128)S(1)}, u32[]{:S(2)}, u32[]{:S(2)}) collective-permute-start(f32[48,256]{1,0:T(8,128)S(1)} %get-tuple-element.53.z2), channel_id=1, source_target_pairs={{0,1},{1,0},{2,3},{3,2},{4,8},{5,9},{6,10},{7,11},{8,4},{9,5},{10,... | collective-permute-start | bytes 147464 | tf_op jit(solution)/shard_map/ppermute | solution.py:78
  38.0 0.0 collective-permute-done.7.x3
  38.0 0.0 collective-permute-done.9.e2
  38.0 0.0 collective-permute-done.8.e1.x1
  38.0 5.2 %tin_sweep.3 = f32[64,16,1024]{2,1,0:T(8,128)} custom-call(f32[64,16,1024]{2,1,0:T(8,128)S(1)} %tin_sweep.2.u, s32[64,16,1024]{2,1,0:T(8,128)S(1)} %copy-done.1, f32[96,256]{1,0:T(8,128)S(1)} %collective-permute-done.6.x2, f32[96,256]{1,0:T(8,128)S(1)} %collective-permute-done.7.x3, f32[64,1280]{1,0:T(8,128)S(1)} %collective-permute-done.8.e1.x1, ...), custom_call_target="tpu_custom_call" | custom-call | bytes 20971520 | tf_op jit(solution)/shard_map/tin_sweep/pallas_call | solution.py:631
  43.2 0.0 collective-permute-done.10.y1
  43.3 0.0 collective-permute-done.11.y2
  43.3 3.9 %floor_sweep.3 = f32[48,64,256]{2,1,0:T(8,128)} custom-call(f32[48,64,256]{2,1,0:T(8,128)S(1)} %get-tuple-element.45.g_new.g, f32[48,64,256]{2,1,0:T(8,128)S(1)} %get-tuple-element.38.ce, f32[48,64,256]{2,1,0:T(8,128)S(1)} %get-tuple-element.39.cw, f32[48,64,256]{2,1,0:T(8,128)S(1)} %get-tuple-element.40.cn, f32[48,64,256]{2,1,0:T(8,128)S(1)} %get-tuple-element.41.cz, ...), custom_call_target="tpu_custom_call" | custom-call | bytes 16777216 | tf_op jit(solution)/shard_map/floor_sweep/pallas_call | solution.py:444
Async XLA Ops:
  0.6 0.7 %copy-start.3 = (f32[3]{0:T(128)S(1)}, f32[3]{0:T(128)}, u32[]{:S(2)}) copy-start(f32[3]{0:T(128)} %cond.3) | copy-start | bytes 40
  1.3 9.3 %copy-start.4 = (f32[3]{0:T(128)S(1)}, f32[3]{0:T(128)}, u32[]{:S(2)}) copy-start(f32[3]{0:T(128)} %cond.3) | copy-start | bytes 40
  5.2 12.8 %collective-permute-start.2 = (f32[64,1280]{1,0:T(8,128)S(1)}, f32[64,1280]{1,0:T(8,128)S(1)}, u32[]{:S(2)}, u32[]{:S(2)}) collective-permute-start(f32[64,1280]{1,0:T(8,128)S(1)} %get-tuple-element.35), channel_id=1, source_target_pairs={{0,1},{1,0},{2,3},{3,2},{4,5},{5,4},{6,7},{7,6},{8,9},{9,8},{10,11... | collective-permute-start | bytes 983048 | tf_op jit(solution)/shard_map/ppermute | solution.py:78
  5.3 17.0 %collective-permute-start.3 = (f32[64,1024]{1,0:T(8,128)S(1)}, f32[64,1024]{1,0:T(8,128)S(1)}, u32[]{:S(2)}, u32[]{:S(2)}) collective-permute-start(f32[64,1024]{1,0:T(8,128)S(1)} %get-tuple-element.36), channel_id=1, source_target_pairs={{0,16},{1,2},{2,1},{3,4},{4,3},{5,6},{6,5},{7,8},{8,7},{9,10},{10,... | collective-permute-start | bytes 786440 | tf_op jit(solution)/shard_map/ppermute | solution.py:78
  6.8 9.9 %collective-permute-start = (f32[96,256]{1,0:T(8,128)S(1)}, f32[96,256]{1,0:T(8,128)S(1)}, u32[]{:S(2)}, u32[]{:S(2)}) collective-permute-start(f32[96,256]{1,0:T(8,128)S(1)} %get-tuple-element.32), channel_id=1, source_target_pairs={{0,2},{1,3},{2,0},{3,1},{4,6},{5,7},{6,4},{7,5},{8,10},{9,11},{10,... | collective-permute-start | bytes 294920 | tf_op jit(solution)/shard_map/ppermute | solution.py:78
  7.4 9.3 %collective-permute-start.4 = (f32[96,256]{1,0:T(8,128)S(1)}, f32[96,256]{1,0:T(8,128)S(1)}, u32[]{:S(2)}, u32[]{:S(2)}) collective-permute-start(f32[96,256]{1,0:T(8,128)S(1)} %get-tuple-element.42.z1), channel_id=1, source_target_pairs={{0,4},{1,5},{2,6},{3,7},{4,0},{5,1},{6,2},{7,3},{8,12},{9,13},{10,... | collective-permute-start | bytes 294920 | tf_op jit(solution)/shard_map/ppermute | solution.py:78
  7.4 9.3 %collective-permute-start.5 = (f32[96,256]{1,0:T(8,128)S(1)}, f32[96,256]{1,0:T(8,128)S(1)}, u32[]{:S(2)}, u32[]{:S(2)}) collective-permute-start(f32[96,256]{1,0:T(8,128)S(1)} %get-tuple-element.43.z2), channel_id=1, source_target_pairs={{0,1},{1,0},{2,3},{3,2},{4,8},{5,9},{6,10},{7,11},{8,4},{9,5},{10,... | collective-permute-start | bytes 294920 | tf_op jit(solution)/shard_map/ppermute | solution.py:78
  10.6 7.4 %copy-start = (f32[64,16,1024]{2,1,0:T(8,128)S(1)}, f32[64,16,1024]{2,1,0:T(8,128)}, u32[]{:S(2)}) copy-start(f32[64,16,1024]{2,1,0:T(8,128)} %u.9) | copy-start | bytes 12582916
  16.7 1.3 %collective-permute-start.1 = (f32[96,256]{1,0:T(8,128)S(1)}, f32[96,256]{1,0:T(8,128)S(1)}, u32[]{:S(2)}, u32[]{:S(2)}) collective-permute-start(f32[96,256]{1,0:T(8,128)S(1)} %collective-permute-done.x2), channel_id=1, source_target_pairs={{0,1},{1,0},{2,3},{3,2},{4,5},{5,4},{6,7},{7,6},{8,9},{9,8},{10,11... | collective-permute-start | bytes 294920 | tf_op jit(solution)/shard_map/ppermute | solution.py:78
  18.0 4.3 %copy-start.1 = (s32[64,16,1024]{2,1,0:T(8,128)S(1)}, s32[64,16,1024]{2,1,0:T(8,128)}, u32[]{:S(2)}) copy-start(s32[64,16,1024]{2,1,0:T(8,128)} %f.7) | copy-start | bytes 12582916
  18.0 4.3 %copy-start.2 = (f32[2,64]{1,0:T(2,128)S(1)}, f32[2,64]{1,0:T(2,128)}, u32[]{:S(2)}) copy-start(f32[2,64]{1,0:T(2,128)} %speeds.5) | copy-start | bytes 1540
  23.9 14.1 %collective-permute-start.8 = (f32[64,1280]{1,0:T(8,128)S(1)}, f32[64,1280]{1,0:T(8,128)S(1)}, u32[]{:S(2)}, u32[]{:S(2)}) collective-permute-start(f32[64,1280]{1,0:T(8,128)S(1)} %get-tuple-element.50), channel_id=1, source_target_pairs={{0,1},{1,0},{2,3},{3,2},{4,5},{5,4},{6,7},{7,6},{8,9},{9,8},{10,11... | collective-permute-start | bytes 983048 | tf_op jit(solution)/shard_map/ppermute | solution.py:78
  24.1 13.9 %collective-permute-start.9 = (f32[64,1024]{1,0:T(8,128)S(1)}, f32[64,1024]{1,0:T(8,128)S(1)}, u32[]{:S(2)}, u32[]{:S(2)}) collective-permute-start(f32[64,1024]{1,0:T(8,128)S(1)} %get-tuple-element.51), channel_id=1, source_target_pairs={{0,16},{1,2},{2,1},{3,4},{4,3},{5,6},{6,5},{7,8},{8,7},{9,10},{10,... | collective-permute-start | bytes 786440 | tf_op jit(solution)/shard_map/ppermute | solution.py:78
  24.3 11.0 %collective-permute-start.6 = (f32[96,256]{1,0:T(8,128)S(1)}, f32[96,256]{1,0:T(8,128)S(1)}, u32[]{:S(2)}, u32[]{:S(2)}) collective-permute-start(f32[96,256]{1,0:T(8,128)S(1)} %get-tuple-element.47), channel_id=1, source_target_pairs={{0,2},{1,3},{2,0},{3,1},{4,6},{5,7},{6,4},{7,5},{8,10},{9,11},{10,... | collective-permute-start | bytes 294920 | tf_op jit(solution)/shard_map/ppermute | solution.py:78
  35.4 2.6 %collective-permute-start.7 = (f32[96,256]{1,0:T(8,128)S(1)}, f32[96,256]{1,0:T(8,128)S(1)}, u32[]{:S(2)}, u32[]{:S(2)}) collective-permute-start(f32[96,256]{1,0:T(8,128)S(1)} %collective-permute-done.6.x2), channel_id=1, source_target_pairs={{0,1},{1,0},{2,3},{3,2},{4,5},{5,4},{6,7},{7,6},{8,9},{9,8},{10,11... | collective-permute-start | bytes 294920 | tf_op jit(solution)/shard_map/ppermute | solution.py:78
  35.4 7.9 %collective-permute-start.10 = (f32[48,256]{1,0:T(8,128)S(1)}, f32[48,256]{1,0:T(8,128)S(1)}, u32[]{:S(2)}, u32[]{:S(2)}) collective-permute-start(f32[48,256]{1,0:T(8,128)S(1)} %get-tuple-element.52.z1), channel_id=1, source_target_pairs={{0,4},{1,5},{2,6},{3,7},{4,0},{5,1},{6,2},{7,3},{8,12},{9,13},{10,... | collective-permute-start | bytes 147464 | tf_op jit(solution)/shard_map/ppermute | solution.py:78
  35.4 7.9 %collective-permute-start.11 = (f32[48,256]{1,0:T(8,128)S(1)}, f32[48,256]{1,0:T(8,128)S(1)}, u32[]{:S(2)}, u32[]{:S(2)}) collective-permute-start(f32[48,256]{1,0:T(8,128)S(1)} %get-tuple-element.53.z2), channel_id=1, source_target_pairs={{0,1},{1,0},{2,3},{3,2},{4,8},{5,9},{6,10},{7,11},{8,4},{9,5},{10,... | collective-permute-start | bytes 147464 | tf_op jit(solution)/shard_map/ppermute | solution.py:78

commit v2 on v1

--- a/solution.py
+++ b/solution.py
@@ -16,7 +16,6 @@
 F32 = jnp.float32
 ANY = pl.BlockSpec(memory_space=pl.ANY)
 VMEM = pl.BlockSpec(memory_space=pltpu.VMEM)
-SMEM = pl.BlockSpec(memory_space=pltpu.SMEM)
 
 
 def params(mib):
@@ -60,6 +59,7 @@
         "e1": lambda: pos ^ 1,
         "e2": lambda: pos + 1 if pos % 2 else pos - 1,
         "x2": lambda: pos ^ 2,
+        "x3": lambda: pos ^ 3,
         "z1": lambda: pos ^ TILE_Y,
         "z2": lambda: pos + TILE_Y if (pos // TILE_Y) % 2 else pos - TILE_Y,
     }[kind]()
@@ -88,10 +88,10 @@
         pltpu.make_async_copy(*second, sem).start()
 
 
-def half_lookup(ids, cond):
-    value = jnp.full(ids.shape, 0.5 * cond[0], F32)
-    for i in range(1, cond.shape[0]):
-        value = jnp.where(ids == i, 0.5 * cond[i], value)
+def half_coded(codes, halves):
+    value = jnp.zeros(codes.shape, F32)
+    for i in range(halves.shape[0]):
+        value = jnp.where(codes == i + 1.0, halves[i, 0:1, 0:1], value)
     return value
 
 
@@ -131,20 +131,20 @@
     own[1, rs, :] = right
 
 
-def put_parts(e1_aux, x2, own, b_plane, p_plane, column, odd):
+def put_parts(e1_aux, x2, x3, own, b_plane, p_plane, column, odd):
     nx = b_plane.shape[0]
     left, right = own[0], own[1]
     put_columns(e1_aux, jnp.where(odd, left, right))
     put_planes(e1_aux, b_plane, p_plane, column ^ 1)
     put_planes(x2, b_plane, p_plane, column ^ 2)
-    aux = x2.at[2 * nx :]
     inner = (column > 0) & (column < TILE_Y - 1)
-    put_columns(aux, jnp.where(inner, jnp.where(odd, right, left), 0.0))
-    put_planes(aux, b_plane, p_plane, column ^ 3)
+    put_columns(x3, jnp.where(inner, jnp.where(odd, right, left), 0.0))
+    put_planes(x3, b_plane, p_plane, column ^ 3)
 
 
 def pack_kernel(
-    u, floor, ids, cond, e1, e2, x2, z1, z2, own, gv, mv, own_m, b_plane, mrow, sem
+    u, floor, ids, speeds, cond, e1, e2, x2, x3, z1, z2, own, gv, mv, rates, halves,
+    own_m, b_plane, mrow, speeds_v, cond_v, sem
 ):
     g, m = floor.at[0], ids.at[0]
     group, column, odd, godd = place()
@@ -175,6 +175,12 @@
         copy.start()
     select_copy(godd, (low, z1.at[:nr]), (high, z1.at[:nr]), sem.at[base + 3])
     select_copy(godd, (high, z2.at[:nr]), (low, z2.at[:nr]), sem.at[base + 4])
+    small = (
+        pltpu.make_async_copy(speeds, speeds_v, sem.at[base + 7]),
+        pltpu.make_async_copy(cond, cond_v, sem.at[base + 8]),
+    )
+    for copy in small:
+        copy.start()
     rows_out = e1.at[:, :ny]
     select_copy(odd, (u.at[:, nx - 1, :], e2), (u.at[:, 0, :], e2), sem.at[base + 5])
     select_copy(odd, (u.at[:, 0, :], rows_out), (u.at[:, nx - 1, :], rows_out), sem.at[base + 6])
@@ -202,24 +208,36 @@
     is_k = lax.broadcasted_iota(jnp.int32, (cx, LANES), 1) >= shift
     for s in range(2):
         codes = pltpu.roll(own_m[s], s, 1)
-        own[s, :, :] = jnp.where(is_k, half_lookup(codes, cond), pltpu.roll(own[s], s, 1))
+        own[s, :, :] = jnp.where(is_k, codes.astype(F32) + 1.0, pltpu.roll(own[s], s, 1))
     plane.wait()
-    put_parts(e1.at[:, ny:], x2, own, b_plane, gv.at[0], column, odd)
+    put_parts(e1.at[:, ny:], x2, x3, own, b_plane, gv.at[0], column, odd)
     for copy in mrows:
         copy.wait()
-    k_low, k_high = half_lookup(mrow[0], cond), half_lookup(mrow[1], cond)
-    z1[nr:, :] = jnp.where(godd, k_low, k_high)
-    z2[nr:, :] = jnp.where(godd, k_high, k_low)
+    m_low, m_high = mrow[0].astype(F32) + 1.0, mrow[1].astype(F32) + 1.0
+    z1[nr:, :] = jnp.where(godd, m_low, m_high)
+    z2[nr:, :] = jnp.where(godd, m_high, m_low)
+    for copy in small:
+        copy.wait()
+    zt = u.shape[0]
+    diagonal = lax.broadcasted_iota(jnp.int32, (zt, zt), 0) == lax.broadcasted_iota(
+        jnp.int32, (zt, zt), 1
+    )
+    for s in range(2):
+        spread = jnp.where(diagonal, jnp.broadcast_to(speeds_v[s : s + 1, :], (zt, zt)), 0.0)
+        along = jnp.sum(spread, axis=1, keepdims=True)
+        rates[s, :, :] = jnp.broadcast_to(along, (zt, LANES))
+    for i in range(halves.shape[0]):
+        halves[i, :, :] = jnp.broadcast_to(0.5 * cond_v[0:1, i : i + 1], (SUBL, LANES))
     wait_bytes(low, z1.at[:nr], sem.at[base + 3])
     wait_bytes(low, z2.at[:nr], sem.at[base + 4])
     wait_bytes(u.at[:, 0, :], e2, sem.at[base + 5])
     wait_bytes(u.at[:, 0, :], rows_out, sem.at[base + 6])
 
 
-def coefficients_kernel(m, cond, u, f, ce, cw, cn, cz, urows, frows, kv, sem):
+def coefficients_kernel(m, halves, u, f, ce, cw, cn, cz, urows, frows, kv, sem):
     nr, cx, width = m.shape
     nx = u.shape[1]
-    picks = [(u.at[:, r, :], urows.at[i]) for i, r in enumerate((0, 1, nx - 2, nx - 1))]
+    picks = [(u.at[:, r, :], urows.at[i]) for i, r in enumerate((1, nx - 2))]
     picks += [(f.at[:, r, :], frows.at[i]) for i, r in enumerate((0, nx - 1))]
     picks = [pltpu.make_async_copy(a, b, sem.at[i]) for i, (a, b) in enumerate(picks)]
     for copy in picks:
@@ -229,13 +247,20 @@
     tiles, wide = cx // SUBL, width // LANES
     spans = [slice(j * LANES, (j + 1) * LANES) for j in range(wide)]
     step = SUBL
+    values = [halves[i] for i in range(halves.shape[0])]
+
+    def lookup(ids):
+        value = values[0]
+        for i in range(1, len(values)):
+            value = jnp.where(ids == i, values[i], value)
+        return value
 
     def layer(z):
         before = jnp.maximum(z - 1, 0)
 
         def tile(t):
             rs = slice(t * SUBL, (t + 1) * SUBL)
-            ks = [half_lookup(m[z, rs, at], cond) for at in spans]
+            ks = [lookup(m[z, rs, at]) for at in spans]
             return ks, [pltpu.roll(k, SUBL - 1, 0) for k in ks]
 
         ks, ups = tile(0)
@@ -281,8 +306,8 @@
     nr, cx, width = g.shape
     nx, ny = u.shape[1], u.shape[2]
     if emit:
-        out, own_new, o1, o2, kc, kr = rest[:6]
-        ov, rest = out, rest[6:]
+        halves, out, own_new, o1, o2, kc, kr = rest[:7]
+        ov, rest = out, rest[7:]
     else:
         kc, kr, out, ov = rest[:4]
         rest = rest[4:]
@@ -292,18 +317,19 @@
     step = SUBL
     chunks = nr // step
     shift = LANES // 2
-    aux, x3 = x1.at[:, ny:], x3.at[2 * nx :]
+    aux = x1.at[:, ny:]
     groups = lax.axis_size("len") // TILE_Y
     known = (group ^ 1) < groups, jnp.where(godd, group + 1 < groups, group > 0)
     one, three = get_columns(aux), get_columns(x3)
     for s, halo in ((0, jnp.where(odd, one, three)), (1, jnp.where(odd, three, one))):
         if emit:
-            kc[s, :, :] = pltpu.roll(own[s] + halo, shift, 1)
+            both = half_coded(own[s], halves) + half_coded(halo, halves)
+            kc[s, :, :] = pltpu.roll(both, shift, 1)
         tcol[s, :, :] = kc[s] * (halo - own[s])
     for s, (mine, halo) in enumerate(((z1, y1), (z2, y2))):
         halo = jnp.where(known[s], halo[...], 0.0)
         if emit:
-            kr[s, :, :] = mine[nr:, :] + halo[nr:, :]
+            kr[s, :, :] = half_coded(mine[nr:, :], halves) + half_coded(halo[nr:, :], halves)
         side = kr[s] * (halo[:nr, :] - mine[:nr, :])
         trow[jnp.where(godd, s, 1 - s), :, :] = side
     row = lambda other: pl.ds(pl.multiple_of(other * nx, SUBL), nx)
@@ -410,62 +436,74 @@
     lax.fori_loop(0, chunks, chunk, 0)
     if emit:
         own_new[1, :, :] = pltpu.roll(own_new[1], 1, 1)
-    for c in range(chunks):
-        if emit:
+    if emit:
+        for c in range(chunks):
             at = pl.ds(c * step, step)
             wait_bytes(ov.at[at, 0, :], o1.at[at], sem.at[chunks + c])
             wait_bytes(ov.at[at, 0, :], o2.at[at], sem.at[2 * chunks + c])
-        else:
-            store(c).wait()
-
-
-def floor_sweep(emit, g, coefs, u, x1, x2, x3, z1, z2, y1, y2, own, halos=()):
-    nr, cx, width = g.shape
-    scratch = [
+        return []
+    return [store(c) for c in range(chunks)]
+
+
+def floor_scratch(dims):
+    nr, cx, width = dims
+    return [
         pltpu.VMEM((cx, width), F32),
         pltpu.VMEM((2, cx, LANES), F32),
         pltpu.VMEM((2, nr, width), F32),
         pltpu.VMEM((cx, width), F32),
         pltpu.SemaphoreType.DMA((3 * nr // SUBL,)),
     ]
-    if emit:
-        outs = [
+
+
+def floor_first(g, coefs, u, x1, x2, x3, z1, z2, y1, y2, own, halves):
+    nr, cx, width = g.shape
+
+    def kernel(*refs):
+        floor_kernel(True, *refs)
+
+    return pl.pallas_call(
+        kernel,
+        out_shape=[
             shape(g.shape),
             shape(own.shape),
             shape((nr, width)),
             shape((nr, width)),
             shape(own.shape),
             shape((2, nr, width)),
-        ]
-        specs = [VMEM] * 6
-    else:
-        outs, specs = [far(g.shape)], [ANY]
-        scratch = [pltpu.VMEM(g.shape, F32)] + scratch
-    return pl.pallas_call(
-        functools.partial(floor_kernel, emit),
-        out_shape=outs,
-        in_specs=[VMEM] * (14 + len(halos)),
-        out_specs=specs,
-        scratch_shapes=scratch,
-        compiler_params=params(2 if emit else 6),
+        ],
+        in_specs=[VMEM] * 15,
+        out_specs=[VMEM] * 6,
+        scratch_shapes=floor_scratch(g.shape),
+        compiler_params=params(2),
         cost_estimate=cost(0, 16 << 20),
-        name="floor_sweep",
-    )(*in_vmem(g, *coefs, u, x1, x2, x3, z1, z2, y1, y2, own, *halos))
-
-
-def tin_layer(u, f, e1, e2, speeds, start, offset, out):
+        name="floor_first",
+    )(*in_vmem(g, *coefs, u, x1, x2, x3, z1, z2, y1, y2, own, halves))
+
+
+def fill_halo(halo, e1, e2):
+    odd, pos, ny = place()[2], lax.axis_index("len"), halo.shape[2]
+    alone = (pos == 0) | (pos == lax.axis_size("len") - 1)
+    one, two = e1[:, :ny], jnp.where(alone, 0.0, e2[...])
+    halo[0, :, :] = jnp.where(odd, one, two)
+    halo[1, :, :] = jnp.where(odd, two, one)
+
+
+def tin_layer(u, f, halo, rates, start, offset, out):
     zt, nx, ny = u.shape
-    _, _, odd, _ = place()
-    pos = lax.axis_index("len")
-    alone = (pos == 0) | (pos == lax.axis_size("len") - 1)
     rows, lanes = iotas()
     r_first, r_last = rows == 0, rows == SUBL - 1
     l_first, l_last = lanes == 0, lanes == LANES - 1
     tiles, wide = nx // SUBL, ny // LANES
     zero = jnp.zeros((SUBL, LANES), F32)
     z = start + offset
-    sx, sy = speeds[0, z], speeds[1, z]
-    centre = 1.0 - 6.0 * KT - sx - sy - jnp.where(z == 0, HT, 0.0)
+    sx, sy = (
+        jnp.broadcast_to(rates[s, pl.ds(start, SUBL), :][offset : offset + 1], (SUBL, LANES))
+        for s in range(2)
+    )
+    centre = 1.0 - 6.0 * KT - sx - sy
+    if offset == 0:
+        centre = centre - jnp.where(z == 0, HT, 0.0)
     above, below = jnp.minimum(z + 1, zt - 1), jnp.maximum(z - 1, 0)
 
     def get(ref, z_, t, j):
@@ -481,10 +519,10 @@
             nxt_turned = [pltpu.roll(v, LANES - 1, 1) for v in nxt]
         else:
             nxt, nxt_turned = None, [zero] * tiles
-        one = e1[pl.ds(start, SUBL), at][offset : offset + 1]
-        two = jnp.where(alone, 0.0, e2[pl.ds(start, SUBL), at][offset : offset + 1])
-        low = jnp.broadcast_to(jnp.where(odd, one, two), (SUBL, LANES))
-        high = jnp.broadcast_to(jnp.where(odd, two, one), (SUBL, LANES))
+        low, high = (
+            jnp.broadcast_to(halo[s, pl.ds(start, SUBL), at][offset : offset + 1], (SUBL, LANES))
+            for s in range(2)
+        )
         downs = [low] + [pltpu.roll(v, 1, 0) for v in now]
         ups = [pltpu.roll(v, SUBL - 1, 0) for v in now] + [high]
         for t in range(tiles):
@@ -509,19 +547,20 @@
     column = place()[1]
     lanes_at = lambda other: pl.ds(pl.multiple_of(other * width, LANES), width)
     pv[:, lanes_at(column)] = g[0, pl.ds(pl.multiple_of(column * nx, SUBL), nx), :]
-    for k, ref in ((1, e1.at[:, ny:]), (2, x2), (3, x3.at[2 * nx :])):
+    for k, ref in ((1, e1.at[:, ny:]), (2, x2), (3, x3)):
         pv[:, lanes_at(column ^ k)] = ref[nx : 2 * nx, :]
 
 
-def edge_kernel(u, f, urows, frows, x2, x3, e1, e2, g, g_new, own, speeds, ox2, o1, o2, pv, plane):
+def edge_kernel(
+    u, f, mine1, mine2, urows, frows, x2, x3, e1, e2, g, g_new, own, rates, ox2, ox3, o1, o2, pv, plane, halo
+):
     zt, nx, ny = u.shape
     group, column, odd, _ = place()
-    pos = lax.axis_index("len")
-    alone = (pos == 0) | (pos == lax.axis_size("len") - 1)
     gather_floor_top(pv, e1, x2, x3, g)
-    tin_layer(u, f, e1, e2, speeds, 0, 0, plane)
+    fill_halo(halo, e1, e2)
+    tin_layer(u, f, halo, rates, 0, 0, plane)
     plane[...] = plane[...] + HT * pv[...]
-    put_parts(o1.at[:, ny:], ox2, own, plane, g_new.at[0], column, odd)
+    put_parts(o1.at[:, ny:], ox2, ox3, own, plane, g_new.at[0], column, odd)
     rows, lanes = iotas()
     r_first, r_last = rows == 0, rows == SUBL - 1
     l_first, l_last = lanes == 0, lanes == LANES - 1
@@ -534,26 +573,25 @@
         before = pl.ds(pl.multiple_of(jnp.maximum(start - SUBL, 0), SUBL), SUBL)
         after = pl.ds(pl.multiple_of(jnp.minimum(start + SUBL, zt - SUBL), SUBL), SUBL)
         bottom, top = b == 0, b == blocks - 1
-        sx = sy = zero
-        for i in range(SUBL):
-            sx = jnp.where(rows == i, speeds[0, start + i], sx)
-            sy = jnp.where(rows == i, speeds[1, start + i], sy)
+        sx, sy = rates[0, here, :], rates[1, here, :]
         contact = jnp.where(r_first & bottom, HT, 0.0)
         centre = 1.0 - 6.0 * KT - sx - sy - contact
         outs = []
-        for s, (edge, inner, side) in enumerate(((0, 1, 0), (3, 2, nx - 1))):
-            vs = [urows[edge, here, j * LANES : (j + 1) * LANES] for j in range(wide)]
+        def own_row(s, rows_, at):
+            one, two = mine1[rows_, at], mine2[rows_, at]
+            return jnp.where(odd, two, one) if s else jnp.where(odd, one, two)
+
+        for s, side in ((0, 0), (1, nx - 1)):
+            vs = [own_row(s, here, slice(j * LANES, (j + 1) * LANES)) for j in range(wide)]
             east = [pltpu.roll(v, LANES - 1, 1) for v in vs] + [zero]
             west = [zero] + [pltpu.roll(v, 1, 1) for v in vs]
             for j in range(wide):
                 at = slice(j * LANES, (j + 1) * LANES)
-                v, code, inside = vs[j], frows[s, here, at], urows[inner, here, at]
-                one, two = e1[here, at], jnp.where(alone, 0.0, e2[here, at])
-                outside = jnp.where(odd, two, one) if s else jnp.where(odd, one, two)
+                v, code, inside, outside = vs[j], frows[s, here, at], urows[s, here, at], halo[s, here, at]
                 xm, xp = (inside, outside) if s else (outside, inside)
                 ym = jnp.where(l_first, west[j], west[j + 1])
                 yp = jnp.where(l_last, east[j + 1], east[j])
-                above, below = urows[edge, after, at], urows[edge, before, at]
+                above, below = own_row(s, after, at), own_row(s, before, at)
                 above = jnp.where(top, pltpu.roll(v, 1, 0), above)
                 below = jnp.where(bottom, pltpu.roll(v, SUBL - 1, 0), below)
                 above = jnp.where(r_last, pltpu.roll(above, SUBL - 1, 0), pltpu.roll(v, SUBL - 1, 0))
@@ -574,29 +612,25 @@
     lax.fori_loop(0, blocks, block, 0)
 
 
-def edge_sweep(u, f, urows, frows, x2, x3, e1, e2, g, g_new, own, speeds):
+def edge_sweep(u, f, mine1, mine2, urows, frows, x2, x3, e1, e2, g, g_new, own, rates):
     plane = pltpu.VMEM(u.shape[1:], F32)
     return pl.pallas_call(
         edge_kernel,
-        out_shape=[shape(v.shape) for v in (x2, e1, e2)],
-        in_specs=[VMEM] * 11 + [SMEM],
-        out_specs=[VMEM] * 3,
-        scratch_shapes=[plane, plane],
+        out_shape=[shape(v.shape) for v in (x2, x3, e1, e2)],
+        in_specs=[VMEM] * 14,
+        out_specs=[VMEM] * 4,
+        scratch_shapes=[plane, plane, pltpu.VMEM((2, *e2.shape), F32)],
         compiler_params=params(2),
         cost_estimate=cost(0, 4 << 20),
         name="edge",
-    )(*in_vmem(u, f, urows, frows, x2, x3, e1, e2, g, g_new, own), speeds)
-
-
-def tin_kernel(final, u, f, x2, x3, e1, e2, g, speeds, out, *rest):
+    )(*in_vmem(u, f, mine1, mine2, urows, frows, x2, x3, e1, e2, g, g_new, own, rates))
+
+
+def tin_kernel(final, u, f, x2, x3, e1, e2, g, rates, out, ov, pv, halo, sem):
     zt, nx, ny = u.shape
-    if final:
-        ov, rest = rest[0], rest[1:]
-    else:
-        ov = out
-    pv, sem = rest
     step = SUBL
     gather_floor_top(pv, e1, x2, x3, g)
+    fill_halo(halo, e1, e2)
 
     def store(c):
         at = pl.ds(c * step, step)
@@ -605,7 +639,7 @@
     def chunk(c, _):
         start = pl.multiple_of(c * step, SUBL)
         for offset in range(step):
-            tin_layer(u, f, e1, e2, speeds, start, offset, ov.at[start + offset])
+            tin_layer(u, f, halo, rates, start, offset, ov.at[start + offset])
 
         @pl.when(c == 0)
         def _():
@@ -616,88 +650,126 @@
         return 0
 
     lax.fori_loop(0, zt // step, chunk, 0)
-    if final:
-        for c in range(zt // step):
-            store(c).wait()
-
-
-def tin_sweep(final, u, f, x2, x3, e1, e2, g, speeds):
-    zt, nx, ny = u.shape
-    scratch = [pltpu.VMEM((nx, ny), F32), pltpu.SemaphoreType.DMA((zt // SUBL,))]
-    if final:
-        out, spec, scratch = far(u.shape), ANY, [pltpu.VMEM(u.shape, F32)] + scratch
-    else:
-        out, spec = shape(u.shape), VMEM
+    return [store(c) for c in range(zt // step)] if final else []
+
+
+def tin_scratch(dims):
+    zt, nx, ny = dims
+    return [
+        pltpu.VMEM((nx, ny), F32),
+        pltpu.VMEM((2, zt, ny), F32),
+        pltpu.SemaphoreType.DMA((zt // SUBL,)),
+    ]
+
+
+def tin_first(u, f, x2, x3, e1, e2, g, rates):
+    def kernel(u, f, x2, x3, e1, e2, g, rates, out, *scratch):
+        tin_kernel(False, u, f, x2, x3, e1, e2, g, rates, out, out, *scratch)
+
     return pl.pallas_call(
-        functools.partial(tin_kernel, final),
-        out_shape=out,
-        in_specs=[VMEM] * 7 + [SMEM],
-        out_specs=spec,
-        scratch_shapes=scratch,
-        compiler_params=params(6 if final else 2),
+        kernel,
+        out_shape=shape(u.shape),
+        in_specs=[VMEM] * 8,
+        out_specs=VMEM,
+        scratch_shapes=tin_scratch(u.shape),
+        compiler_params=params(2),
         cost_estimate=cost(0, 20 << 20),
-        name="tin_sweep",
-    )(*in_vmem(u, f, x2, x3, e1, e2, g), speeds)
+        name="tin_first",
+    )(*in_vmem(u, f, x2, x3, e1, e2, g, rates))
+
+
+def last_sweep(u, f, x2, x3, x1, e2, g, rates, coefs, z1, z2, y1, y2, own, kc, kr):
+    def kernel(
+        u, f, x2, x3, x1, e2, g, ce, cw, cn, cz, z1, z2, y1, y2, own, kc, kr, rates,
+        u_out, g_out, uv, gv, *scratch
+    ):
+        stores = tin_kernel(
+            True, u, f, x2, x3, x1, e2, g, rates, u_out, uv, *scratch[:3]
+        )
+        stores += floor_kernel(
+            False, g, ce, cw, cn, cz, u, x1, x2, x3, z1, z2, y1, y2, own, kc, kr, g_out, gv,
+            *scratch[3:]
+        )
+        for copy in stores:
+            copy.wait()
+
+    return pl.pallas_call(
+        kernel,
+        out_shape=[far(u.shape), far(g.shape)],
+        in_specs=[VMEM] * 19,
+        out_specs=[ANY] * 2,
+        scratch_shapes=[pltpu.VMEM(u.shape, F32), pltpu.VMEM(g.shape, F32)]
+        + tin_scratch(u.shape)
+        + floor_scratch(g.shape),
+        compiler_params=params(10),
+        cost_estimate=cost(0, 36 << 20),
+        name="last_sweep",
+    )(*in_vmem(u, f, x2, x3, x1, e2, g, *coefs, z1, z2, y1, y2, own, kc, kr, rates))
 
 
 def local(tin_temp, flow_code, speeds, floor_temp, material, conductivity):
     u, f, g, m = tin_temp, flow_code, floor_temp[0], material[0]
     zt, nx, ny = u.shape
     nr, cx, width = g.shape
-    e1, e2, x2, z1, z2, own, gv, mv = pl.pallas_call(
+    e1, e2, x2, x3, z1, z2, own, gv, mv, rates, halves = pl.pallas_call(
         pack_kernel,
         out_shape=[
             shape((zt, ny + 2 * LANES)),
             shape((zt, ny)),
-            shape((2 * nx + cx, width)),
+            shape((2 * nx, width)),
+            shape((cx, 2 * LANES)),
             shape((2 * nr, width)),
             shape((2 * nr, width)),
             shape((2, cx, LANES)),
             shape(g.shape),
             shape(g.shape, jnp.int32),
+            shape((2, zt, LANES)),
+            shape((conductivity.shape[0], SUBL, LANES)),
         ],
-        in_specs=[ANY, ANY, ANY, SMEM],
-        out_specs=[VMEM] * 8,
+        in_specs=[ANY] * 5,
+        out_specs=[VMEM] * 11,
         scratch_shapes=[
             pltpu.VMEM((2, cx, LANES), jnp.int32),
             pltpu.VMEM((nx, ny), F32),
             pltpu.VMEM((2, nr, width), jnp.int32),
-            pltpu.SemaphoreType.DMA((2 * nr // SUBL + 7,)),
+            pltpu.VMEM(speeds.shape, F32),
+            pltpu.VMEM((1, conductivity.shape[0]), F32),
+            pltpu.SemaphoreType.DMA((2 * nr // SUBL + 9,)),
         ],
         compiler_params=params(2),
         cost_estimate=cost(0, 12 << 20),
         name="pack",
-    )(*in_hbm(u, floor_temp, material), conductivity)
-    x2 = swap(x2, "x2")
+    )(*in_hbm(u, floor_temp, material, speeds, conductivity[None]))
+    mine1, mine2 = e1, e2
+    e1, e2 = swap(e1, "e1"), swap(e2, "e2")
+    e1, x3 = lax.optimization_barrier((e1, x3))
+    x2, x3 = swap(x2, "x2"), swap(x3, "x3")
     y1, y2 = swap(z1, "z1"), swap(z2, "z2")
-    e1, e2 = swap(e1, "e1"), swap(e2, "e2")
     *coefs, urows, frows = pl.pallas_call(
         coefficients_kernel,
         out_shape=[shape(g.shape)] * 4
-        + [shape((4, zt, ny)), shape((2, zt, ny), jnp.int32)],
-        in_specs=[VMEM, SMEM, ANY, ANY],
+        + [shape((2, zt, ny)), shape((2, zt, ny), jnp.int32)],
+        in_specs=[VMEM, VMEM, ANY, ANY],
         out_specs=[VMEM] * 6,
-        scratch_shapes=[pltpu.VMEM(g.shape, F32), pltpu.SemaphoreType.DMA((6,))],
+        scratch_shapes=[pltpu.VMEM(g.shape, F32), pltpu.SemaphoreType.DMA((4,))],
         compiler_params=params(6),
         cost_estimate=cost(0, 16 << 20),
         name="coefficients",
-    )(*in_vmem(mv), conductivity, *in_hbm(u, f))
-    x2, coefs[0] = lax.optimization_barrier((x2, coefs[0]))
-    x3 = swap(x2, "e1")
-    g1, own1, z1, z2, kc, kr = floor_sweep(
-        True, gv, coefs, u, e1, x2, x3, z1, z2, y1, y2, own
+    )(*in_vmem(mv, halves), *in_hbm(u, f))
+    g1, own1, z1, z2, kc, kr = floor_first(
+        gv, coefs, u, e1, x2, x3, z1, z2, y1, y2, own, halves
     )
-    w2, w1, d2 = edge_sweep(u, f, urows, frows, x2, x3, e1, e2, gv, g1, own1, speeds)
-    w2 = swap(w2, "x2")
+    w2, w3, w1, d2 = edge_sweep(
+        u, f, mine1, mine2, urows, frows, x2, x3, e1, e2, gv, g1, own1, rates
+    )
+    w1, d2 = swap(w1, "e1"), swap(d2, "e2")
+    w1, w3 = lax.optimization_barrier((w1, w3))
+    w2, w3 = swap(w2, "x2"), swap(w3, "x3")
     y1, y2 = swap(z1, "z1"), swap(z2, "z2")
-    w1, d2 = swap(w1, "e1"), swap(d2, "e2")
-    u1 = tin_sweep(False, u, f, x2, x3, e1, e2, gv, speeds)
-    w2, u1 = lax.optimization_barrier((w2, u1))
-    w3 = swap(w2, "e1")
-    (g2,) = floor_sweep(
-        False, g1, coefs, u1, w1, w2, w3, z1, z2, y1, y2, own1, (kc, kr)
+    u1 = tin_first(u, f, x2, x3, e1, e2, gv, rates)
+    u2, g2 = last_sweep(
+        u1, f, w2, w3, w1, d2, g1, rates, coefs, z1, z2, y1, y2, own1, kc, kr
     )
-    u2 = tin_sweep(True, u1, f, w2, w3, w1, d2, g1, speeds)
     return u2, g2[None]
 
 

time: 48 us -> 40.6 us (0.85); the launches traced: 47.2 us -> 40.5 us
  waiting for transfers between devices: 8.44 us -> 4.37 us
  Pallas kernels: 27.1 us -> 23.8 us
  starting transfers between devices: 10.2 us -> 11.5 us
  local copies, waits for them, and re-layouts: 0.67 us -> 0.01 us
    ppermute x12, waiting for transfers between devices: 8.44 us -> 4.37 us  [swap(): return lax.ppermute(value, ('grp', 'len'), pairs)]
    pallas_call x5 -> x4, Pallas kernels: 19.5 us -> 17.2 us  [the longest x1 7.65 us: last_sweep(): pl.pallas_call(kernel, out_shape=[far(u.shape), far(g.shape)], in_specs=[...]
    ppermute x12, starting transfers between devices: 10.2 us -> 11.5 us  [swap(): return lax.ppermute(value, ('grp', 'len'), pairs)]
    unnamed x10 -> x4, local copies, waits for them, and re-layouts: 0.67 us -> 0.01 us
    pallas_call x1, Pallas kernels: 3.72 us -> 3.12 us  [local(): pl.pallas_call(coefficients_kernel, out_shape=[shape(g.shape)] * 4 + [sha...]
  transfers between devices with their start and end apart: 12 -> 12, of which waited for: 3 -> 3; matrix products, arithmetic and copies ran while one was open for 0% -> 0% of each run, Pallas kernels for 38% -> 29%
where the time goes in v2:
time: 40.6 us; the launch traced here: 40.5 us
  Pallas kernels  23.8 us (59%)
  starting transfers between devices  11.5 us (28%)
  waiting for transfers between devices  4.37 us (11%)
  between operations  0.74 us (2%)
    ppermute x12, starting transfers between devices, swap(): return lax.ppermute(value, ('grp', 'len'), pairs)  11.5 us
    pallas_call x1, Pallas kernels, last_sweep(): pl.pallas_call(kernel, out_shape=[far(u.shape), far(g.shape)], in_specs=[...  7.65 us
    pallas_call x1, Pallas kernels, floor_first(): pl.pallas_call(kernel, out_shape=[shape(g.shape), shape(own.shape), shape...  4.55 us
    ppermute x12, waiting for transfers between devices, swap(): return lax.ppermute(value, ('grp', 'len'), pairs)  4.37 us
    pallas_call x1, Pallas kernels, tin_first(): pl.pallas_call(kernel, out_shape=shape(u.shape), in_specs=[VMEM] * 8, out...  3.92 us
    pallas_call x1, Pallas kernels, local(): pl.pallas_call(pack_kernel, out_shape=[shape((zt, ny + 2 * LANES)), shape...  3.48 us
    pallas_call x1, Pallas kernels, local(): pl.pallas_call(coefficients_kernel, out_shape=[shape(g.shape)] * 4 + [sha...  3.12 us
    pallas_call x1, Pallas kernels, edge_sweep(): pl.pallas_call(edge_kernel, out_shape=[shape(v.shape) for v in (x2, x3, e...  1.11 us
  transfers between devices with their start and end apart: 12, of which 3 were waited for; matrix products, arithmetic and copies ran while one was open for 0% of the time, Pallas kernels for 29%

profile of v2, /device:TPU:8, one launch (start us, length us, event | category | flops | bytes accessed | tf_op | source)
XLA Modules:
  0.0 40.5 jit_solution(935964078391719664)
XLA Ops:
  0.6 3.5 %pack.1 = (f32[64,1280]{1,0:T(8,128)S(1)}, f32[64,1024]{1,0:T(8,128)S(1)}, f32[32,256]{1,0:T(8,128)S(1)}, f32[64,256]{1,0:T(8,128)S(1)}, f32[96,256]{1,0:T(8,128...) custom-call(f32[64,16,1024]{2,1,0:T(8,128)} %u.7, ...), custom_call_target="tpu_custom_call" | custom-call | bytes 12582912 | tf_op jit(solution)/shard_map/pack/pallas_call | solution.py:714
  4.1 0.1 collective-permute-start.1
  4.2 1.5 %collective-permute-start.3 = (f32[64,1024]{1,0:T(8,128)S(1)}, f32[64,1024]{1,0:T(8,128)S(1)}, u32[]{:S(2)}, u32[]{:S(2)}) collective-permute-start(f32[64,1024]{1,0:T(8,128)S(1)} %get-tuple-element.40.mine2), channel_id=1, source_target_pairs={{0,16},{1,2},{2,1},{3,4},{4,3},{5,6},{6,5},{7,8},{8,7},{9,10},{10,... | collective-permute-start | bytes 786440 | tf_op jit(solution)/shard_map/ppermute | solution.py:78
  5.7 0.5 %collective-permute-start.4 = (f32[96,256]{1,0:T(8,128)S(1)}, f32[96,256]{1,0:T(8,128)S(1)}, u32[]{:S(2)}, u32[]{:S(2)}) collective-permute-start(f32[96,256]{1,0:T(8,128)S(1)} %get-tuple-element.51.refs_9_), channel_id=1, source_target_pairs={{0,4},{1,5},{2,6},{3,7},{4,0},{5,1},{6,2},{7,3},{8,12},{9,13},{10,... | collective-permute-start | bytes 294920 | tf_op jit(solution)/shard_map/ppermute | solution.py:78
  6.2 2.7 %collective-permute-start.5 = (f32[96,256]{1,0:T(8,128)S(1)}, f32[96,256]{1,0:T(8,128)S(1)}, u32[]{:S(2)}, u32[]{:S(2)}) collective-permute-start(f32[96,256]{1,0:T(8,128)S(1)} %get-tuple-element.52.refs_10_), channel_id=1, source_target_pairs={{0,1},{1,0},{2,3},{3,2},{4,8},{5,9},{6,10},{7,11},{8,4},{9,5},{10,... | collective-permute-start | bytes 294920 | tf_op jit(solution)/shard_map/ppermute | solution.py:78
  8.9 0.0 collective-permute-done.1.e1.refs_6_
  8.9 0.8 %collective-permute-start.2 = (f32[64,256]{1,0:T(8,128)S(1)}, f32[64,256]{1,0:T(8,128)S(1)}, u32[]{:S(2)}, u32[]{:S(2)}) collective-permute-start(f32[64,256]{1,0:T(8,128)S(1)} %get-tuple-element.38), channel_id=1, source_target_pairs={{0,3},{1,2},{2,1},{3,0},{4,7},{5,6},{6,5},{7,4},{8,11},{9,10},{10,... | collective-permute-start | bytes 196616 | tf_op jit(solution)/shard_map/ppermute | solution.py:78
  9.6 0.5 %collective-permute-start = (f32[32,256]{1,0:T(8,128)S(1)}, f32[32,256]{1,0:T(8,128)S(1)}, u32[]{:S(2)}, u32[]{:S(2)}) collective-permute-start(f32[32,256]{1,0:T(8,128)S(1)} %get-tuple-element.35), channel_id=1, source_target_pairs={{0,2},{1,3},{2,0},{3,1},{4,6},{5,7},{6,4},{7,5},{8,10},{9,11},{10,... | collective-permute-start | bytes 98312 | tf_op jit(solution)/shard_map/ppermute | solution.py:78
  10.1 0.0 copy-start
  10.1 3.1 %coefficients.1 = (f32[48,64,256]{2,1,0:T(8,128)S(1)}, f32[48,64,256]{2,1,0:T(8,128)S(1)}, f32[48,64,256]{2,1,0:T(8,128)S(1)}, f32[48,64,256]{2,1,0:T(8,128)S(1)...) custom-call(s32[48,64,256]{2,1,0:T(8,128)S(1)} %get-tuple-element.43.m, ...), custom_call_target="tpu_custom_call" | custom-call | bytes 16777216 | tf_op jit(solution)/shard_map/coefficients/pallas_call | solution.py:748
  13.3 2.3 %collective-permute-done.x2.refs_7_ = f32[32,256]{1,0:T(8,128)S(1)} collective-permute-done((f32[32,256]{1,0:T(8,128)S(1)}, f32[32,256]{1,0:T(8,128)S(1)}, u32[]{:S(2)}, u32[]{:S(2)}) %collective-permute-start) | collective-permute-done | bytes 32800 | tf_op jit(solution)/shard_map/ppermute | solution.py:78
  15.6 0.0 collective-permute-done.4.refs_11_
  15.6 0.0 collective-permute-done.5.refs_12_
  15.6 0.0 collective-permute-done.2.x3.refs_8_
  15.6 0.0 copy-done
  15.6 0.0 copy-start.1
  15.6 4.5 %floor_first.1 = (f32[48,64,256]{2,1,0:T(8,128)S(1)}, f32[2,64,128]{2,1,0:T(8,128)S(1)}, f32[48,256]{1,0:T(8,128)S(1)}, f32[48,256]{1,0:T(8,128)S(1)}, f32[2,64,...) custom-call(f32[48,64,256]{2,1,0:T(8,128)S(1)} %get-tuple-element.41.g.refs_0_, ...), custom_call_target="tpu_custom_call" | custom-call | bytes 16777216 | tf_op jit(solution)/shard_map/floor_first/pallas_call | solution.py:465
  20.2 0.0 collective-permute-done.3.e2
  20.2 0.0 copy-done.1
  20.2 1.1 %edge.1 = (f32[32,256]{1,0:T(8,128)S(1)}, f32[64,256]{1,0:T(8,128)S(1)}, f32[64,1280]{1,0:T(8,128)S(1)}, f32[64,1024]{1,0:T(8,128)S(1)}) custom-call(f32[64,16,1024]{2,1,0:T(8,128)S(1)} %copy-done, s32[64,16,1024]{2,1,0:T(8,128)S(1)} %copy-done.1, f32[64,1280]{1,0:T(8,128)S(1)} %get-tuple-element.36.mine1, f32[64,1024]{1,0:T(8,128)S(1)} %get-tuple-element.40.mine2, ...), custom_call_target="tpu_custom_call" | custom-call | bytes 4194304 | tf_op jit(solution)/shard_map/edge/pallas_call | solution.py:617
  21.3 0.1 collective-permute-start.7
  21.4 0.5 %collective-permute-start.9 = (f32[64,1024]{1,0:T(8,128)S(1)}, f32[64,1024]{1,0:T(8,128)S(1)}, u32[]{:S(2)}, u32[]{:S(2)}) collective-permute-start(f32[64,1024]{1,0:T(8,128)S(1)} %get-tuple-element.61), channel_id=1, source_target_pairs={{0,16},{1,2},{2,1},{3,4},{4,3},{5,6},{6,5},{7,8},{8,7},{9,10},{10,... | collective-permute-start | bytes 786440 | tf_op jit(solution)/shard_map/ppermute | solution.py:78
  21.9 1.1 %collective-permute-done.7.x1 = f32[64,1280]{1,0:T(8,128)S(1)} collective-permute-done((f32[64,1280]{1,0:T(8,128)S(1)}, f32[64,1280]{1,0:T(8,128)S(1)}, u32[]{:S(2)}, u32[]{:S(2)}) %collective-permute-start.7) | collective-permute-done | bytes 327712 | tf_op jit(solution)/shard_map/ppermute | solution.py:78
  23.0 1.2 %collective-permute-start.8 = (f32[64,256]{1,0:T(8,128)S(1)}, f32[64,256]{1,0:T(8,128)S(1)}, u32[]{:S(2)}, u32[]{:S(2)}) collective-permute-start(f32[64,256]{1,0:T(8,128)S(1)} %get-tuple-element.59), channel_id=1, source_target_pairs={{0,3},{1,2},{2,1},{3,0},{4,7},{5,6},{6,5},{7,4},{8,11},{9,10},{10,... | collective-permute-start | bytes 196616 | tf_op jit(solution)/shard_map/ppermute | solution.py:78
  24.2 0.4 %collective-permute-start.10 = (f32[48,256]{1,0:T(8,128)S(1)}, f32[48,256]{1,0:T(8,128)S(1)}, u32[]{:S(2)}, u32[]{:S(2)}) collective-permute-start(f32[48,256]{1,0:T(8,128)S(1)} %get-tuple-element.62.z1), channel_id=1, source_target_pairs={{0,4},{1,5},{2,6},{3,7},{4,0},{5,1},{6,2},{7,3},{8,12},{9,13},{10,... | collective-permute-start | bytes 147464 | tf_op jit(solution)/shard_map/ppermute | solution.py:78
  24.7 1.5 %collective-permute-start.11 = (f32[48,256]{1,0:T(8,128)S(1)}, f32[48,256]{1,0:T(8,128)S(1)}, u32[]{:S(2)}, u32[]{:S(2)}) collective-permute-start(f32[48,256]{1,0:T(8,128)S(1)} %get-tuple-element.63.z2), channel_id=1, source_target_pairs={{0,1},{1,0},{2,3},{3,2},{4,8},{5,9},{6,10},{7,11},{8,4},{9,5},{10,... | collective-permute-start | bytes 147464 | tf_op jit(solution)/shard_map/ppermute | solution.py:78
  26.2 1.8 %collective-permute-start.6 = (f32[32,256]{1,0:T(8,128)S(1)}, f32[32,256]{1,0:T(8,128)S(1)}, u32[]{:S(2)}, u32[]{:S(2)}) collective-permute-start(f32[32,256]{1,0:T(8,128)S(1)} %get-tuple-element.56), channel_id=1, source_target_pairs={{0,2},{1,3},{2,0},{3,1},{4,6},{5,7},{6,4},{7,5},{8,10},{9,11},{10,... | collective-permute-start | bytes 98312 | tf_op jit(solution)/shard_map/ppermute | solution.py:78
  28.0 3.9 %tin_first.1.u = f32[64,16,1024]{2,1,0:T(8,128)S(1)} custom-call(f32[64,16,1024]{2,1,0:T(8,128)S(1)} %copy-done, s32[64,16,1024]{2,1,0:T(8,128)S(1)} %copy-done.1, f32[32,256]{1,0:T(8,128)S(1)} %collective-permute-done.x2.refs_7_, f32[64,256]{1,0:T(8,128)S(1)} %collective-permute-done.2.x3.refs_8_, f32[64,1280]{1,0:T(8,128)S(1)} %collective-permute-done.1.e1.refs_6_, ...), custom_call_target="tpu_custom_call" | custom-call | bytes 20971520 | tf_op jit(solution)/shard_map/tin_first/pallas_call | solution.py:669
  31.9 0.9 %collective-permute-done.6.x2 = f32[32,256]{1,0:T(8,128)S(1)} collective-permute-done((f32[32,256]{1,0:T(8,128)S(1)}, f32[32,256]{1,0:T(8,128)S(1)}, u32[]{:S(2)}, u32[]{:S(2)}) %collective-permute-start.6) | collective-permute-done | bytes 32800 | tf_op jit(solution)/shard_map/ppermute | solution.py:78
  32.8 0.0 collective-permute-done.10.y1
  32.8 0.0 collective-permute-done.11.y2
  32.8 0.0 collective-permute-done.9.e2
  32.8 0.0 collective-permute-done.8.x3
  32.8 7.7 %last_sweep.1 = (f32[64,16,1024]{2,1,0:T(8,128)}, f32[48,64,256]{2,1,0:T(8,128)}) custom-call(f32[64,16,1024]{2,1,0:T(8,128)S(1)} %tin_first.1.u, s32[64,16,1024]{2,1,0:T(8,128)S(1)} %copy-done.1, f32[32,256]{1,0:T(8,128)S(1)} %collective-permute-done.6.x2, f32[64,256]{1,0:T(8,128)S(1)} %collective-permute-done.8.x3, ...), custom_call_target="tpu_custom_call" | custom-call | bytes 37748736 | tf_op jit(solution)/shard_map/last_sweep/pallas_call | solution.py:696
Async XLA Ops:
  4.1 4.7 %collective-permute-start.1 = (f32[64,1280]{1,0:T(8,128)S(1)}, f32[64,1280]{1,0:T(8,128)S(1)}, u32[]{:S(2)}, u32[]{:S(2)}) collective-permute-start(f32[64,1280]{1,0:T(8,128)S(1)} %get-tuple-element.36.mine1), channel_id=1, source_target_pairs={{0,1},{1,0},{2,3},{3,2},{4,5},{5,4},{6,7},{7,6},{8,9},{9,8},{10,11... | collective-permute-start | bytes 983048 | tf_op jit(solution)/shard_map/ppermute | solution.py:78
  4.2 16.0 %collective-permute-start.3 = (f32[64,1024]{1,0:T(8,128)S(1)}, f32[64,1024]{1,0:T(8,128)S(1)}, u32[]{:S(2)}, u32[]{:S(2)}) collective-permute-start(f32[64,1024]{1,0:T(8,128)S(1)} %get-tuple-element.40.mine2), channel_id=1, source_target_pairs={{0,16},{1,2},{2,1},{3,4},{4,3},{5,6},{6,5},{7,8},{8,7},{9,10},{10,... | collective-permute-start | bytes 786440 | tf_op jit(solution)/shard_map/ppermute | solution.py:78
  5.7 9.9 %collective-permute-start.4 = (f32[96,256]{1,0:T(8,128)S(1)}, f32[96,256]{1,0:T(8,128)S(1)}, u32[]{:S(2)}, u32[]{:S(2)}) collective-permute-start(f32[96,256]{1,0:T(8,128)S(1)} %get-tuple-element.51.refs_9_), channel_id=1, source_target_pairs={{0,4},{1,5},{2,6},{3,7},{4,0},{5,1},{6,2},{7,3},{8,12},{9,13},{10,... | collective-permute-start | bytes 294920 | tf_op jit(solution)/shard_map/ppermute | solution.py:78
  6.2 9.4 %collective-permute-start.5 = (f32[96,256]{1,0:T(8,128)S(1)}, f32[96,256]{1,0:T(8,128)S(1)}, u32[]{:S(2)}, u32[]{:S(2)}) collective-permute-start(f32[96,256]{1,0:T(8,128)S(1)} %get-tuple-element.52.refs_10_), channel_id=1, source_target_pairs={{0,1},{1,0},{2,3},{3,2},{4,8},{5,9},{6,10},{7,11},{8,4},{9,5},{10,... | collective-permute-start | bytes 294920 | tf_op jit(solution)/shard_map/ppermute | solution.py:78
  8.9 6.7 %collective-permute-start.2 = (f32[64,256]{1,0:T(8,128)S(1)}, f32[64,256]{1,0:T(8,128)S(1)}, u32[]{:S(2)}, u32[]{:S(2)}) collective-permute-start(f32[64,256]{1,0:T(8,128)S(1)} %get-tuple-element.38), channel_id=1, source_target_pairs={{0,3},{1,2},{2,1},{3,0},{4,7},{5,6},{6,5},{7,4},{8,11},{9,10},{10,... | collective-permute-start | bytes 196616 | tf_op jit(solution)/shard_map/ppermute | solution.py:78
  9.6 6.0 %collective-permute-start = (f32[32,256]{1,0:T(8,128)S(1)}, f32[32,256]{1,0:T(8,128)S(1)}, u32[]{:S(2)}, u32[]{:S(2)}) collective-permute-start(f32[32,256]{1,0:T(8,128)S(1)} %get-tuple-element.35), channel_id=1, source_target_pairs={{0,2},{1,3},{2,0},{3,1},{4,6},{5,7},{6,4},{7,5},{8,10},{9,11},{10,... | collective-permute-start | bytes 98312 | tf_op jit(solution)/shard_map/ppermute | solution.py:78
  10.1 5.5 %copy-start = (f32[64,16,1024]{2,1,0:T(8,128)S(1)}, f32[64,16,1024]{2,1,0:T(8,128)}, u32[]{:S(2)}) copy-start(f32[64,16,1024]{2,1,0:T(8,128)} %u.7) | copy-start | bytes 12582916
  15.6 4.6 %copy-start.1 = (s32[64,16,1024]{2,1,0:T(8,128)S(1)}, s32[64,16,1024]{2,1,0:T(8,128)}, u32[]{:S(2)}) copy-start(s32[64,16,1024]{2,1,0:T(8,128)} %f.7) | copy-start | bytes 12582916
  21.3 1.7 %collective-permute-start.7 = (f32[64,1280]{1,0:T(8,128)S(1)}, f32[64,1280]{1,0:T(8,128)S(1)}, u32[]{:S(2)}, u32[]{:S(2)}) collective-permute-start(f32[64,1280]{1,0:T(8,128)S(1)} %get-tuple-element.57), channel_id=1, source_target_pairs={{0,1},{1,0},{2,3},{3,2},{4,5},{5,4},{6,7},{7,6},{8,9},{9,8},{10,11... | collective-permute-start | bytes 983048 | tf_op jit(solution)/shard_map/ppermute | solution.py:78
  21.4 11.4 %collective-permute-start.9 = (f32[64,1024]{1,0:T(8,128)S(1)}, f32[64,1024]{1,0:T(8,128)S(1)}, u32[]{:S(2)}, u32[]{:S(2)}) collective-permute-start(f32[64,1024]{1,0:T(8,128)S(1)} %get-tuple-element.61), channel_id=1, source_target_pairs={{0,16},{1,2},{2,1},{3,4},{4,3},{5,6},{6,5},{7,8},{8,7},{9,10},{10,... | collective-permute-start | bytes 786440 | tf_op jit(solution)/shard_map/ppermute | solution.py:78
  23.0 9.8 %collective-permute-start.8 = (f32[64,256]{1,0:T(8,128)S(1)}, f32[64,256]{1,0:T(8,128)S(1)}, u32[]{:S(2)}, u32[]{:S(2)}) collective-permute-start(f32[64,256]{1,0:T(8,128)S(1)} %get-tuple-element.59), channel_id=1, source_target_pairs={{0,3},{1,2},{2,1},{3,0},{4,7},{5,6},{6,5},{7,4},{8,11},{9,10},{10,... | collective-permute-start | bytes 196616 | tf_op jit(solution)/shard_map/ppermute | solution.py:78
  24.2 8.6 %collective-permute-start.10 = (f32[48,256]{1,0:T(8,128)S(1)}, f32[48,256]{1,0:T(8,128)S(1)}, u32[]{:S(2)}, u32[]{:S(2)}) collective-permute-start(f32[48,256]{1,0:T(8,128)S(1)} %get-tuple-element.62.z1), channel_id=1, source_target_pairs={{0,4},{1,5},{2,6},{3,7},{4,0},{5,1},{6,2},{7,3},{8,12},{9,13},{10,... | collective-permute-start | bytes 147464 | tf_op jit(solution)/shard_map/ppermute | solution.py:78
  24.7 8.1 %collective-permute-start.11 = (f32[48,256]{1,0:T(8,128)S(1)}, f32[48,256]{1,0:T(8,128)S(1)}, u32[]{:S(2)}, u32[]{:S(2)}) collective-permute-start(f32[48,256]{1,0:T(8,128)S(1)} %get-tuple-element.63.z2), channel_id=1, source_target_pairs={{0,1},{1,0},{2,3},{3,2},{4,8},{5,9},{6,10},{7,11},{8,4},{9,5},{10,... | collective-permute-start | bytes 147464 | tf_op jit(solution)/shard_map/ppermute | solution.py:78
  26.2 6.6 %collective-permute-start.6 = (f32[32,256]{1,0:T(8,128)S(1)}, f32[32,256]{1,0:T(8,128)S(1)}, u32[]{:S(2)}, u32[]{:S(2)}) collective-permute-start(f32[32,256]{1,0:T(8,128)S(1)} %get-tuple-element.56), channel_id=1, source_target_pairs={{0,2},{1,3},{2,0},{3,1},{4,6},{5,7},{6,4},{7,5},{8,10},{9,11},{10,... | collective-permute-start | bytes 98312 | tf_op jit(solution)/shard_map/ppermute | solution.py:78

commit v3 on v2

--- a/solution.py
+++ b/solution.py
@@ -234,7 +234,7 @@
     wait_bytes(u.at[:, 0, :], rows_out, sem.at[base + 6])
 
 
-def coefficients_kernel(m, halves, u, f, ce, cw, cn, cz, urows, frows, kv, sem):
+def inner_kernel(m, g, halves, u, f, out, ce, cw, cn, cz, urows, frows, kv, fzv, sem):
     nr, cx, width = m.shape
     nx = u.shape[1]
     picks = [(u.at[:, r, :], urows.at[i]) for i, r in enumerate((1, nx - 2))]
@@ -243,11 +243,13 @@
     for copy in picks:
         copy.start()
     rows, lanes = iotas()
-    r_last, l_first, l_last = rows == SUBL - 1, lanes == 0, lanes == LANES - 1
+    r_first, r_last = rows == 0, rows == SUBL - 1
+    l_first, l_last = lanes == 0, lanes == LANES - 1
     tiles, wide = cx // SUBL, width // LANES
     spans = [slice(j * LANES, (j + 1) * LANES) for j in range(wide)]
     step = SUBL
     values = [halves[i] for i in range(halves.shape[0])]
+    zero = jnp.zeros((SUBL, LANES), F32)
 
     def lookup(ids):
         value = values[0]
@@ -255,80 +257,98 @@
             value = jnp.where(ids == i, values[i], value)
         return value
 
-    def layer(z):
-        before = jnp.maximum(z - 1, 0)
+    for t in range(tiles):
+        rs = slice(t * SUBL, (t + 1) * SUBL)
+        for at in spans:
+            kv[0, rs, at] = lookup(m[0, rs, at])
+    fzv[...] = jnp.zeros_like(fzv)
+    turn = lambda vs, by, axis: [pltpu.roll(v, by, axis) for v in vs]
+
+    def layer(start, offset):
+        z = start + offset
+        above, here, there = z + 1, offset % 2, (offset + 1) % 2
+        last = offset == step - 1
+        if last:
+            above = jnp.minimum(above, nr - 1)
+            scale = jnp.where(z + 1 < nr, 1.0, 0.0)
 
         def tile(t):
             rs = slice(t * SUBL, (t + 1) * SUBL)
-            ks = [lookup(m[z, rs, at]) for at in spans]
-            return ks, [pltpu.roll(k, SUBL - 1, 0) for k in ks]
-
-        ks, ups = tile(0)
+            gs = [g[z, rs, at] for at in spans]
+            ks = [kv[here, rs, at] for at in spans]
+            return gs, ks, turn(gs, SUBL - 1, 0), turn(ks, SUBL - 1, 0)
+
+        now = tile(0)
+        prev = [zero] * wide
         for t in range(tiles):
             rs = slice(t * SUBL, (t + 1) * SUBL)
+            gs, ks, g_up, k_up = now
             if t + 1 < tiles:
-                kn, un = tile(t + 1)
-            east = [pltpu.roll(k, LANES - 1, 1) for k in ks]
-            west = [pltpu.roll(k, 1, 1) for k in ks]
+                now = tile(t + 1)
+            ge, gw = turn(gs, LANES - 1, 1), turn(gs, 1, 1)
+            ke, kw = turn(ks, LANES - 1, 1), turn(ks, 1, 1)
             for j, at in enumerate(spans):
-                k = ks[j]
-                kv[z, rs, at] = k
-                cz[before, rs, at] = kv[before, rs, at] + k
+                v, k = gs[j], ks[j]
+                k_next, v_next = lookup(m[above, rs, at]), g[above, rs, at]
+                if last:
+                    k_next, v_next = scale * k_next, scale * v_next
+                kv[there, rs, at] = k_next
+                below = k + k_next
                 if t + 1 < tiles:
-                    cn[z, rs, at] = k + jnp.where(r_last, un[j], ups[j])
+                    north = k + jnp.where(r_last, now[3][j], k_up[j])
+                    xp = jnp.where(r_last, now[2][j], g_up[j])
                 else:
-                    cn[z, rs, at] = jnp.where(r_last, 0.0, k + ups[j])
+                    north, xp = jnp.where(r_last, 0.0, k + k_up[j]), g_up[j]
                 if j + 1 < wide:
-                    ce[z, rs, at] = k + jnp.where(l_last, east[j + 1], east[j])
+                    east = k + jnp.where(l_last, ke[j + 1], ke[j])
+                    yp = jnp.where(l_last, ge[j + 1], ge[j])
                 else:
-                    ce[z, rs, at] = jnp.where(l_last, 0.0, k + east[j])
+                    east, yp = jnp.where(l_last, 0.0, k + ke[j]), ge[j]
                 if j > 0:
-                    cw[z, rs, at] = k + jnp.where(l_first, west[j - 1], west[j])
+                    west = k + jnp.where(l_first, kw[j - 1], kw[j])
+                    ym = jnp.where(l_first, gw[j - 1], gw[j])
                 else:
-                    cw[z, rs, at] = jnp.where(l_first, 0.0, k + west[j])
-            if t + 1 < tiles:
-                ks, ups = kn, un
+                    west, ym = jnp.where(l_first, 0.0, k + kw[j]), gw[j]
+                ce[z, rs, at], cw[z, rs, at] = east, west
+                cn[z, rs, at], cz[z, rs, at] = north, below
+                fx = north * (xp - v)
+                turned = pltpu.roll(fx, 1, 0)
+                fxm = jnp.where(r_first, prev[j], turned)
+                prev[j] = turned
+                fz = below * (v_next - v)
+                side = east * (yp - v) + west * (ym - v)
+                out[z, rs, at] = v + ((fx - fxm) + side + (fz - fzv[rs, at]))
+                fzv[rs, at] = fz
 
     def chunk(c, _):
+        start = pl.multiple_of(c * step, SUBL)
         for offset in range(step):
-            layer(c * step + offset)
+            layer(start, offset)
         return 0
 
     lax.fori_loop(0, nr // step, chunk, 0)
-    cz[nr - 1, :, :] = kv[nr - 1]
     for copy in picks:
         copy.wait()
 
 
-def floor_kernel(
-    emit, g, ce, cw, cn, cz, u, x1, x2, x3, z1, z2, y1, y2, own, *rest
-):
-    nr, cx, width = g.shape
+def floor_sides(halves, u, x1, x2, x3, z1, z2, y1, y2, own, kc, kr, tcol, trow, bv):
+    nr = kr.shape[1]
     nx, ny = u.shape[1], u.shape[2]
-    if emit:
-        halves, out, own_new, o1, o2, kc, kr = rest[:7]
-        ov, rest = out, rest[7:]
-    else:
-        kc, kr, out, ov = rest[:4]
-        rest = rest[4:]
-    fzv, tcol, trow, bv, sem = rest
+    width = bv.shape[1]
     group, column, odd, godd = place()
-    tiles, wide = cx // SUBL, width // LANES
-    step = SUBL
-    chunks = nr // step
     shift = LANES // 2
     aux = x1.at[:, ny:]
     groups = lax.axis_size("len") // TILE_Y
     known = (group ^ 1) < groups, jnp.where(godd, group + 1 < groups, group > 0)
     one, three = get_columns(aux), get_columns(x3)
     for s, halo in ((0, jnp.where(odd, one, three)), (1, jnp.where(odd, three, one))):
-        if emit:
+        if halves is not None:
             both = half_coded(own[s], halves) + half_coded(halo, halves)
             kc[s, :, :] = pltpu.roll(both, shift, 1)
         tcol[s, :, :] = kc[s] * (halo - own[s])
     for s, (mine, halo) in enumerate(((z1, y1), (z2, y2))):
         halo = jnp.where(known[s], halo[...], 0.0)
-        if emit:
+        if halves is not None:
             kr[s, :, :] = half_coded(mine[nr:, :], halves) + half_coded(halo[nr:, :], halves)
         side = kr[s] * (halo[:nr, :] - mine[:nr, :])
         trow[jnp.where(godd, s, 1 - s), :, :] = side
@@ -336,12 +356,20 @@
     bv[row(column), :] = u[0, :, pl.ds(pl.multiple_of(column * width, LANES), width)]
     for k, ref in ((1, aux), (2, x2), (3, x3)):
         bv[row(column ^ k), :] = ref[:nx, :]
+
+
+def floor_kernel(
+    g, ce, cw, cn, cz, u, x1, x2, x3, z1, z2, y1, y2, own, kc, kr, out, ov, fzv, tcol, trow, bv, sem
+):
+    nr, cx, width = g.shape
+    tiles, wide = cx // SUBL, width // LANES
+    step = SUBL
+    chunks = nr // step
+    floor_sides(None, u, x1, x2, x3, z1, z2, y1, y2, own, kc, kr, tcol, trow, bv)
     rows, lanes = iotas()
     r_first, r_last = rows == 0, rows == SUBL - 1
     l_first, l_last = lanes == 0, lanes == LANES - 1
     fzv[...] = jnp.zeros_like(fzv)
-    if emit:
-        own_new[...] = jnp.zeros_like(own_new)
     spans = [slice(j * LANES, (j + 1) * LANES) for j in range(wide)]
 
     def layer(start, offset):
@@ -398,24 +426,9 @@
             if t + 1 < tiles:
                 gs, ups = gn, un
 
-    def columns(start):
-        for t in range(tiles):
-            rs = slice(t * SUBL, (t + 1) * SUBL)
-            edges = lambda offset: (
-                ov[start + offset, rs, spans[0]],
-                ov[start + offset, rs, spans[-1]],
-            )
-            keep_columns(own_new, 0, start, step, rs, edges)
-
     def store(c):
         at = pl.ds(c * step, step)
         return pltpu.make_async_copy(ov.at[at], out.at[at], sem.at[c])
-
-    def store_rows(c):
-        at = pl.ds(pl.multiple_of(c * step, SUBL), step)
-        low, high = ov.at[at, 0, :], ov.at[at, cx - 1, :]
-        select_copy(godd, (low, o1.at[at]), (high, o1.at[at]), sem.at[chunks + c])
-        select_copy(godd, (high, o2.at[at]), (low, o2.at[at]), sem.at[2 * chunks + c])
 
     def chunk(c, _):
         start = pl.multiple_of(c * step, SUBL)
@@ -426,22 +439,10 @@
         def _():
             ov[0, :, :] = ov[0] + HR * (bv[...] - g[0])
 
-        if emit:
-            store_rows(c)
-            columns(start)
-        else:
-            store(c).start()
+        store(c).start()
         return 0
 
     lax.fori_loop(0, chunks, chunk, 0)
-    if emit:
-        own_new[1, :, :] = pltpu.roll(own_new[1], 1, 1)
-    if emit:
-        for c in range(chunks):
-            at = pl.ds(c * step, step)
-            wait_bytes(ov.at[at, 0, :], o1.at[at], sem.at[chunks + c])
-            wait_bytes(ov.at[at, 0, :], o2.at[at], sem.at[2 * chunks + c])
-        return []
     return [store(c) for c in range(chunks)]
 
 
@@ -456,29 +457,69 @@
     ]
 
 
-def floor_first(g, coefs, u, x1, x2, x3, z1, z2, y1, y2, own, halves):
+def floor_finish(part, g, tcol, trow, bv, out, own, o1, o2, sem):
     nr, cx, width = g.shape
-
-    def kernel(*refs):
-        floor_kernel(True, *refs)
-
-    return pl.pallas_call(
-        kernel,
-        out_shape=[
-            shape(g.shape),
-            shape(own.shape),
-            shape((nr, width)),
-            shape((nr, width)),
-            shape(own.shape),
-            shape((2, nr, width)),
-        ],
-        in_specs=[VMEM] * 15,
-        out_specs=[VMEM] * 6,
-        scratch_shapes=floor_scratch(g.shape),
-        compiler_params=params(2),
-        cost_estimate=cost(0, 16 << 20),
-        name="floor_first",
-    )(*in_vmem(g, *coefs, u, x1, x2, x3, z1, z2, y1, y2, own, halves))
+    godd = place()[3]
+    rows, lanes = iotas()
+    r_first, r_last = rows == 0, rows == SUBL - 1
+    l_first, l_last = lanes == 0, lanes == LANES - 1
+    tiles, wide = cx // SUBL, width // LANES
+    spans = [slice(j * LANES, (j + 1) * LANES) for j in range(wide)]
+    step = SUBL
+    chunks = nr // step
+    own[...] = jnp.zeros_like(own)
+
+    def rows_of(c):
+        at = pl.ds(pl.multiple_of(c * step, SUBL), step)
+        low, high = out.at[at, 0, :], out.at[at, cx - 1, :]
+        return low, high, o1.at[at], o2.at[at]
+
+    def chunk(c, _):
+        start = pl.multiple_of(c * step, SUBL)
+
+        for offset in range(step):
+            z = start + offset
+            back = lax.rem(LANES - z, LANES)
+            for t in range(tiles):
+                rs = slice(t * SUBL, (t + 1) * SUBL)
+                for j, at in enumerate(spans):
+                    v = part[z, rs, at]
+                    if j == 0:
+                        west = pltpu.roll(tcol[0, rs, :], back, 1)
+                        v = v + jnp.where(l_first, west, 0.0)
+                    if j + 1 == wide:
+                        east = pltpu.roll(tcol[1, rs, :], LANES - 1 - z, 1)
+                        v = v + jnp.where(l_last, east, 0.0)
+                    for s, edge, mask in ((0, 0, r_first), (1, tiles - 1, r_last)):
+                        if t == edge:
+                            side = trow[s, pl.ds(start, SUBL), at][offset : offset + 1]
+                            v = v + jnp.where(mask, jnp.broadcast_to(side, v.shape), 0.0)
+                    out[z, rs, at] = v
+
+        @pl.when(c == 0)
+        def _():
+            out[0, :, :] = out[0] + HR * (bv[...] - g[0])
+
+        low, high, to1, to2 = rows_of(c)
+        select_copy(godd, (low, to1), (high, to1), sem.at[c])
+        select_copy(godd, (high, to2), (low, to2), sem.at[chunks + c])
+        for t in range(tiles):
+            rs = slice(t * SUBL, (t + 1) * SUBL)
+            edges = lambda offset: (
+                out[start + offset, rs, spans[0]],
+                out[start + offset, rs, spans[-1]],
+            )
+            keep_columns(own, 0, start, step, rs, edges)
+        return 0
+
+    lax.fori_loop(0, chunks, chunk, 0)
+    own[1, :, :] = pltpu.roll(own[1], 1, 1)
+    copies = []
+    for c in range(chunks):
+        low, _, to1, to2 = rows_of(c)
+        copies.append(pltpu.make_async_copy(low, to1, sem.at[c]))
+        copies.append(pltpu.make_async_copy(low, to2, sem.at[chunks + c]))
+    return copies
 
 
 def fill_halo(halo, e1, e2):
@@ -552,15 +593,19 @@
 
 
 def edge_kernel(
-    u, f, mine1, mine2, urows, frows, x2, x3, e1, e2, g, g_new, own, rates, ox2, ox3, o1, o2, pv, plane, halo
+    u, f, mine1, mine2, urows, frows, x2, x3, e1, e2, g, part, z1, z2, y1, y2, own, halves, rates,
+    ox2, ox3, o1, o2, g_new, own_new, oz1, oz2, kc, kr,
+    pv, plane, halo, tcol, trow, bv, sem
 ):
+    floor_sides(halves, u, e1, x2, x3, z1, z2, y1, y2, own, kc, kr, tcol, trow, bv)
+    copies = floor_finish(part, g, tcol, trow, bv, g_new, own_new, oz1, oz2, sem)
     zt, nx, ny = u.shape
     group, column, odd, _ = place()
     gather_floor_top(pv, e1, x2, x3, g)
     fill_halo(halo, e1, e2)
     tin_layer(u, f, halo, rates, 0, 0, plane)
     plane[...] = plane[...] + HT * pv[...]
-    put_parts(o1.at[:, ny:], ox2, ox3, own, plane, g_new.at[0], column, odd)
+    put_parts(o1.at[:, ny:], ox2, ox3, own_new, plane, g_new.at[0], column, odd)
     rows, lanes = iotas()
     r_first, r_last = rows == 0, rows == SUBL - 1
     l_first, l_last = lanes == 0, lanes == LANES - 1
@@ -610,20 +655,31 @@
         return 0
 
     lax.fori_loop(0, blocks, block, 0)
-
-
-def edge_sweep(u, f, mine1, mine2, urows, frows, x2, x3, e1, e2, g, g_new, own, rates):
+    for copy in copies:
+        copy.wait()
+
+
+def edge_sweep(
+    u, f, mine1, mine2, urows, frows, x2, x3, e1, e2, g, part, z1, z2, y1, y2, own, halves, rates
+):
     plane = pltpu.VMEM(u.shape[1:], F32)
+    nr, cx, width = g.shape
     return pl.pallas_call(
         edge_kernel,
-        out_shape=[shape(v.shape) for v in (x2, x3, e1, e2)],
-        in_specs=[VMEM] * 14,
-        out_specs=[VMEM] * 4,
-        scratch_shapes=[plane, plane, pltpu.VMEM((2, *e2.shape), F32)],
+        out_shape=[shape(v.shape) for v in (x2, x3, e1, e2, g, own)]
+        + [shape((nr, width))] * 2
+        + [shape(own.shape), shape((2, nr, width))],
+        in_specs=[VMEM] * 19,
+        out_specs=[VMEM] * 10,
+        scratch_shapes=[plane, plane, pltpu.VMEM((2, *e2.shape), F32), *floor_scratch(g.shape)[1:]],
         compiler_params=params(2),
-        cost_estimate=cost(0, 4 << 20),
+        cost_estimate=cost(0, 10 << 20),
         name="edge",
-    )(*in_vmem(u, f, mine1, mine2, urows, frows, x2, x3, e1, e2, g, g_new, own, rates))
+    )(
+        *in_vmem(
+            u, f, mine1, mine2, urows, frows, x2, x3, e1, e2, g, part, z1, z2, y1, y2, own, halves, rates
+        )
+    )
 
 
 def tin_kernel(final, u, f, x2, x3, e1, e2, g, rates, out, ov, pv, halo, sem):
@@ -687,7 +743,7 @@
             True, u, f, x2, x3, x1, e2, g, rates, u_out, uv, *scratch[:3]
         )
         stores += floor_kernel(
-            False, g, ce, cw, cn, cz, u, x1, x2, x3, z1, z2, y1, y2, own, kc, kr, g_out, gv,
+            g, ce, cw, cn, cz, u, x1, x2, x3, z1, z2, y1, y2, own, kc, kr, g_out, gv,
             *scratch[3:]
         )
         for copy in stores:
@@ -745,22 +801,23 @@
     e1, x3 = lax.optimization_barrier((e1, x3))
     x2, x3 = swap(x2, "x2"), swap(x3, "x3")
     y1, y2 = swap(z1, "z1"), swap(z2, "z2")
-    *coefs, urows, frows = pl.pallas_call(
-        coefficients_kernel,
-        out_shape=[shape(g.shape)] * 4
+    part, *coefs, urows, frows = pl.pallas_call(
+        inner_kernel,
+        out_shape=[shape(g.shape)] * 5
         + [shape((2, zt, ny)), shape((2, zt, ny), jnp.int32)],
-        in_specs=[VMEM, VMEM, ANY, ANY],
-        out_specs=[VMEM] * 6,
-        scratch_shapes=[pltpu.VMEM(g.shape, F32), pltpu.SemaphoreType.DMA((4,))],
-        compiler_params=params(6),
-        cost_estimate=cost(0, 16 << 20),
-        name="coefficients",
-    )(*in_vmem(mv, halves), *in_hbm(u, f))
-    g1, own1, z1, z2, kc, kr = floor_first(
-        gv, coefs, u, e1, x2, x3, z1, z2, y1, y2, own, halves
-    )
-    w2, w3, w1, d2 = edge_sweep(
-        u, f, mine1, mine2, urows, frows, x2, x3, e1, e2, gv, g1, own1, rates
+        in_specs=[VMEM] * 3 + [ANY] * 2,
+        out_specs=[VMEM] * 7,
+        scratch_shapes=[
+            pltpu.VMEM((2, cx, width), F32),
+            pltpu.VMEM((cx, width), F32),
+            pltpu.SemaphoreType.DMA((4,)),
+        ],
+        compiler_params=params(2),
+        cost_estimate=cost(0, 24 << 20),
+        name="inner",
+    )(*in_vmem(mv, gv, halves), *in_hbm(u, f))
+    w2, w3, w1, d2, g1, own1, z1, z2, kc, kr = edge_sweep(
+        u, f, mine1, mine2, urows, frows, x2, x3, e1, e2, gv, part, z1, z2, y1, y2, own, halves, rates
     )
     w1, d2 = swap(w1, "e1"), swap(d2, "e2")
     w1, w3 = lax.optimization_barrier((w1, w3))

time: 40.6 us -> 38.6 us (0.951)
  waiting for transfers between devices: 4.37 us -> 3.33 us
  Pallas kernels: 23.8 us -> 22.9 us
    pallas_call x2 -> x1, Pallas kernels: 7.67 us -> 4.16 us  [local(): pl.pallas_call(inner_kernel, out_shape=[shape(g.shape)] * 5 + [shape((2,...]
    pallas_call x1, Pallas kernels: 1.11 us -> 3.67 us  [edge_sweep(): pl.pallas_call(edge_kernel, out_shape=[shape(v.shape) for v in (x2, x3, e...]
    ppermute x12, waiting for transfers between devices: 4.37 us -> 3.33 us  [swap(): return lax.ppermute(value, ('grp', 'len'), pairs)]
  transfers between devices with their start and end apart: 12 -> 12, of which waited for: 3 -> 3; matrix products, arithmetic and copies ran while one was open for 0% -> 0% of each run, Pallas kernels for 29% -> 21%
where the time goes in v3:
time: 38.6 us; the launch traced here: 38.5 us
  Pallas kernels  22.9 us (59%)
  starting transfers between devices  11.5 us (30%)
  waiting for transfers between devices  3.33 us (9%)
  between operations  0.73 us (2%)
    ppermute x12, starting transfers between devices, swap(): return lax.ppermute(value, ('grp', 'len'), pairs)  11.5 us
    pallas_call x1, Pallas kernels, last_sweep(): pl.pallas_call(kernel, out_shape=[far(u.shape), far(g.shape)], in_specs=[...  7.65 us
    pallas_call x1, Pallas kernels, local(): pl.pallas_call(inner_kernel, out_shape=[shape(g.shape)] * 5 + [shape((2,...  4.16 us
    pallas_call x1, Pallas kernels, tin_first(): pl.pallas_call(kernel, out_shape=shape(u.shape), in_specs=[VMEM] * 8, out...  3.92 us
    pallas_call x1, Pallas kernels, edge_sweep(): pl.pallas_call(edge_kernel, out_shape=[shape(v.shape) for v in (x2, x3, e...  3.67 us
    pallas_call x1, Pallas kernels, local(): pl.pallas_call(pack_kernel, out_shape=[shape((zt, ny + 2 * LANES)), shape...  3.49 us
    ppermute x12, waiting for transfers between devices, swap(): return lax.ppermute(value, ('grp', 'len'), pairs)  3.33 us
  transfers between devices with their start and end apart: 12, of which 3 were waited for; matrix products, arithmetic and copies ran while one was open for 0% of the time, Pallas kernels for 21%

profile of v3, /device:TPU:8, one launch (start us, length us, event | category | flops | bytes accessed | tf_op | source)
XLA Modules:
  0.0 38.5 jit_solution(12284822100221045445)
XLA Ops:
  0.6 3.5 %pack.1 = (f32[64,1280]{1,0:T(8,128)S(1)}, f32[64,1024]{1,0:T(8,128)S(1)}, f32[32,256]{1,0:T(8,128)S(1)}, f32[64,256]{1,0:T(8,128)S(1)}, f32[96,256]{1,0:T(8,128...) custom-call(f32[64,16,1024]{2,1,0:T(8,128)} %u.7, ...), custom_call_target="tpu_custom_call" | custom-call | bytes 12582912 | tf_op jit(solution)/shard_map/pack/pallas_call | solution.py:770
  4.1 0.1 collective-permute-start.1
  4.2 1.5 %collective-permute-start.3 = (f32[64,1024]{1,0:T(8,128)S(1)}, f32[64,1024]{1,0:T(8,128)S(1)}, u32[]{:S(2)}, u32[]{:S(2)}) collective-permute-start(f32[64,1024]{1,0:T(8,128)S(1)} %get-tuple-element.41.mine2), channel_id=1, source_target_pairs={{0,16},{1,2},{2,1},{3,4},{4,3},{5,6},{6,5},{7,8},{8,7},{9,10},{10,... | collective-permute-start | bytes 786440 | tf_op jit(solution)/shard_map/ppermute | solution.py:78
  5.7 0.5 %collective-permute-start.4 = (f32[96,256]{1,0:T(8,128)S(1)}, f32[96,256]{1,0:T(8,128)S(1)}, u32[]{:S(2)}, u32[]{:S(2)}) collective-permute-start(f32[96,256]{1,0:T(8,128)S(1)} %get-tuple-element.49.z1), channel_id=1, source_target_pairs={{0,4},{1,5},{2,6},{3,7},{4,0},{5,1},{6,2},{7,3},{8,12},{9,13},{10,... | collective-permute-start | bytes 294920 | tf_op jit(solution)/shard_map/ppermute | solution.py:78
  6.2 2.7 %collective-permute-start.5 = (f32[96,256]{1,0:T(8,128)S(1)}, f32[96,256]{1,0:T(8,128)S(1)}, u32[]{:S(2)}, u32[]{:S(2)}) collective-permute-start(f32[96,256]{1,0:T(8,128)S(1)} %get-tuple-element.50.z2), channel_id=1, source_target_pairs={{0,1},{1,0},{2,3},{3,2},{4,8},{5,9},{6,10},{7,11},{8,4},{9,5},{10,... | collective-permute-start | bytes 294920 | tf_op jit(solution)/shard_map/ppermute | solution.py:78
  8.9 0.0 collective-permute-done.1.e1
  8.9 0.8 %collective-permute-start.2 = (f32[64,256]{1,0:T(8,128)S(1)}, f32[64,256]{1,0:T(8,128)S(1)}, u32[]{:S(2)}, u32[]{:S(2)}) collective-permute-start(f32[64,256]{1,0:T(8,128)S(1)} %get-tuple-element.39), channel_id=1, source_target_pairs={{0,3},{1,2},{2,1},{3,0},{4,7},{5,6},{6,5},{7,4},{8,11},{9,10},{10,... | collective-permute-start | bytes 196616 | tf_op jit(solution)/shard_map/ppermute | solution.py:78
  9.6 0.5 %collective-permute-start = (f32[32,256]{1,0:T(8,128)S(1)}, f32[32,256]{1,0:T(8,128)S(1)}, u32[]{:S(2)}, u32[]{:S(2)}) collective-permute-start(f32[32,256]{1,0:T(8,128)S(1)} %get-tuple-element.36), channel_id=1, source_target_pairs={{0,2},{1,3},{2,0},{3,1},{4,6},{5,7},{6,4},{7,5},{8,10},{9,11},{10,... | collective-permute-start | bytes 98312 | tf_op jit(solution)/shard_map/ppermute | solution.py:78
  10.1 0.0 copy-start
  10.1 0.0 copy-start.1
  10.1 4.2 %inner.1 = (f32[48,64,256]{2,1,0:T(8,128)S(1)}, f32[48,64,256]{2,1,0:T(8,128)S(1)}, f32[48,64,256]{2,1,0:T(8,128)S(1)}, f32[48,64,256]{2,1,0:T(8,128)S(1)}, f32[...) custom-call(s32[48,64,256]{2,1,0:T(8,128)S(1)} %get-tuple-element.44.m, ...), custom_call_target="tpu_custom_call" | custom-call | bytes 25165824 | tf_op jit(solution)/shard_map/inner/pallas_call | solution.py:804
  14.3 1.3 %collective-permute-done.x2 = f32[32,256]{1,0:T(8,128)S(1)} collective-permute-done((f32[32,256]{1,0:T(8,128)S(1)}, f32[32,256]{1,0:T(8,128)S(1)}, u32[]{:S(2)}, u32[]{:S(2)}) %collective-permute-start) | collective-permute-done | bytes 32800 | tf_op jit(solution)/shard_map/ppermute | solution.py:78
  15.6 0.0 collective-permute-done.4.y1
  15.6 0.0 collective-permute-done.5.y2
  15.6 0.0 collective-permute-done.3.e2
  15.6 0.0 collective-permute-done.2.x3
  15.6 0.0 copy-done
  15.6 0.0 copy-done.1
  15.6 3.7 %edge.1 = (f32[32,256]{1,0:T(8,128)S(1)}, f32[64,256]{1,0:T(8,128)S(1)}, f32[64,1280]{1,0:T(8,128)S(1)}, f32[64,1024]{1,0:T(8,128)S(1)}, f32[48,64,256]{2,1,0:T(...) custom-call(f32[64,16,1024]{2,1,0:T(8,128)S(1)} %copy-done, ...), custom_call_target="tpu_custom_call" | custom-call | bytes 10485760 | tf_op jit(solution)/shard_map/edge/pallas_call | solution.py:667
  19.3 0.1 collective-permute-start.7
  19.4 0.5 %collective-permute-start.9 = (f32[64,1024]{1,0:T(8,128)S(1)}, f32[64,1024]{1,0:T(8,128)S(1)}, u32[]{:S(2)}, u32[]{:S(2)}) collective-permute-start(f32[64,1024]{1,0:T(8,128)S(1)} %get-tuple-element.57), channel_id=1, source_target_pairs={{0,16},{1,2},{2,1},{3,4},{4,3},{5,6},{6,5},{7,8},{8,7},{9,10},{10,... | collective-permute-start | bytes 786440 | tf_op jit(solution)/shard_map/ppermute | solution.py:78
  19.9 1.1 %collective-permute-done.7.x1 = f32[64,1280]{1,0:T(8,128)S(1)} collective-permute-done((f32[64,1280]{1,0:T(8,128)S(1)}, f32[64,1280]{1,0:T(8,128)S(1)}, u32[]{:S(2)}, u32[]{:S(2)}) %collective-permute-start.7) | collective-permute-done | bytes 327712 | tf_op jit(solution)/shard_map/ppermute | solution.py:78
  21.0 1.2 %collective-permute-start.8 = (f32[64,256]{1,0:T(8,128)S(1)}, f32[64,256]{1,0:T(8,128)S(1)}, u32[]{:S(2)}, u32[]{:S(2)}) collective-permute-start(f32[64,256]{1,0:T(8,128)S(1)} %get-tuple-element.55), channel_id=1, source_target_pairs={{0,3},{1,2},{2,1},{3,0},{4,7},{5,6},{6,5},{7,4},{8,11},{9,10},{10,... | collective-permute-start | bytes 196616 | tf_op jit(solution)/shard_map/ppermute | solution.py:78
  22.2 0.4 %collective-permute-start.10 = (f32[48,256]{1,0:T(8,128)S(1)}, f32[48,256]{1,0:T(8,128)S(1)}, u32[]{:S(2)}, u32[]{:S(2)}) collective-permute-start(f32[48,256]{1,0:T(8,128)S(1)} %get-tuple-element.63.z1), channel_id=1, source_target_pairs={{0,4},{1,5},{2,6},{3,7},{4,0},{5,1},{6,2},{7,3},{8,12},{9,13},{10,... | collective-permute-start | bytes 147464 | tf_op jit(solution)/shard_map/ppermute | solution.py:78
  22.7 1.5 %collective-permute-start.11 = (f32[48,256]{1,0:T(8,128)S(1)}, f32[48,256]{1,0:T(8,128)S(1)}, u32[]{:S(2)}, u32[]{:S(2)}) collective-permute-start(f32[48,256]{1,0:T(8,128)S(1)} %get-tuple-element.64.z2), channel_id=1, source_target_pairs={{0,1},{1,0},{2,3},{3,2},{4,8},{5,9},{6,10},{7,11},{8,4},{9,5},{10,... | collective-permute-start | bytes 147464 | tf_op jit(solution)/shard_map/ppermute | solution.py:78
  24.2 1.8 %collective-permute-start.6 = (f32[32,256]{1,0:T(8,128)S(1)}, f32[32,256]{1,0:T(8,128)S(1)}, u32[]{:S(2)}, u32[]{:S(2)}) collective-permute-start(f32[32,256]{1,0:T(8,128)S(1)} %get-tuple-element.52), channel_id=1, source_target_pairs={{0,2},{1,3},{2,0},{3,1},{4,6},{5,7},{6,4},{7,5},{8,10},{9,11},{10,... | collective-permute-start | bytes 98312 | tf_op jit(solution)/shard_map/ppermute | solution.py:78
  26.0 3.9 %tin_first.1.u = f32[64,16,1024]{2,1,0:T(8,128)S(1)} custom-call(f32[64,16,1024]{2,1,0:T(8,128)S(1)} %copy-done, s32[64,16,1024]{2,1,0:T(8,128)S(1)} %copy-done.1, f32[32,256]{1,0:T(8,128)S(1)} %collective-permute-done.x2, f32[64,256]{1,0:T(8,128)S(1)} %collective-permute-done.2.x3, f32[64,1280]{1,0:T(8,128)S(1)} %collective-permute-done.1.e1, ...), custom_call_target="tpu_custom_call" | custom-call | bytes 20971520 | tf_op jit(solution)/shard_map/tin_first/pallas_call | solution.py:725
  29.9 0.9 %collective-permute-done.6.x2 = f32[32,256]{1,0:T(8,128)S(1)} collective-permute-done((f32[32,256]{1,0:T(8,128)S(1)}, f32[32,256]{1,0:T(8,128)S(1)}, u32[]{:S(2)}, u32[]{:S(2)}) %collective-permute-start.6) | collective-permute-done | bytes 32800 | tf_op jit(solution)/shard_map/ppermute | solution.py:78
  30.8 0.0 collective-permute-done.10.y1
  30.8 0.0 collective-permute-done.11.y2
  30.8 0.0 collective-permute-done.9.e2
  30.8 0.0 collective-permute-done.8.x3
  30.8 7.7 %last_sweep.1 = (f32[64,16,1024]{2,1,0:T(8,128)}, f32[48,64,256]{2,1,0:T(8,128)}) custom-call(f32[64,16,1024]{2,1,0:T(8,128)S(1)} %tin_first.1.u, s32[64,16,1024]{2,1,0:T(8,128)S(1)} %copy-done.1, f32[32,256]{1,0:T(8,128)S(1)} %collective-permute-done.6.x2, f32[64,256]{1,0:T(8,128)S(1)} %collective-permute-done.8.x3, ...), custom_call_target="tpu_custom_call" | custom-call | bytes 37748736 | tf_op jit(solution)/shard_map/last_sweep/pallas_call | solution.py:752
Async XLA Ops:
  4.1 4.7 %collective-permute-start.1 = (f32[64,1280]{1,0:T(8,128)S(1)}, f32[64,1280]{1,0:T(8,128)S(1)}, u32[]{:S(2)}, u32[]{:S(2)}) collective-permute-start(f32[64,1280]{1,0:T(8,128)S(1)} %get-tuple-element.37.mine1), channel_id=1, source_target_pairs={{0,1},{1,0},{2,3},{3,2},{4,5},{5,4},{6,7},{7,6},{8,9},{9,8},{10,11... | collective-permute-start | bytes 983048 | tf_op jit(solution)/shard_map/ppermute | solution.py:78
  4.2 11.4 %collective-permute-start.3 = (f32[64,1024]{1,0:T(8,128)S(1)}, f32[64,1024]{1,0:T(8,128)S(1)}, u32[]{:S(2)}, u32[]{:S(2)}) collective-permute-start(f32[64,1024]{1,0:T(8,128)S(1)} %get-tuple-element.41.mine2), channel_id=1, source_target_pairs={{0,16},{1,2},{2,1},{3,4},{4,3},{5,6},{6,5},{7,8},{8,7},{9,10},{10,... | collective-permute-start | bytes 786440 | tf_op jit(solution)/shard_map/ppermute | solution.py:78
  5.7 9.9 %collective-permute-start.4 = (f32[96,256]{1,0:T(8,128)S(1)}, f32[96,256]{1,0:T(8,128)S(1)}, u32[]{:S(2)}, u32[]{:S(2)}) collective-permute-start(f32[96,256]{1,0:T(8,128)S(1)} %get-tuple-element.49.z1), channel_id=1, source_target_pairs={{0,4},{1,5},{2,6},{3,7},{4,0},{5,1},{6,2},{7,3},{8,12},{9,13},{10,... | collective-permute-start | bytes 294920 | tf_op jit(solution)/shard_map/ppermute | solution.py:78
  6.2 9.4 %collective-permute-start.5 = (f32[96,256]{1,0:T(8,128)S(1)}, f32[96,256]{1,0:T(8,128)S(1)}, u32[]{:S(2)}, u32[]{:S(2)}) collective-permute-start(f32[96,256]{1,0:T(8,128)S(1)} %get-tuple-element.50.z2), channel_id=1, source_target_pairs={{0,1},{1,0},{2,3},{3,2},{4,8},{5,9},{6,10},{7,11},{8,4},{9,5},{10,... | collective-permute-start | bytes 294920 | tf_op jit(solution)/shard_map/ppermute | solution.py:78
  8.9 6.7 %collective-permute-start.2 = (f32[64,256]{1,0:T(8,128)S(1)}, f32[64,256]{1,0:T(8,128)S(1)}, u32[]{:S(2)}, u32[]{:S(2)}) collective-permute-start(f32[64,256]{1,0:T(8,128)S(1)} %get-tuple-element.39), channel_id=1, source_target_pairs={{0,3},{1,2},{2,1},{3,0},{4,7},{5,6},{6,5},{7,4},{8,11},{9,10},{10,... | collective-permute-start | bytes 196616 | tf_op jit(solution)/shard_map/ppermute | solution.py:78
  9.6 6.0 %collective-permute-start = (f32[32,256]{1,0:T(8,128)S(1)}, f32[32,256]{1,0:T(8,128)S(1)}, u32[]{:S(2)}, u32[]{:S(2)}) collective-permute-start(f32[32,256]{1,0:T(8,128)S(1)} %get-tuple-element.36), channel_id=1, source_target_pairs={{0,2},{1,3},{2,0},{3,1},{4,6},{5,7},{6,4},{7,5},{8,10},{9,11},{10,... | collective-permute-start | bytes 98312 | tf_op jit(solution)/shard_map/ppermute | solution.py:78
  10.1 5.5 %copy-start = (f32[64,16,1024]{2,1,0:T(8,128)S(1)}, f32[64,16,1024]{2,1,0:T(8,128)}, u32[]{:S(2)}) copy-start(f32[64,16,1024]{2,1,0:T(8,128)} %u.7) | copy-start | bytes 12582916
  10.1 5.5 %copy-start.1 = (s32[64,16,1024]{2,1,0:T(8,128)S(1)}, s32[64,16,1024]{2,1,0:T(8,128)}, u32[]{:S(2)}) copy-start(s32[64,16,1024]{2,1,0:T(8,128)} %f.7) | copy-start | bytes 12582916
  19.3 1.7 %collective-permute-start.7 = (f32[64,1280]{1,0:T(8,128)S(1)}, f32[64,1280]{1,0:T(8,128)S(1)}, u32[]{:S(2)}, u32[]{:S(2)}) collective-permute-start(f32[64,1280]{1,0:T(8,128)S(1)} %get-tuple-element.53), channel_id=1, source_target_pairs={{0,1},{1,0},{2,3},{3,2},{4,5},{5,4},{6,7},{7,6},{8,9},{9,8},{10,11... | collective-permute-start | bytes 983048 | tf_op jit(solution)/shard_map/ppermute | solution.py:78
  19.4 11.4 %collective-permute-start.9 = (f32[64,1024]{1,0:T(8,128)S(1)}, f32[64,1024]{1,0:T(8,128)S(1)}, u32[]{:S(2)}, u32[]{:S(2)}) collective-permute-start(f32[64,1024]{1,0:T(8,128)S(1)} %get-tuple-element.57), channel_id=1, source_target_pairs={{0,16},{1,2},{2,1},{3,4},{4,3},{5,6},{6,5},{7,8},{8,7},{9,10},{10,... | collective-permute-start | bytes 786440 | tf_op jit(solution)/shard_map/ppermute | solution.py:78
  21.0 9.8 %collective-permute-start.8 = (f32[64,256]{1,0:T(8,128)S(1)}, f32[64,256]{1,0:T(8,128)S(1)}, u32[]{:S(2)}, u32[]{:S(2)}) collective-permute-start(f32[64,256]{1,0:T(8,128)S(1)} %get-tuple-element.55), channel_id=1, source_target_pairs={{0,3},{1,2},{2,1},{3,0},{4,7},{5,6},{6,5},{7,4},{8,11},{9,10},{10,... | collective-permute-start | bytes 196616 | tf_op jit(solution)/shard_map/ppermute | solution.py:78
  22.2 8.6 %collective-permute-start.10 = (f32[48,256]{1,0:T(8,128)S(1)}, f32[48,256]{1,0:T(8,128)S(1)}, u32[]{:S(2)}, u32[]{:S(2)}) collective-permute-start(f32[48,256]{1,0:T(8,128)S(1)} %get-tuple-element.63.z1), channel_id=1, source_target_pairs={{0,4},{1,5},{2,6},{3,7},{4,0},{5,1},{6,2},{7,3},{8,12},{9,13},{10,... | collective-permute-start | bytes 147464 | tf_op jit(solution)/shard_map/ppermute | solution.py:78
  22.7 8.1 %collective-permute-start.11 = (f32[48,256]{1,0:T(8,128)S(1)}, f32[48,256]{1,0:T(8,128)S(1)}, u32[]{:S(2)}, u32[]{:S(2)}) collective-permute-start(f32[48,256]{1,0:T(8,128)S(1)} %get-tuple-element.64.z2), channel_id=1, source_target_pairs={{0,1},{1,0},{2,3},{3,2},{4,8},{5,9},{6,10},{7,11},{8,4},{9,5},{10,... | collective-permute-start | bytes 147464 | tf_op jit(solution)/shard_map/ppermute | solution.py:78
  24.2 6.6 %collective-permute-start.6 = (f32[32,256]{1,0:T(8,128)S(1)}, f32[32,256]{1,0:T(8,128)S(1)}, u32[]{:S(2)}, u32[]{:S(2)}) collective-permute-start(f32[32,256]{1,0:T(8,128)S(1)} %get-tuple-element.52), channel_id=1, source_target_pairs={{0,2},{1,3},{2,0},{3,1},{4,6},{5,7},{6,4},{7,5},{8,10},{9,11},{10,... | collective-permute-start | bytes 98312 | tf_op jit(solution)/shard_map/ppermute | solution.py:78

commit v4 on v3

--- a/solution.py
+++ b/solution.py
@@ -46,6 +46,11 @@
     pos = lax.axis_index("len")
     group, column = pos // TILE_Y, pos % TILE_Y
     return group, column, pos % 2 == 1, group % 2 == 1
+
+
+def alone():
+    pos = lax.axis_index("len")
+    return (pos == 0) | (pos == lax.axis_size("len") - 1)
 
 
 def iotas():
@@ -131,65 +136,66 @@
     own[1, rs, :] = right
 
 
-def put_parts(e1_aux, x2, x3, own, b_plane, p_plane, column, odd):
+def put_parts(x1, x2, x3, own, b_plane, p_plane, column, odd):
     nx = b_plane.shape[0]
     left, right = own[0], own[1]
-    put_columns(e1_aux, jnp.where(odd, left, right))
-    put_planes(e1_aux, b_plane, p_plane, column ^ 1)
+    put_columns(x1, jnp.where(odd, left, right))
+    put_planes(x1, b_plane, p_plane, column ^ 1)
     put_planes(x2, b_plane, p_plane, column ^ 2)
     inner = (column > 0) & (column < TILE_Y - 1)
     put_columns(x3, jnp.where(inner, jnp.where(odd, right, left), 0.0))
     put_planes(x3, b_plane, p_plane, column ^ 3)
 
 
-def pack_kernel(
-    u, floor, ids, speeds, cond, e1, e2, x2, x3, z1, z2, own, gv, mv, rates, halves,
-    own_m, b_plane, mrow, speeds_v, cond_v, sem
-):
+def pack_rows_kernel(u, floor, ids, e1, e2, z1, z2, mrow, sem):
     g, m = floor.at[0], ids.at[0]
     group, column, odd, godd = place()
-    nx, ny = u.shape[1], u.shape[2]
+    nx = u.shape[1]
+    nr, cx, width = g.shape
+    low, high = g.at[:, 0, :], g.at[:, cx - 1, :]
+    mrows = [
+        pltpu.make_async_copy(m.at[:, r, :], mrow.at[s], sem.at[s]) for r, s in ((0, 0), (cx - 1, 1))
+    ]
+    for copy in mrows:
+        copy.start()
+    select_copy(odd, (u.at[:, nx - 1, :], e2), (u.at[:, 0, :], e2), sem.at[4])
+    select_copy(godd, (low, z1.at[:nr]), (high, z1.at[:nr]), sem.at[2])
+    select_copy(godd, (high, z2.at[:nr]), (low, z2.at[:nr]), sem.at[3])
+    select_copy(odd, (u.at[:, 0, :], e1), (u.at[:, nx - 1, :], e1), sem.at[5])
+    for copy in mrows:
+        copy.wait()
+    m_low, m_high = mrow[0].astype(F32) + 1.0, mrow[1].astype(F32) + 1.0
+    z1[nr:, :] = jnp.where(godd, m_low, m_high)
+    z2[nr:, :] = jnp.where(godd, m_high, m_low)
+    wait_bytes(low, z1.at[:nr], sem.at[2])
+    wait_bytes(low, z2.at[:nr], sem.at[3])
+    wait_bytes(u.at[:, 0, :], e2, sem.at[4])
+
+    @pl.when(alone())
+    def _():
+        e2[...] = jnp.zeros_like(e2)
+
+    wait_bytes(u.at[:, 0, :], e1, sem.at[5])
+
+
+def pack_columns_kernel(
+    g, m, u, speeds, cond, x1, x2, x3, own, rates, halves, b_plane, own_m, speeds_v, cond_v, sem
+):
+    group, column, odd, godd = place()
     nr, cx, width = g.shape
     step = SUBL
-    chunks = nr // step
     shift = LANES // 2
-
-    def load(c):
-        at = pl.ds(c * step, step)
-        return (
-            pltpu.make_async_copy(g.at[at], gv.at[at], sem.at[2 * c]),
-            pltpu.make_async_copy(m.at[at], mv.at[at], sem.at[2 * c + 1]),
-        )
-
-    base = 2 * chunks
-    for copy in load(0):
-        copy.start()
-    plane = pltpu.make_async_copy(u.at[0], b_plane, sem.at[base])
-    plane.start()
-    low, high = g.at[:, 0, :], g.at[:, cx - 1, :]
-    mrows = [
-        pltpu.make_async_copy(m.at[:, r, :], mrow.at[s], sem.at[base + 1 + s])
-        for r, s in ((0, 0), (cx - 1, 1))
-    ]
-    for copy in mrows + [copy for c in range(1, chunks) for copy in load(c)]:
-        copy.start()
-    select_copy(godd, (low, z1.at[:nr]), (high, z1.at[:nr]), sem.at[base + 3])
-    select_copy(godd, (high, z2.at[:nr]), (low, z2.at[:nr]), sem.at[base + 4])
     small = (
-        pltpu.make_async_copy(speeds, speeds_v, sem.at[base + 7]),
-        pltpu.make_async_copy(cond, cond_v, sem.at[base + 8]),
+        pltpu.make_async_copy(u.at[0], b_plane, sem.at[0]),
+        pltpu.make_async_copy(speeds, speeds_v, sem.at[1]),
+        pltpu.make_async_copy(cond, cond_v, sem.at[2]),
     )
     for copy in small:
         copy.start()
-    rows_out = e1.at[:, :ny]
-    select_copy(odd, (u.at[:, nx - 1, :], e2), (u.at[:, 0, :], e2), sem.at[base + 5])
-    select_copy(odd, (u.at[:, 0, :], rows_out), (u.at[:, nx - 1, :], rows_out), sem.at[base + 6])
     own[...] = jnp.zeros_like(own)
     own_m[...] = jnp.zeros_like(own_m)
 
     def chunk(c, _):
-        for copy in load(c):
-            copy.wait()
         start = c * step
         for t in range(cx // SUBL):
             rs = slice(t * SUBL, (t + 1) * SUBL)
@@ -200,24 +206,18 @@
                     ref[start + offset, rs, width - LANES :],
                 )
 
-            keep_columns(own, 0, start, step, rs, edges(gv))
-            keep_columns(own_m, shift, start, step, rs, edges(mv))
+            keep_columns(own, 0, start, step, rs, edges(g))
+            keep_columns(own_m, shift, start, step, rs, edges(m))
         return 0
 
-    lax.fori_loop(0, chunks, chunk, 0)
+    lax.fori_loop(0, nr // step, chunk, 0)
     is_k = lax.broadcasted_iota(jnp.int32, (cx, LANES), 1) >= shift
     for s in range(2):
         codes = pltpu.roll(own_m[s], s, 1)
         own[s, :, :] = jnp.where(is_k, codes.astype(F32) + 1.0, pltpu.roll(own[s], s, 1))
-    plane.wait()
-    put_parts(e1.at[:, ny:], x2, x3, own, b_plane, gv.at[0], column, odd)
-    for copy in mrows:
-        copy.wait()
-    m_low, m_high = mrow[0].astype(F32) + 1.0, mrow[1].astype(F32) + 1.0
-    z1[nr:, :] = jnp.where(godd, m_low, m_high)
-    z2[nr:, :] = jnp.where(godd, m_high, m_low)
     for copy in small:
         copy.wait()
+    put_parts(x1, x2, x3, own, b_plane, g.at[0], column, odd)
     zt = u.shape[0]
     diagonal = lax.broadcasted_iota(jnp.int32, (zt, zt), 0) == lax.broadcasted_iota(
         jnp.int32, (zt, zt), 1
@@ -228,16 +228,16 @@
         rates[s, :, :] = jnp.broadcast_to(along, (zt, LANES))
     for i in range(halves.shape[0]):
         halves[i, :, :] = jnp.broadcast_to(0.5 * cond_v[0:1, i : i + 1], (SUBL, LANES))
-    wait_bytes(low, z1.at[:nr], sem.at[base + 3])
-    wait_bytes(low, z2.at[:nr], sem.at[base + 4])
-    wait_bytes(u.at[:, 0, :], e2, sem.at[base + 5])
-    wait_bytes(u.at[:, 0, :], rows_out, sem.at[base + 6])
-
-
-def inner_kernel(m, g, halves, u, f, out, ce, cw, cn, cz, urows, frows, kv, fzv, sem):
+
+
+def inner_kernel(m, g, halves, u, f, out, ce, cw, cn, cz, urows, frows, padded, kv, fzv, sem):
     nr, cx, width = m.shape
     nx = u.shape[1]
-    picks = [(u.at[:, r, :], urows.at[i]) for i, r in enumerate((1, nx - 2))]
+    picks = [
+        (u.at[:, :, j * LANES : (j + 1) * LANES], padded.at[:, j, SUBL : SUBL + nx, :])
+        for j in range(padded.shape[1])
+    ]
+    picks += [(u.at[:, r, :], urows.at[i]) for i, r in enumerate((0, 1, nx - 2, nx - 1))]
     picks += [(f.at[:, r, :], frows.at[i]) for i, r in enumerate((0, nx - 1))]
     picks = [pltpu.make_async_copy(a, b, sem.at[i]) for i, (a, b) in enumerate(picks)]
     for copy in picks:
@@ -331,21 +331,24 @@
         copy.wait()
 
 
-def floor_sides(halves, u, x1, x2, x3, z1, z2, y1, y2, own, kc, kr, tcol, trow, bv):
+def floor_sides(halves, plane, x1, x2, x3, z1, z2, y1, y2, own, kc, kr, tcol, trow, bv):
     nr = kr.shape[1]
-    nx, ny = u.shape[1], u.shape[2]
+    nx, ny = plane.shape
     width = bv.shape[1]
     group, column, odd, godd = place()
     shift = LANES // 2
-    aux = x1.at[:, ny:]
     groups = lax.axis_size("len") // TILE_Y
     known = (group ^ 1) < groups, jnp.where(godd, group + 1 < groups, group > 0)
-    one, three = get_columns(aux), get_columns(x3)
+    sides = []
+    one, three = get_columns(x1), get_columns(x3)
     for s, halo in ((0, jnp.where(odd, one, three)), (1, jnp.where(odd, three, one))):
         if halves is not None:
             both = half_coded(own[s], halves) + half_coded(halo, halves)
             kc[s, :, :] = pltpu.roll(both, shift, 1)
-        tcol[s, :, :] = kc[s] * (halo - own[s])
+        sides.append(kc[s] * (halo - own[s]))
+    west, east = sides[0], pltpu.roll(sides[1], LANES - 1, 1)
+    even = lax.broadcasted_iota(jnp.int32, west.shape, 1) % 2 == 0
+    tcol[0, :, :], tcol[1, :, :] = jnp.where(even, west, east), jnp.where(even, east, west)
     for s, (mine, halo) in enumerate(((z1, y1), (z2, y2))):
         halo = jnp.where(known[s], halo[...], 0.0)
         if halves is not None:
@@ -353,19 +356,19 @@
         side = kr[s] * (halo[:nr, :] - mine[:nr, :])
         trow[jnp.where(godd, s, 1 - s), :, :] = side
     row = lambda other: pl.ds(pl.multiple_of(other * nx, SUBL), nx)
-    bv[row(column), :] = u[0, :, pl.ds(pl.multiple_of(column * width, LANES), width)]
-    for k, ref in ((1, aux), (2, x2), (3, x3)):
+    bv[row(column), :] = plane[:, pl.ds(pl.multiple_of(column * width, LANES), width)]
+    for k, ref in ((1, x1), (2, x2), (3, x3)):
         bv[row(column ^ k), :] = ref[:nx, :]
 
 
 def floor_kernel(
-    g, ce, cw, cn, cz, u, x1, x2, x3, z1, z2, y1, y2, own, kc, kr, out, ov, fzv, tcol, trow, bv, sem
+    g, ce, cw, cn, cz, plane, x1, x2, x3, z1, z2, y1, y2, own, kc, kr, out, ov, fzv, tcol, trow, bv, sem
 ):
     nr, cx, width = g.shape
     tiles, wide = cx // SUBL, width // LANES
     step = SUBL
     chunks = nr // step
-    floor_sides(None, u, x1, x2, x3, z1, z2, y1, y2, own, kc, kr, tcol, trow, bv)
+    floor_sides(None, plane, x1, x2, x3, z1, z2, y1, y2, own, kc, kr, tcol, trow, bv)
     rows, lanes = iotas()
     r_first, r_last = rows == 0, rows == SUBL - 1
     l_first, l_last = lanes == 0, lanes == LANES - 1
@@ -398,8 +401,7 @@
                 gn, un = tile(t + 1)
             east = [pltpu.roll(v, LANES - 1, 1) for v in gs]
             west = [pltpu.roll(v, 1, 1) for v in gs]
-            t_west = pltpu.roll(tcol[0, rs, :], back, 1)
-            t_east = pltpu.roll(tcol[1, rs, :], LANES - 1 - z, 1)
+            sides = pltpu.roll(tcol[offset % 2, rs, :], back, 1)
             for j, at in enumerate(spans):
                 v = gs[j]
                 if t + 1 < tiles:
@@ -413,9 +415,9 @@
                 ym = jnp.where(l_first, west[j - 1], west[j]) if j > 0 else west[j]
                 side = ce[z, rs, at] * (yp - v) + cw[z, rs, at] * (ym - v)
                 if j == 0:
-                    side = side + jnp.where(l_first, t_west, 0.0)
+                    side = side + jnp.where(l_first, sides, 0.0)
                 if j + 1 == wide:
-                    side = side + jnp.where(l_last, t_east, 0.0)
+                    side = side + jnp.where(l_last, sides, 0.0)
                 nxt = g[above, rs, at]
                 if offset == step - 1:
                     nxt = scale * nxt
@@ -482,14 +484,13 @@
             back = lax.rem(LANES - z, LANES)
             for t in range(tiles):
                 rs = slice(t * SUBL, (t + 1) * SUBL)
+                sides = pltpu.roll(tcol[offset % 2, rs, :], back, 1)
                 for j, at in enumerate(spans):
                     v = part[z, rs, at]
                     if j == 0:
-                        west = pltpu.roll(tcol[0, rs, :], back, 1)
-                        v = v + jnp.where(l_first, west, 0.0)
+                        v = v + jnp.where(l_first, sides, 0.0)
                     if j + 1 == wide:
-                        east = pltpu.roll(tcol[1, rs, :], LANES - 1 - z, 1)
-                        v = v + jnp.where(l_last, east, 0.0)
+                        v = v + jnp.where(l_last, sides, 0.0)
                     for s, edge, mask in ((0, 0, r_first), (1, tiles - 1, r_last)):
                         if t == edge:
                             side = trow[s, pl.ds(start, SUBL), at][offset : offset + 1]
@@ -522,20 +523,25 @@
     return copies
 
 
-def fill_halo(halo, e1, e2):
-    odd, pos, ny = place()[2], lax.axis_index("len"), halo.shape[2]
-    alone = (pos == 0) | (pos == lax.axis_size("len") - 1)
-    one, two = e1[:, :ny], jnp.where(alone, 0.0, e2[...])
-    halo[0, :, :] = jnp.where(odd, one, two)
-    halo[1, :, :] = jnp.where(odd, two, one)
-
-
-def tin_layer(u, f, halo, rates, start, offset, out):
-    zt, nx, ny = u.shape
-    rows, lanes = iotas()
-    r_first, r_last = rows == 0, rows == SUBL - 1
+def fill_rows(padded, e1, e2, start):
+    odd = place()[2]
+    here = pl.ds(start, SUBL)
+    for j in range(padded.shape[1]):
+        at = slice(j * LANES, (j + 1) * LANES)
+        one, two = e1[here, at], e2[here, at]
+        for row, v in (
+            (SUBL - 1, jnp.where(odd, one, two)),
+            (padded.shape[2] - SUBL, jnp.where(odd, two, one)),
+        ):
+            for i in range(SUBL):
+                padded[start + i, j, row : row + 1, :] = v[i : i + 1, :]
+
+
+def tin_layer(padded, f, rates, start, offset, store):
+    zt, wide, _, _ = padded.shape
+    lanes = lax.broadcasted_iota(jnp.int32, (SUBL, LANES), 1)
     l_first, l_last = lanes == 0, lanes == LANES - 1
-    tiles, wide = nx // SUBL, ny // LANES
+    tiles = f.shape[1] // SUBL
     zero = jnp.zeros((SUBL, LANES), F32)
     z = start + offset
     sx, sy = (
@@ -547,65 +553,59 @@
         centre = centre - jnp.where(z == 0, HT, 0.0)
     above, below = jnp.minimum(z + 1, zt - 1), jnp.maximum(z - 1, 0)
 
-    def get(ref, z_, t, j):
-        return ref[z_, t * SUBL : (t + 1) * SUBL, j * LANES : (j + 1) * LANES]
+    def get(layer, t, j, by=0):
+        return padded[layer, j, (t + 1) * SUBL + by : (t + 2) * SUBL + by, :]
 
     left = [zero] * tiles
-    now = [get(u, z, t, 0) for t in range(tiles)]
+    now = [get(z, t, 0) for t in range(tiles)]
     turned = [pltpu.roll(v, LANES - 1, 1) for v in now]
     for j in range(wide):
         at = slice(j * LANES, (j + 1) * LANES)
         if j + 1 < wide:
-            nxt = [get(u, z, t, j + 1) for t in range(tiles)]
+            nxt = [get(z, t, j + 1) for t in range(tiles)]
             nxt_turned = [pltpu.roll(v, LANES - 1, 1) for v in nxt]
         else:
             nxt, nxt_turned = None, [zero] * tiles
-        low, high = (
-            jnp.broadcast_to(halo[s, pl.ds(start, SUBL), at][offset : offset + 1], (SUBL, LANES))
-            for s in range(2)
-        )
-        downs = [low] + [pltpu.roll(v, 1, 0) for v in now]
-        ups = [pltpu.roll(v, SUBL - 1, 0) for v in now] + [high]
         for t in range(tiles):
-            v = now[t]
-            xm = jnp.where(r_first, downs[t], downs[t + 1])
-            xp = jnp.where(r_last, ups[t + 1], ups[t])
+            v, xm, xp = now[t], get(z, t, j, -1), get(z, t, j, 1)
             turn = pltpu.roll(v, 1, 1)
             ym = jnp.where(l_first, left[t], turn)
             yp = jnp.where(l_last, nxt_turned[t], turned[t])
             left[t] = turn
-            code = get(f, z, t, j)
+            code = f[z, t * SUBL : (t + 1) * SUBL, at]
             xs = jnp.where((code & 1) == 0, xm, xp)
             ys = jnp.where(code < 2, ym, yp)
-            spread = (xm + xp) + (ym + yp) + (get(u, above, t, j) + get(u, below, t, j))
-            out[t * SUBL : (t + 1) * SUBL, at] = (centre * v + KT * spread) + (sx * xs + sy * ys)
+            spread = (xm + xp) + (ym + yp) + (get(above, t, j) + get(below, t, j))
+            store(t, j, (centre * v + KT * spread) + (sx * xs + sy * ys))
         now, turned = nxt, nxt_turned
 
 
-def gather_floor_top(pv, e1, x2, x3, g):
+def flat_store(ref):
+    def store(t, j, value):
+        ref[t * SUBL : (t + 1) * SUBL, j * LANES : (j + 1) * LANES] = value
+
+    return store
+
+
+def gather_floor_top(pv, x1, x2, x3, g):
     nx, ny = pv.shape
     width = x2.shape[1]
     column = place()[1]
     lanes_at = lambda other: pl.ds(pl.multiple_of(other * width, LANES), width)
     pv[:, lanes_at(column)] = g[0, pl.ds(pl.multiple_of(column * nx, SUBL), nx), :]
-    for k, ref in ((1, e1.at[:, ny:]), (2, x2), (3, x3)):
+    for k, ref in ((1, x1), (2, x2), (3, x3)):
         pv[:, lanes_at(column ^ k)] = ref[nx : 2 * nx, :]
 
 
-def edge_kernel(
-    u, f, mine1, mine2, urows, frows, x2, x3, e1, e2, g, part, z1, z2, y1, y2, own, halves, rates,
-    ox2, ox3, o1, o2, g_new, own_new, oz1, oz2, kc, kr,
-    pv, plane, halo, tcol, trow, bv, sem
+def tin_edge_kernel(
+    padded_in, f, urows, frows, x1, x2, x3, e1, e2, g, rates, padded, o1, o2, plane, pv
 ):
-    floor_sides(halves, u, e1, x2, x3, z1, z2, y1, y2, own, kc, kr, tcol, trow, bv)
-    copies = floor_finish(part, g, tcol, trow, bv, g_new, own_new, oz1, oz2, sem)
-    zt, nx, ny = u.shape
-    group, column, odd, _ = place()
-    gather_floor_top(pv, e1, x2, x3, g)
-    fill_halo(halo, e1, e2)
-    tin_layer(u, f, halo, rates, 0, 0, plane)
+    zt, nx, ny = f.shape
+    odd, lonely = place()[2], alone()
+    gather_floor_top(pv, x1, x2, x3, g)
+    fill_rows(padded, e1, e2, 0)
+    tin_layer(padded, f, rates, 0, 0, flat_store(plane))
     plane[...] = plane[...] + HT * pv[...]
-    put_parts(o1.at[:, ny:], ox2, ox3, own_new, plane, g_new.at[0], column, odd)
     rows, lanes = iotas()
     r_first, r_last = rows == 0, rows == SUBL - 1
     l_first, l_last = lanes == 0, lanes == LANES - 1
@@ -622,21 +622,20 @@
         contact = jnp.where(r_first & bottom, HT, 0.0)
         centre = 1.0 - 6.0 * KT - sx - sy - contact
         outs = []
-        def own_row(s, rows_, at):
-            one, two = mine1[rows_, at], mine2[rows_, at]
-            return jnp.where(odd, two, one) if s else jnp.where(odd, one, two)
-
         for s, side in ((0, 0), (1, nx - 1)):
-            vs = [own_row(s, here, slice(j * LANES, (j + 1) * LANES)) for j in range(wide)]
+            edge, inner = (3, 2) if s else (0, 1)
+            vs = [urows[edge, here, j * LANES : (j + 1) * LANES] for j in range(wide)]
             east = [pltpu.roll(v, LANES - 1, 1) for v in vs] + [zero]
             west = [zero] + [pltpu.roll(v, 1, 1) for v in vs]
             for j in range(wide):
                 at = slice(j * LANES, (j + 1) * LANES)
-                v, code, inside, outside = vs[j], frows[s, here, at], urows[s, here, at], halo[s, here, at]
+                v, code, inside = vs[j], frows[s, here, at], urows[inner, here, at]
+                one, two = e1[here, at], e2[here, at]
+                outside = jnp.where(odd, two, one) if s else jnp.where(odd, one, two)
                 xm, xp = (inside, outside) if s else (outside, inside)
                 ym = jnp.where(l_first, west[j], west[j + 1])
                 yp = jnp.where(l_last, east[j + 1], east[j])
-                above, below = own_row(s, after, at), own_row(s, before, at)
+                above, below = urows[edge, after, at], urows[edge, before, at]
                 above = jnp.where(top, pltpu.roll(v, 1, 0), above)
                 below = jnp.where(bottom, pltpu.roll(v, SUBL - 1, 0), below)
                 above = jnp.where(r_last, pltpu.roll(above, SUBL - 1, 0), pltpu.roll(v, SUBL - 1, 0))
@@ -651,42 +650,98 @@
             at = slice(j * LANES, (j + 1) * LANES)
             low, high = outs[j], outs[wide + j]
             o1[here, at] = jnp.where(odd, low, high)
-            o2[here, at] = jnp.where(odd, high, low)
+            o2[here, at] = jnp.where(lonely, 0.0, jnp.where(odd, high, low))
         return 0
 
     lax.fori_loop(0, blocks, block, 0)
+
+
+def tin_edges(*arrays):
+    padded, f, _, _, _, _, _, e1, e2, _, _ = arrays
+    plane = f.shape[1:]
+    return pl.pallas_call(
+        tin_edge_kernel,
+        out_shape=[shape(padded.shape), shape(e1.shape), shape(e2.shape), shape(plane)],
+        in_specs=[VMEM] * 11,
+        out_specs=[VMEM] * 4,
+        input_output_aliases={0: 0},
+        scratch_shapes=[pltpu.VMEM(plane, F32)],
+        compiler_params=params(2),
+        cost_estimate=cost(0, 4 << 20),
+        name="tin_edges",
+    )(*in_vmem(*arrays))
+
+
+def floor_edge_kernel(
+    b_plane, plane, x1, x2, x3, g, part, z1, z2, y1, y2, own, halves,
+    ox1, ox2, ox3, g_new, own_new, oz1, oz2, kc, kr, tcol, trow, bv, sem
+):
+    group, column, odd, _ = place()
+    floor_sides(halves, b_plane, x1, x2, x3, z1, z2, y1, y2, own, kc, kr, tcol, trow, bv)
+    copies = floor_finish(part, g, tcol, trow, bv, g_new, own_new, oz1, oz2, sem)
+    put_parts(ox1, ox2, ox3, own_new, plane, g_new.at[0], column, odd)
     for copy in copies:
         copy.wait()
 
 
-def edge_sweep(
-    u, f, mine1, mine2, urows, frows, x2, x3, e1, e2, g, part, z1, z2, y1, y2, own, halves, rates
-):
-    plane = pltpu.VMEM(u.shape[1:], F32)
+def floor_edges(*arrays):
+    _, _, x1, x2, x3, g, _, _, _, _, _, own, _ = arrays
     nr, cx, width = g.shape
     return pl.pallas_call(
-        edge_kernel,
-        out_shape=[shape(v.shape) for v in (x2, x3, e1, e2, g, own)]
+        floor_edge_kernel,
+        out_shape=[shape(v.shape) for v in (x1, x2, x3, g, own)]
         + [shape((nr, width))] * 2
         + [shape(own.shape), shape((2, nr, width))],
-        in_specs=[VMEM] * 19,
-        out_specs=[VMEM] * 10,
-        scratch_shapes=[plane, plane, pltpu.VMEM((2, *e2.shape), F32), *floor_scratch(g.shape)[1:]],
+        in_specs=[VMEM] * 13,
+        out_specs=[VMEM] * 9,
+        scratch_shapes=floor_scratch(g.shape)[1:],
         compiler_params=params(2),
         cost_estimate=cost(0, 10 << 20),
-        name="edge",
-    )(
-        *in_vmem(
-            u, f, mine1, mine2, urows, frows, x2, x3, e1, e2, g, part, z1, z2, y1, y2, own, halves, rates
-        )
-    )
-
-
-def tin_kernel(final, u, f, x2, x3, e1, e2, g, rates, out, ov, pv, halo, sem):
-    zt, nx, ny = u.shape
-    step = SUBL
-    gather_floor_top(pv, e1, x2, x3, g)
-    fill_halo(halo, e1, e2)
+        name="floor_edges",
+    )(*in_vmem(*arrays))
+
+
+def tin_first(padded, f, x1, x2, x3, e1, e2, g, rates):
+    zt, wide, _, _ = padded.shape
+    nx, step = f.shape[1], SUBL
+    tiles = nx // SUBL
+
+    def kernel(padded_in, f, x1, x2, x3, e1, e2, g, rates, padded, out, pv):
+        gather_floor_top(pv, x1, x2, x3, g)
+
+        def chunk(c, _):
+            start = pl.multiple_of(c * step, SUBL)
+            fill_rows(padded, e1, e2, start)
+            for offset in range(step):
+
+                def store(t, j, value):
+                    out[start + offset, j, (t + 1) * SUBL : (t + 2) * SUBL, :] = value
+
+                tin_layer(padded, f, rates, start, offset, store)
+            return 0
+
+        lax.fori_loop(0, zt // step, chunk, 0)
+        for t in range(tiles):
+            rs = slice((t + 1) * SUBL, (t + 2) * SUBL)
+            for j in range(wide):
+                top = pv[t * SUBL : (t + 1) * SUBL, j * LANES : (j + 1) * LANES]
+                out[0, j, rs, :] = out[0, j, rs, :] + HT * top
+
+    return pl.pallas_call(
+        kernel,
+        out_shape=[shape(padded.shape)] * 2,
+        in_specs=[VMEM] * 9,
+        out_specs=[VMEM] * 2,
+        input_output_aliases={0: 0},
+        scratch_shapes=[pltpu.VMEM((nx, wide * LANES), F32)],
+        compiler_params=params(2),
+        cost_estimate=cost(0, 20 << 20),
+        name="tin_first",
+    )(*in_vmem(padded, f, x1, x2, x3, e1, e2, g, rates))[1]
+
+
+def tin_last(padded, f, e1, e2, pv, rates, out, ov, sem):
+    zt, step = padded.shape[0], SUBL
 
     def store(c):
         at = pl.ds(c * step, step)
@@ -694,138 +749,133 @@
 
     def chunk(c, _):
         start = pl.multiple_of(c * step, SUBL)
+        fill_rows(padded, e1, e2, start)
         for offset in range(step):
-            tin_layer(u, f, halo, rates, start, offset, ov.at[start + offset])
+            tin_layer(padded, f, rates, start, offset, flat_store(ov.at[start + offset]))
 
         @pl.when(c == 0)
         def _():
             ov[0, :, :] = ov[0] + HT * pv[...]
 
-        if final:
-            store(c).start()
+        store(c).start()
         return 0
 
     lax.fori_loop(0, zt // step, chunk, 0)
-    return [store(c) for c in range(zt // step)] if final else []
-
-
-def tin_scratch(dims):
-    zt, nx, ny = dims
-    return [
-        pltpu.VMEM((nx, ny), F32),
-        pltpu.VMEM((2, zt, ny), F32),
-        pltpu.SemaphoreType.DMA((zt // SUBL,)),
-    ]
-
-
-def tin_first(u, f, x2, x3, e1, e2, g, rates):
-    def kernel(u, f, x2, x3, e1, e2, g, rates, out, *scratch):
-        tin_kernel(False, u, f, x2, x3, e1, e2, g, rates, out, out, *scratch)
+    return [store(c) for c in range(zt // step)]
+
+
+def last_sweep(padded, f, plane, x1, x2, x3, e1, e2, g, rates, coefs, z1, z2, y1, y2, own, kc, kr):
+    zt, wide, _, _ = padded.shape
+
+    def kernel(
+        padded_in, f, plane, x1, x2, x3, e1, e2, g, ce, cw, cn, cz, z1, z2, y1, y2, own, kc, kr, rates,
+        padded, u_out, g_out, uv, gv, pv, sem, *scratch
+    ):
+        stores = floor_kernel(
+            g, ce, cw, cn, cz, plane, x1, x2, x3, z1, z2, y1, y2, own, kc, kr, g_out, gv, *scratch
+        )
+        gather_floor_top(pv, x1, x2, x3, g)
+        stores += tin_last(padded, f, e1, e2, pv, rates, u_out, uv, sem)
+        for copy in stores:
+            copy.wait()
 
     return pl.pallas_call(
         kernel,
-        out_shape=shape(u.shape),
-        in_specs=[VMEM] * 8,
-        out_specs=VMEM,
-        scratch_shapes=tin_scratch(u.shape),
-        compiler_params=params(2),
-        cost_estimate=cost(0, 20 << 20),
-        name="tin_first",
-    )(*in_vmem(u, f, x2, x3, e1, e2, g, rates))
-
-
-def last_sweep(u, f, x2, x3, x1, e2, g, rates, coefs, z1, z2, y1, y2, own, kc, kr):
-    def kernel(
-        u, f, x2, x3, x1, e2, g, ce, cw, cn, cz, z1, z2, y1, y2, own, kc, kr, rates,
-        u_out, g_out, uv, gv, *scratch
-    ):
-        stores = tin_kernel(
-            True, u, f, x2, x3, x1, e2, g, rates, u_out, uv, *scratch[:3]
-        )
-        stores += floor_kernel(
-            g, ce, cw, cn, cz, u, x1, x2, x3, z1, z2, y1, y2, own, kc, kr, g_out, gv,
-            *scratch[3:]
-        )
-        for copy in stores:
-            copy.wait()
-
-    return pl.pallas_call(
-        kernel,
-        out_shape=[far(u.shape), far(g.shape)],
-        in_specs=[VMEM] * 19,
-        out_specs=[ANY] * 2,
-        scratch_shapes=[pltpu.VMEM(u.shape, F32), pltpu.VMEM(g.shape, F32)]
-        + tin_scratch(u.shape)
+        out_shape=[shape(padded.shape), far(f.shape), far(g.shape)],
+        in_specs=[VMEM] * 21,
+        out_specs=[VMEM, ANY, ANY],
+        input_output_aliases={0: 0},
+        scratch_shapes=[
+            pltpu.VMEM(f.shape, F32),
+            pltpu.VMEM(g.shape, F32),
+            pltpu.VMEM(plane.shape, F32),
+            pltpu.SemaphoreType.DMA((zt // SUBL,)),
+        ]
         + floor_scratch(g.shape),
         compiler_params=params(10),
         cost_estimate=cost(0, 36 << 20),
         name="last_sweep",
-    )(*in_vmem(u, f, x2, x3, x1, e2, g, *coefs, z1, z2, y1, y2, own, kc, kr, rates))
+    )(*in_vmem(padded, f, plane, x1, x2, x3, e1, e2, g, *coefs, z1, z2, y1, y2, own, kc, kr, rates))[1:]
 
 
 def local(tin_temp, flow_code, speeds, floor_temp, material, conductivity):
     u, f, g, m = tin_temp, flow_code, floor_temp[0], material[0]
     zt, nx, ny = u.shape
     nr, cx, width = g.shape
-    e1, e2, x2, x3, z1, z2, own, gv, mv, rates, halves = pl.pallas_call(
-        pack_kernel,
+    e1, e2, z1, z2 = pl.pallas_call(
+        pack_rows_kernel,
+        out_shape=[shape((zt, ny))] * 2 + [shape((2 * nr, width))] * 2,
+        in_specs=[ANY] * 3,
+        out_specs=[VMEM] * 4,
+        scratch_shapes=[pltpu.VMEM((2, nr, width), jnp.int32), pltpu.SemaphoreType.DMA((6,))],
+        compiler_params=params(2),
+        cost_estimate=cost(0, 6 << 20),
+        name="pack_rows",
+    )(*in_hbm(u, floor_temp, material))
+    e2, e1 = swap(e2, "e2"), swap(e1, "e1")
+    y1, y2 = swap(z1, "z1"), swap(z2, "z2")
+    x1, x2, x3, own, rates, halves, b_plane = pl.pallas_call(
+        pack_columns_kernel,
         out_shape=[
-            shape((zt, ny + 2 * LANES)),
-            shape((zt, ny)),
+            shape((cx, 2 * LANES)),
             shape((2 * nx, width)),
             shape((cx, 2 * LANES)),
-            shape((2 * nr, width)),
-            shape((2 * nr, width)),
             shape((2, cx, LANES)),
-            shape(g.shape),
-            shape(g.shape, jnp.int32),
             shape((2, zt, LANES)),
             shape((conductivity.shape[0], SUBL, LANES)),
+            shape((nx, ny)),
         ],
-        in_specs=[ANY] * 5,
-        out_specs=[VMEM] * 11,
+        in_specs=[VMEM] * 2 + [ANY] * 3,
+        out_specs=[VMEM] * 7,
         scratch_shapes=[
             pltpu.VMEM((2, cx, LANES), jnp.int32),
-            pltpu.VMEM((nx, ny), F32),
-            pltpu.VMEM((2, nr, width), jnp.int32),
             pltpu.VMEM(speeds.shape, F32),
             pltpu.VMEM((1, conductivity.shape[0]), F32),
-            pltpu.SemaphoreType.DMA((2 * nr // SUBL + 9,)),
+            pltpu.SemaphoreType.DMA((3,)),
         ],
         compiler_params=params(2),
         cost_estimate=cost(0, 12 << 20),
-        name="pack",
-    )(*in_hbm(u, floor_temp, material, speeds, conductivity[None]))
-    mine1, mine2 = e1, e2
-    e1, e2 = swap(e1, "e1"), swap(e2, "e2")
+        name="pack_columns",
+    )(*in_vmem(g, m), *in_hbm(u, speeds, conductivity[None]))
+    x1 = swap(x1, "e1")
     e1, x3 = lax.optimization_barrier((e1, x3))
+    x1, x2 = lax.optimization_barrier((x1, x2))
     x2, x3 = swap(x2, "x2"), swap(x3, "x3")
-    y1, y2 = swap(z1, "z1"), swap(z2, "z2")
-    part, *coefs, urows, frows = pl.pallas_call(
+    part, *coefs, urows, frows, padded = pl.pallas_call(
         inner_kernel,
         out_shape=[shape(g.shape)] * 5
-        + [shape((2, zt, ny)), shape((2, zt, ny), jnp.int32)],
+        + [
+            shape((4, zt, ny)),
+            shape((2, zt, ny), jnp.int32),
+            shape((zt, ny // LANES, nx + 2 * SUBL, LANES)),
+        ],
         in_specs=[VMEM] * 3 + [ANY] * 2,
-        out_specs=[VMEM] * 7,
+        out_specs=[VMEM] * 8,
         scratch_shapes=[
             pltpu.VMEM((2, cx, width), F32),
             pltpu.VMEM((cx, width), F32),
-            pltpu.SemaphoreType.DMA((4,)),
+            pltpu.SemaphoreType.DMA((6 + ny // LANES,)),
         ],
         compiler_params=params(2),
         cost_estimate=cost(0, 24 << 20),
         name="inner",
-    )(*in_vmem(mv, gv, halves), *in_hbm(u, f))
-    w2, w3, w1, d2, g1, own1, z1, z2, kc, kr = edge_sweep(
-        u, f, mine1, mine2, urows, frows, x2, x3, e1, e2, gv, part, z1, z2, y1, y2, own, halves, rates
+    )(*in_vmem(m, g, halves), *in_hbm(u, f))
+    rates, y1, y2 = lax.optimization_barrier((rates, y1, y2))
+    padded, d1, d2, plane = tin_edges(
+        padded, f, urows, frows, x1, x2, x3, e1, e2, g, rates
     )
-    w1, d2 = swap(w1, "e1"), swap(d2, "e2")
-    w1, w3 = lax.optimization_barrier((w1, w3))
+    d1, d2 = swap(d1, "e1"), swap(d2, "e2")
+    w1, w2, w3, g1, own1, z1, z2, kc, kr = floor_edges(
+        b_plane, plane, x1, x2, x3, g, part, z1, z2, y1, y2, own, halves
+    )
+    w1 = swap(w1, "e1")
+    d1, w3 = lax.optimization_barrier((d1, w3))
+    w1, w2 = lax.optimization_barrier((w1, w2))
     w2, w3 = swap(w2, "x2"), swap(w3, "x3")
     y1, y2 = swap(z1, "z1"), swap(z2, "z2")
-    u1 = tin_first(u, f, x2, x3, e1, e2, gv, rates)
+    u1 = tin_first(padded, f, x1, x2, x3, e1, e2, g, rates)
     u2, g2 = last_sweep(
-        u1, f, w2, w3, w1, d2, g1, rates, coefs, z1, z2, y1, y2, own1, kc, kr
+        u1, f, plane, w1, w2, w3, d1, d2, g1, rates, coefs, z1, z2, y1, y2, own1, kc, kr
     )
     return u2, g2[None]
 

time: 38.6 us -> 35.7 us (0.925)
  the two profiles are of different devices: /device:TPU:8 before, /device:TPU:0 now
where the time goes in v4:
time: 35.7 us; the launch traced here: 35.6 us
  Pallas kernels  21.2 us (59%)
  starting transfers between devices  13.5 us (38%)
  between operations  0.8 us (2%)
    ppermute x14, starting transfers between devices, swap(): return lax.ppermute(value, ('grp', 'len'), pairs)  13.5 us
    pallas_call x1, Pallas kernels, last_sweep(): pl.pallas_call(kernel, out_shape=[shape(padded.shape), far(f.shape), far(...  7.35 us
    pallas_call x1, Pallas kernels, local(): pl.pallas_call(inner_kernel, out_shape=[shape(g.shape)] * 5 + [shape((4,...  4.35 us
    pallas_call x1, Pallas kernels, tin_first(): pl.pallas_call(kernel, out_shape=[shape(padded.shape)] * 2, in_specs=[VME...  3.21 us
    pallas_call x1, Pallas kernels, floor_edges(): pl.pallas_call(floor_edge_kernel, out_shape=[shape(v.shape) for v in (x1,...  2.33 us
    pallas_call x1, Pallas kernels, local(): pl.pallas_call(pack_columns_kernel, out_shape=[shape((cx, 2 * LANES)), sh...  1.49 us
    pallas_call x1, Pallas kernels, local(): pl.pallas_call(pack_rows_kernel, out_shape=[shape((zt, ny))] * 2 + [shape...  1.42 us
    pallas_call x1, Pallas kernels, tin_edges(): pl.pallas_call(tin_edge_kernel, out_shape=[shape(padded.shape), shape(e1....  1.05 us
  transfers between devices with their start and end apart: 14, of which 0 were waited for; matrix products, arithmetic and copies ran while one was open for 0% of the time, Pallas kernels for 32%

profile of v4, /device:TPU:0, one launch (start us, length us, event | category | flops | bytes accessed | tf_op | source)
XLA Modules:
  0.0 35.6 jit_solution(9060609804789962560)
XLA Ops:
  0.6 0.0 copy-start.2
  0.6 0.0 copy-start
  0.6 1.4 %pack_rows.1 = (f32[64,1024]{1,0:T(8,128)S(1)}, f32[64,1024]{1,0:T(8,128)S(1)}, f32[96,256]{1,0:T(8,128)S(1)}, f32[96,256]{1,0:T(8,128)S(1)}) custom-call(f32[64,16,1024]{2,1,0:T(8,128)} %u.5, f32[1,48,64,256]{3,2,1,0:T(8,128)} %floor.1, s32[1,48,64,256]{3,2,1,0:T(8,128)} %ids.1), custom_call_target="tpu_custom_call" | custom-call | bytes 6291456 | tf_op jit(solution)/shard_map/pack_rows/pallas_call | solution.py:805
  2.1 0.5 %collective-permute-start.2 = (f32[64,1024]{1,0:T(8,128)S(1)}, f32[64,1024]{1,0:T(8,128)S(1)}, u32[]{:S(2)}, u32[]{:S(2)}) collective-permute-start(f32[64,1024]{1,0:T(8,128)S(1)} %get-tuple-element.56), channel_id=1, source_target_pairs={{0,1},{1,0},{2,3},{3,2},{4,5},{5,4},{6,7},{7,6},{8,9},{9,8},{10,11... | collective-permute-start | bytes 786440 | tf_op jit(solution)/shard_map/ppermute | solution.py:83
  2.6 2.6 %collective-permute-start.4 = (f32[64,1024]{1,0:T(8,128)S(1)}, f32[64,1024]{1,0:T(8,128)S(1)}, u32[]{:S(2)}, u32[]{:S(2)}) collective-permute-start(f32[64,1024]{1,0:T(8,128)S(1)} %get-tuple-element.60), channel_id=1, source_target_pairs={{0,16},{1,2},{2,1},{3,4},{4,3},{5,6},{6,5},{7,8},{8,7},{9,10},{10,... | collective-permute-start | bytes 786440 | tf_op jit(solution)/shard_map/ppermute | solution.py:83
  5.2 0.0 copy-done.2
  5.2 0.0 copy-done
  5.2 1.5 %pack_columns.1 = (f32[64,256]{1,0:T(8,128)S(1)}, f32[32,256]{1,0:T(8,128)S(1)}, f32[64,256]{1,0:T(8,128)S(1)}, f32[2,64,128]{2,1,0:T(8,128)S(1)}, f32[2,64,128]...) custom-call(f32[48,64,256]{2,1,0:T(8,128)S(1)} %bitcast.4, s32[48,64,256]{2,1,0:T(8,128)S(1)} %bitcast.9, ...), custom_call_target="tpu_custom_call" | custom-call | bytes 12582912 | tf_op jit(solution)/shard_map/pack_columns/pallas_call | solution.py:817
  6.7 0.2 collective-permute-start
  6.9 1.6 %collective-permute-start.5 = (f32[96,256]{1,0:T(8,128)S(1)}, f32[96,256]{1,0:T(8,128)S(1)}, u32[]{:S(2)}, u32[]{:S(2)}) collective-permute-start(f32[96,256]{1,0:T(8,128)S(1)} %get-tuple-element.62.z1), channel_id=1, source_target_pairs={{0,4},{1,5},{2,6},{3,7},{4,0},{5,1},{6,2},{7,3},{8,12},{9,13},{10,... | collective-permute-start | bytes 294920 | tf_op jit(solution)/shard_map/ppermute | solution.py:83
  8.5 0.2 collective-permute-start.6
  8.6 0.0 collective-permute-done.2.e1
  8.6 1.5 %collective-permute-start.3 = (f32[64,256]{1,0:T(8,128)S(1)}, f32[64,256]{1,0:T(8,128)S(1)}, u32[]{:S(2)}, u32[]{:S(2)}) collective-permute-start(f32[64,256]{1,0:T(8,128)S(1)} %get-tuple-element.58), channel_id=1, source_target_pairs={{0,3},{1,2},{2,1},{3,0},{4,7},{5,6},{6,5},{7,4},{8,11},{9,10},{10,... | collective-permute-start | bytes 196616 | tf_op jit(solution)/shard_map/ppermute | solution.py:83
  10.1 0.0 collective-permute-done.x1
  10.1 0.5 %collective-permute-start.1 = (f32[32,256]{1,0:T(8,128)S(1)}, f32[32,256]{1,0:T(8,128)S(1)}, u32[]{:S(2)}, u32[]{:S(2)}) collective-permute-start(f32[32,256]{1,0:T(8,128)S(1)} %get-tuple-element.55), channel_id=1, source_target_pairs={{0,2},{1,3},{2,0},{3,1},{4,6},{5,7},{6,4},{7,5},{8,10},{9,11},{10,... | collective-permute-start | bytes 98312 | tf_op jit(solution)/shard_map/ppermute | solution.py:83
  10.6 0.0 copy-start.1
  10.6 4.4 %inner.1 = (f32[48,64,256]{2,1,0:T(8,128)S(1)}, f32[48,64,256]{2,1,0:T(8,128)S(1)}, f32[48,64,256]{2,1,0:T(8,128)S(1)}, f32[48,64,256]{2,1,0:T(8,128)S(1)}, f32[...) custom-call(s32[48,64,256]{2,1,0:T(8,128)S(1)} %bitcast.10, ...), custom_call_target="tpu_custom_call" | custom-call | bytes 25165824 | tf_op jit(solution)/shard_map/inner/pallas_call | solution.py:844
  15.0 0.0 collective-permute-done.5.y1
  15.0 0.0 collective-permute-done.6.y2
  15.0 0.0 collective-permute-done.1.x2
  15.0 0.0 collective-permute-done.4.e2
  15.0 0.0 collective-permute-done.3.x3
  15.0 0.0 copy-done.1
  15.0 1.0 %tin_edges.1 = (f32[64,8,32,128]{3,2,1,0:T(8,128)S(1)}, f32[64,1024]{1,0:T(8,128)S(1)}, f32[64,1024]{1,0:T(8,128)S(1)}, f32[16,1024]{1,0:T(8,128)S(1)}) custom-call(f32[64,8,32,128]{3,2,1,0:T(8,128)S(1)} %get-tuple-element.49.padded_in, s32[64,16,1024]{2,1,0:T(8,128)S(1)} %copy-done.1, ...), custom_call_target="tpu_custom_call", output_to_operand_aliasing={{0}: (0, {})} | custom-call | bytes 4194304 | tf_op jit(solution)/shard_map/tin_edges/pallas_call | solution.py:662
  16.1 0.1 collective-permute-start.9
  16.2 1.6 %collective-permute-start.11 = (f32[64,1024]{1,0:T(8,128)S(1)}, f32[64,1024]{1,0:T(8,128)S(1)}, u32[]{:S(2)}, u32[]{:S(2)}) collective-permute-start(f32[64,1024]{1,0:T(8,128)S(1)} %get-tuple-element.81), channel_id=1, source_target_pairs={{0,16},{1,2},{2,1},{3,4},{4,3},{5,6},{6,5},{7,8},{8,7},{9,10},{10,... | collective-permute-start | bytes 786440 | tf_op jit(solution)/shard_map/ppermute | solution.py:83
  17.7 2.3 %floor_edges.1 = (f32[64,256]{1,0:T(8,128)S(1)}, f32[32,256]{1,0:T(8,128)S(1)}, f32[64,256]{1,0:T(8,128)S(1)}, f32[48,64,256]{2,1,0:T(8,128)S(1)}, f32[2,64,128]...) custom-call(f32[16,1024]{1,0:T(8,128)S(1)} %get-tuple-element.68.b_p, ...), custom_call_target="tpu_custom_call" | custom-call | bytes 10485760 | tf_op jit(solution)/shard_map/floor_edges/pallas_call | solution.py:690
  20.1 0.2 collective-permute-start.7
  20.3 0.0 collective-permute-done.9.e1
  20.3 2.4 %collective-permute-start.10 = (f32[64,256]{1,0:T(8,128)S(1)}, f32[64,256]{1,0:T(8,128)S(1)}, u32[]{:S(2)}, u32[]{:S(2)}) collective-permute-start(f32[64,256]{1,0:T(8,128)S(1)} %get-tuple-element.79), channel_id=1, source_target_pairs={{0,3},{1,2},{2,1},{3,0},{4,7},{5,6},{6,5},{7,4},{8,11},{9,10},{10,... | collective-permute-start | bytes 196616 | tf_op jit(solution)/shard_map/ppermute | solution.py:83
  22.7 0.7 %collective-permute-start.12 = (f32[48,256]{1,0:T(8,128)S(1)}, f32[48,256]{1,0:T(8,128)S(1)}, u32[]{:S(2)}, u32[]{:S(2)}) collective-permute-start(f32[48,256]{1,0:T(8,128)S(1)} %get-tuple-element.87.z1), channel_id=1, source_target_pairs={{0,4},{1,5},{2,6},{3,7},{4,0},{5,1},{6,2},{7,3},{8,12},{9,13},{10,... | collective-permute-start | bytes 147464 | tf_op jit(solution)/shard_map/ppermute | solution.py:83
  23.4 0.0 collective-permute-start.13
  23.4 0.0 collective-permute-done.7.x1
  23.4 1.5 %collective-permute-start.8 = (f32[32,256]{1,0:T(8,128)S(1)}, f32[32,256]{1,0:T(8,128)S(1)}, u32[]{:S(2)}, u32[]{:S(2)}) collective-permute-start(f32[32,256]{1,0:T(8,128)S(1)} %get-tuple-element.76), channel_id=1, source_target_pairs={{0,2},{1,3},{2,0},{3,1},{4,6},{5,7},{6,4},{7,5},{8,10},{9,11},{10,... | collective-permute-start | bytes 98312 | tf_op jit(solution)/shard_map/ppermute | solution.py:83
  25.0 3.2 %tin_first.1 = (f32[64,8,32,128]{3,2,1,0:T(8,128)S(1)}, f32[64,8,32,128]{3,2,1,0:T(8,128)S(1)}) custom-call(f32[64,8,32,128]{3,2,1,0:T(8,128)S(1)} %get-tuple-element.65.padded_in, s32[64,16,1024]{2,1,0:T(8,128)S(1)} %copy-done.1, f32[64,256]{1,0:T(8,128)S(1)} %collective-permute-done.x1, ...), custom_call_target="tpu_custom_call", output_to_operand_aliasing={{0}: (0, {})} | custom-call | bytes 20971520 | tf_op jit(solution)/shard_map/tin_first/pallas_call | solution.py:730
  28.2 0.0 collective-permute-done.12.y1
  28.2 0.0 collective-permute-done.13.y2
  28.2 0.0 collective-permute-done.8.x2
  28.2 0.0 collective-permute-done.11.e2
  28.2 0.0 collective-permute-done.10.x3
  28.2 7.4 %last_sweep.1 = (f32[64,8,32,128]{3,2,1,0:T(8,128)S(1)}, f32[64,16,1024]{2,1,0:T(8,128)}, f32[48,64,256]{2,1,0:T(8,128)}) custom-call(f32[64,8,32,128]{3,2,1,0:T(8,128)S(1)} %get-tuple-element.66.padded_in, s32[64,16,1024]{2,1,0:T(8,128)S(1)} %copy-done.1, f32[16,1024]{1,0:T(8,128)S(1)} %get-tuple-element.67.plane, ...), custom_call_target="tpu_custom_call", output_to_operand_aliasing={{0}: (0, {})} | custom-call | bytes 37748736 | tf_op jit(solution)/shard_map/last_sweep/pallas_call | solution.py:782
Async XLA Ops:
  0.6 4.5 %copy-start.2 = (s32[1,48,64,256]{3,2,1,0:T(8,128)S(1)}, s32[1,48,64,256]{3,2,1,0:T(8,128)}, u32[]{:S(2)}) copy-start(s32[1,48,64,256]{3,2,1,0:T(8,128)} %ids.1) | copy-start | bytes 9437188
  0.6 4.5 %copy-start = (f32[1,48,64,256]{3,2,1,0:T(8,128)S(1)}, f32[1,48,64,256]{3,2,1,0:T(8,128)}, u32[]{:S(2)}) copy-start(f32[1,48,64,256]{3,2,1,0:T(8,128)} %floor.1) | copy-start | bytes 9437188
  2.1 6.5 %collective-permute-start.2 = (f32[64,1024]{1,0:T(8,128)S(1)}, f32[64,1024]{1,0:T(8,128)S(1)}, u32[]{:S(2)}, u32[]{:S(2)}) collective-permute-start(f32[64,1024]{1,0:T(8,128)S(1)} %get-tuple-element.56), channel_id=1, source_target_pairs={{0,1},{1,0},{2,3},{3,2},{4,5},{5,4},{6,7},{7,6},{8,9},{9,8},{10,11... | collective-permute-start | bytes 786440 | tf_op jit(solution)/shard_map/ppermute | solution.py:83
  2.6 12.4 %collective-permute-start.4 = (f32[64,1024]{1,0:T(8,128)S(1)}, f32[64,1024]{1,0:T(8,128)S(1)}, u32[]{:S(2)}, u32[]{:S(2)}) collective-permute-start(f32[64,1024]{1,0:T(8,128)S(1)} %get-tuple-element.60), channel_id=1, source_target_pairs={{0,16},{1,2},{2,1},{3,4},{4,3},{5,6},{6,5},{7,8},{8,7},{9,10},{10,... | collective-permute-start | bytes 786440 | tf_op jit(solution)/shard_map/ppermute | solution.py:83
  6.7 3.4 %collective-permute-start = (f32[64,256]{1,0:T(8,128)S(1)}, f32[64,256]{1,0:T(8,128)S(1)}, u32[]{:S(2)}, u32[]{:S(2)}) collective-permute-start(f32[64,256]{1,0:T(8,128)S(1)} %get-tuple-element.52), channel_id=1, source_target_pairs={{0,1},{1,0},{2,3},{3,2},{4,5},{5,4},{6,7},{7,6},{8,9},{9,8},{10,11... | collective-permute-start | bytes 196616 | tf_op jit(solution)/shard_map/ppermute | solution.py:83
  6.9 8.1 %collective-permute-start.5 = (f32[96,256]{1,0:T(8,128)S(1)}, f32[96,256]{1,0:T(8,128)S(1)}, u32[]{:S(2)}, u32[]{:S(2)}) collective-permute-start(f32[96,256]{1,0:T(8,128)S(1)} %get-tuple-element.62.z1), channel_id=1, source_target_pairs={{0,4},{1,5},{2,6},{3,7},{4,0},{5,1},{6,2},{7,3},{8,12},{9,13},{10,... | collective-permute-start | bytes 294920 | tf_op jit(solution)/shard_map/ppermute | solution.py:83
  8.5 6.5 %collective-permute-start.6 = (f32[96,256]{1,0:T(8,128)S(1)}, f32[96,256]{1,0:T(8,128)S(1)}, u32[]{:S(2)}, u32[]{:S(2)}) collective-permute-start(f32[96,256]{1,0:T(8,128)S(1)} %get-tuple-element.63.z2), channel_id=1, source_target_pairs={{0,1},{1,0},{2,3},{3,2},{4,8},{5,9},{6,10},{7,11},{8,4},{9,5},{10,... | collective-permute-start | bytes 294920 | tf_op jit(solution)/shard_map/ppermute | solution.py:83
  8.6 6.4 %collective-permute-start.3 = (f32[64,256]{1,0:T(8,128)S(1)}, f32[64,256]{1,0:T(8,128)S(1)}, u32[]{:S(2)}, u32[]{:S(2)}) collective-permute-start(f32[64,256]{1,0:T(8,128)S(1)} %get-tuple-element.58), channel_id=1, source_target_pairs={{0,3},{1,2},{2,1},{3,0},{4,7},{5,6},{6,5},{7,4},{8,11},{9,10},{10,... | collective-permute-start | bytes 196616 | tf_op jit(solution)/shard_map/ppermute | solution.py:83
  10.1 4.9 %collective-permute-start.1 = (f32[32,256]{1,0:T(8,128)S(1)}, f32[32,256]{1,0:T(8,128)S(1)}, u32[]{:S(2)}, u32[]{:S(2)}) collective-permute-start(f32[32,256]{1,0:T(8,128)S(1)} %get-tuple-element.55), channel_id=1, source_target_pairs={{0,2},{1,3},{2,0},{3,1},{4,6},{5,7},{6,4},{7,5},{8,10},{9,11},{10,... | collective-permute-start | bytes 98312 | tf_op jit(solution)/shard_map/ppermute | solution.py:83
  10.6 4.4 %copy-start.1 = (s32[64,16,1024]{2,1,0:T(8,128)S(1)}, s32[64,16,1024]{2,1,0:T(8,128)}, u32[]{:S(2)}) copy-start(s32[64,16,1024]{2,1,0:T(8,128)} %f.7) | copy-start | bytes 12582916
  16.1 4.2 %collective-permute-start.9 = (f32[64,1024]{1,0:T(8,128)S(1)}, f32[64,1024]{1,0:T(8,128)S(1)}, u32[]{:S(2)}, u32[]{:S(2)}) collective-permute-start(f32[64,1024]{1,0:T(8,128)S(1)} %get-tuple-element.77), channel_id=1, source_target_pairs={{0,1},{1,0},{2,3},{3,2},{4,5},{5,4},{6,7},{7,6},{8,9},{9,8},{10,11... | collective-permute-start | bytes 786440 | tf_op jit(solution)/shard_map/ppermute | solution.py:83
  16.2 12.1 %collective-permute-start.11 = (f32[64,1024]{1,0:T(8,128)S(1)}, f32[64,1024]{1,0:T(8,128)S(1)}, u32[]{:S(2)}, u32[]{:S(2)}) collective-permute-start(f32[64,1024]{1,0:T(8,128)S(1)} %get-tuple-element.81), channel_id=1, source_target_pairs={{0,16},{1,2},{2,1},{3,4},{4,3},{5,6},{6,5},{7,8},{8,7},{9,10},{10,... | collective-permute-start | bytes 786440 | tf_op jit(solution)/shard_map/ppermute | solution.py:83
  20.1 3.4 %collective-permute-start.7 = (f32[64,256]{1,0:T(8,128)S(1)}, f32[64,256]{1,0:T(8,128)S(1)}, u32[]{:S(2)}, u32[]{:S(2)}) collective-permute-start(f32[64,256]{1,0:T(8,128)S(1)} %get-tuple-element.73), channel_id=1, source_target_pairs={{0,1},{1,0},{2,3},{3,2},{4,5},{5,4},{6,7},{7,6},{8,9},{9,8},{10,11... | collective-permute-start | bytes 196616 | tf_op jit(solution)/shard_map/ppermute | solution.py:83
  20.3 8.0 %collective-permute-start.10 = (f32[64,256]{1,0:T(8,128)S(1)}, f32[64,256]{1,0:T(8,128)S(1)}, u32[]{:S(2)}, u32[]{:S(2)}) collective-permute-start(f32[64,256]{1,0:T(8,128)S(1)} %get-tuple-element.79), channel_id=1, source_target_pairs={{0,3},{1,2},{2,1},{3,0},{4,7},{5,6},{6,5},{7,4},{8,11},{9,10},{10,... | collective-permute-start | bytes 196616 | tf_op jit(solution)/shard_map/ppermute | solution.py:83
  22.7 5.5 %collective-permute-start.12 = (f32[48,256]{1,0:T(8,128)S(1)}, f32[48,256]{1,0:T(8,128)S(1)}, u32[]{:S(2)}, u32[]{:S(2)}) collective-permute-start(f32[48,256]{1,0:T(8,128)S(1)} %get-tuple-element.87.z1), channel_id=1, source_target_pairs={{0,4},{1,5},{2,6},{3,7},{4,0},{5,1},{6,2},{7,3},{8,12},{9,13},{10,... | collective-permute-start | bytes 147464 | tf_op jit(solution)/shard_map/ppermute | solution.py:83
  23.4 4.7 %collective-permute-start.13 = (f32[48,256]{1,0:T(8,128)S(1)}, f32[48,256]{1,0:T(8,128)S(1)}, u32[]{:S(2)}, u32[]{:S(2)}) collective-permute-start(f32[48,256]{1,0:T(8,128)S(1)} %get-tuple-element.88.z2), channel_id=1, source_target_pairs={{0,1},{1,0},{2,3},{3,2},{4,8},{5,9},{6,10},{7,11},{8,4},{9,5},{10,... | collective-permute-start | bytes 147464 | tf_op jit(solution)/shard_map/ppermute | solution.py:83
  23.4 4.8 %collective-permute-start.8 = (f32[32,256]{1,0:T(8,128)S(1)}, f32[32,256]{1,0:T(8,128)S(1)}, u32[]{:S(2)}, u32[]{:S(2)}) collective-permute-start(f32[32,256]{1,0:T(8,128)S(1)} %get-tuple-element.76), channel_id=1, source_target_pairs={{0,2},{1,3},{2,0},{3,1},{4,6},{5,7},{6,4},{7,5},{8,10},{9,11},{10,... | collective-permute-start | bytes 98312 | tf_op jit(solution)/shard_map/ppermute | solution.py:83

commit v5 on v4

--- a/solution.py
+++ b/solution.py
@@ -13,6 +13,7 @@
 HR = 0.2
 LANES = 128
 SUBL = 8
+BODY = 16
 F32 = jnp.float32
 ANY = pl.BlockSpec(memory_space=pl.ANY)
 VMEM = pl.BlockSpec(memory_space=pltpu.VMEM)
@@ -321,12 +322,13 @@
                 fzv[rs, at] = fz
 
     def chunk(c, _):
-        start = pl.multiple_of(c * step, SUBL)
-        for offset in range(step):
-            layer(start, offset)
+        for block in range(BODY // step):
+            start = pl.multiple_of(c * BODY + block * step, SUBL)
+            for offset in range(step):
+                layer(start, offset)
         return 0
 
-    lax.fori_loop(0, nr // step, chunk, 0)
+    lax.fori_loop(0, nr // BODY, chunk, 0)
     for copy in picks:
         copy.wait()
 
@@ -367,7 +369,7 @@
     nr, cx, width = g.shape
     tiles, wide = cx // SUBL, width // LANES
     step = SUBL
-    chunks = nr // step
+    chunks = nr // BODY
     floor_sides(None, plane, x1, x2, x3, z1, z2, y1, y2, own, kc, kr, tcol, trow, bv)
     rows, lanes = iotas()
     r_first, r_last = rows == 0, rows == SUBL - 1
@@ -429,13 +431,14 @@
                 gs, ups = gn, un
 
     def store(c):
-        at = pl.ds(c * step, step)
+        at = pl.ds(c * BODY, BODY)
         return pltpu.make_async_copy(ov.at[at], out.at[at], sem.at[c])
 
     def chunk(c, _):
-        start = pl.multiple_of(c * step, SUBL)
-        for offset in range(step):
-            layer(start, offset)
+        for block in range(BODY // step):
+            start = pl.multiple_of(c * BODY + block * step, SUBL)
+            for offset in range(step):
+                layer(start, offset)
 
         @pl.when(c == 0)
         def _():
@@ -459,7 +462,7 @@
     ]
 
 
-def floor_finish(part, g, tcol, trow, bv, out, own, o1, o2, sem):
+def floor_finish(part, g, tcol, trow, bv, out, own, o1, o2):
     nr, cx, width = g.shape
     godd = place()[3]
     rows, lanes = iotas()
@@ -471,14 +474,13 @@
     chunks = nr // step
     own[...] = jnp.zeros_like(own)
 
-    def rows_of(c):
-        at = pl.ds(pl.multiple_of(c * step, SUBL), step)
-        low, high = out.at[at, 0, :], out.at[at, cx - 1, :]
-        return low, high, o1.at[at], o2.at[at]
+    zero = jnp.zeros((SUBL, LANES), F32)
 
     def chunk(c, _):
         start = pl.multiple_of(c * step, SUBL)
 
+        touch = jnp.where(c == 0, HR, 0.0)
+        ends = [[zero] * wide, [zero] * wide]
         for offset in range(step):
             z = start + offset
             back = lax.rem(LANES - z, LANES)
@@ -487,6 +489,8 @@
                 sides = pltpu.roll(tcol[offset % 2, rs, :], back, 1)
                 for j, at in enumerate(spans):
                     v = part[z, rs, at]
+                    if offset == 0:
+                        v = v + touch * (bv[rs, at] - g[z, rs, at])
                     if j == 0:
                         v = v + jnp.where(l_first, sides, 0.0)
                     if j + 1 == wide:
@@ -495,15 +499,9 @@
                         if t == edge:
                             side = trow[s, pl.ds(start, SUBL), at][offset : offset + 1]
                             v = v + jnp.where(mask, jnp.broadcast_to(side, v.shape), 0.0)
+                            turned = pltpu.roll(v, offset + s, 0) if (offset + s) % SUBL else v
+                            ends[s][j] = jnp.where(rows == offset, turned, ends[s][j])
                     out[z, rs, at] = v
-
-        @pl.when(c == 0)
-        def _():
-            out[0, :, :] = out[0] + HR * (bv[...] - g[0])
-
-        low, high, to1, to2 = rows_of(c)
-        select_copy(godd, (low, to1), (high, to1), sem.at[c])
-        select_copy(godd, (high, to2), (low, to2), sem.at[chunks + c])
         for t in range(tiles):
             rs = slice(t * SUBL, (t + 1) * SUBL)
             edges = lambda offset: (
@@ -511,16 +509,13 @@
                 out[start + offset, rs, spans[-1]],
             )
             keep_columns(own, 0, start, step, rs, edges)
+        for at, low, high in zip(spans, *ends):
+            o1[pl.ds(start, step), at] = jnp.where(godd, low, high)
+            o2[pl.ds(start, step), at] = jnp.where(godd, high, low)
         return 0
 
     lax.fori_loop(0, chunks, chunk, 0)
     own[1, :, :] = pltpu.roll(own[1], 1, 1)
-    copies = []
-    for c in range(chunks):
-        low, _, to1, to2 = rows_of(c)
-        copies.append(pltpu.make_async_copy(low, to1, sem.at[c]))
-        copies.append(pltpu.make_async_copy(low, to2, sem.at[chunks + c]))
-    return copies
 
 
 def fill_rows(padded, e1, e2, start):
@@ -674,14 +669,12 @@
 
 def floor_edge_kernel(
     b_plane, plane, x1, x2, x3, g, part, z1, z2, y1, y2, own, halves,
-    ox1, ox2, ox3, g_new, own_new, oz1, oz2, kc, kr, tcol, trow, bv, sem
+    ox1, ox2, ox3, g_new, own_new, oz1, oz2, kc, kr, tcol, trow, bv
 ):
     group, column, odd, _ = place()
     floor_sides(halves, b_plane, x1, x2, x3, z1, z2, y1, y2, own, kc, kr, tcol, trow, bv)
-    copies = floor_finish(part, g, tcol, trow, bv, g_new, own_new, oz1, oz2, sem)
+    floor_finish(part, g, tcol, trow, bv, g_new, own_new, oz1, oz2)
     put_parts(ox1, ox2, ox3, own_new, plane, g_new.at[0], column, odd)
-    for copy in copies:
-        copy.wait()
 
 
 def floor_edges(*arrays):
@@ -694,7 +687,7 @@
         + [shape(own.shape), shape((2, nr, width))],
         in_specs=[VMEM] * 13,
         out_specs=[VMEM] * 9,
-        scratch_shapes=floor_scratch(g.shape)[1:],
+        scratch_shapes=floor_scratch(g.shape)[1:-1],
         compiler_params=params(2),
         cost_estimate=cost(0, 10 << 20),
         name="floor_edges",
@@ -710,17 +703,18 @@
         gather_floor_top(pv, x1, x2, x3, g)
 
         def chunk(c, _):
-            start = pl.multiple_of(c * step, SUBL)
-            fill_rows(padded, e1, e2, start)
-            for offset in range(step):
-
-                def store(t, j, value):
-                    out[start + offset, j, (t + 1) * SUBL : (t + 2) * SUBL, :] = value
-
-                tin_layer(padded, f, rates, start, offset, store)
+            for block in range(BODY // step):
+                start = pl.multiple_of(c * BODY + block * step, SUBL)
+                fill_rows(padded, e1, e2, start)
+                for offset in range(step):
+
+                    def store(t, j, value):
+                        out[start + offset, j, (t + 1) * SUBL : (t + 2) * SUBL, :] = value
+
+                    tin_layer(padded, f, rates, start, offset, store)
             return 0
 
-        lax.fori_loop(0, zt // step, chunk, 0)
+        lax.fori_loop(0, zt // BODY, chunk, 0)
         for t in range(tiles):
             rs = slice((t + 1) * SUBL, (t + 2) * SUBL)
             for j in range(wide):
@@ -744,14 +738,15 @@
     zt, step = padded.shape[0], SUBL
 
     def store(c):
-        at = pl.ds(c * step, step)
+        at = pl.ds(c * BODY, BODY)
         return pltpu.make_async_copy(ov.at[at], out.at[at], sem.at[c])
 
     def chunk(c, _):
-        start = pl.multiple_of(c * step, SUBL)
-        fill_rows(padded, e1, e2, start)
-        for offset in range(step):
-            tin_layer(padded, f, rates, start, offset, flat_store(ov.at[start + offset]))
+        for block in range(BODY // step):
+            start = pl.multiple_of(c * BODY + block * step, SUBL)
+            fill_rows(padded, e1, e2, start)
+            for offset in range(step):
+                tin_layer(padded, f, rates, start, offset, flat_store(ov.at[start + offset]))
 
         @pl.when(c == 0)
         def _():
@@ -760,8 +755,8 @@
         store(c).start()
         return 0
 
-    lax.fori_loop(0, zt // step, chunk, 0)
-    return [store(c) for c in range(zt // step)]
+    lax.fori_loop(0, zt // BODY, chunk, 0)
+    return [store(c) for c in range(zt // BODY)]
 
 
 def last_sweep(padded, f, plane, x1, x2, x3, e1, e2, g, rates, coefs, z1, z2, y1, y2, own, kc, kr):

time: 35.7 us -> 35 us (0.980)
  Pallas kernels: 21.2 us -> 20.5 us
  transfers between devices with their start and end apart: 14 -> 14, of which waited for: 0 -> 0; matrix products, arithmetic and copies ran while one was open for 0% -> 0% of each run, Pallas kernels for 32% -> 31%
where the time goes in v5:
time: 35 us; the launch traced here: 34.8 us
  Pallas kernels  20.5 us (59%)
  starting transfers between devices  13.5 us (39%)
  between operations  0.8 us (2%)
    ppermute x14, starting transfers between devices, swap(): return lax.ppermute(value, ('grp', 'len'), pairs)  13.5 us
    pallas_call x1, Pallas kernels, last_sweep(): pl.pallas_call(kernel, out_shape=[shape(padded.shape), far(f.shape), far(...  7.19 us
    pallas_call x1, Pallas kernels, local(): pl.pallas_call(inner_kernel, out_shape=[shape(g.shape)] * 5 + [shape((4,...  4.27 us
    pallas_call x1, Pallas kernels, tin_first(): pl.pallas_call(kernel, out_shape=[shape(padded.shape)] * 2, in_specs=[VME...  3.09 us
    pallas_call x1, Pallas kernels, floor_edges(): pl.pallas_call(floor_edge_kernel, out_shape=[shape(v.shape) for v in (x1,...  1.98 us
    pallas_call x1, Pallas kernels, local(): pl.pallas_call(pack_columns_kernel, out_shape=[shape((cx, 2 * LANES)), sh...  1.49 us
    pallas_call x1, Pallas kernels, local(): pl.pallas_call(pack_rows_kernel, out_shape=[shape((zt, ny))] * 2 + [shape...  1.42 us
    pallas_call x1, Pallas kernels, tin_edges(): pl.pallas_call(tin_edge_kernel, out_shape=[shape(padded.shape), shape(e1....  1.05 us
  transfers between devices with their start and end apart: 14, of which 0 were waited for; matrix products, arithmetic and copies ran while one was open for 0% of the time, Pallas kernels for 31%

profile of v5, /device:TPU:0, one launch (start us, length us, event | category | flops | bytes accessed | tf_op | source)
XLA Modules:
  0.0 34.8 jit_solution(9822259430982911536)
XLA Ops:
  0.6 0.0 copy-start.2
  0.6 0.0 copy-start
  0.6 1.4 %pack_rows.1 = (f32[64,1024]{1,0:T(8,128)S(1)}, f32[64,1024]{1,0:T(8,128)S(1)}, f32[96,256]{1,0:T(8,128)S(1)}, f32[96,256]{1,0:T(8,128)S(1)}) custom-call(f32[64,16,1024]{2,1,0:T(8,128)} %u.5, f32[1,48,64,256]{3,2,1,0:T(8,128)} %floor.1, s32[1,48,64,256]{3,2,1,0:T(8,128)} %ids.1), custom_call_target="tpu_custom_call" | custom-call | bytes 6291456 | tf_op jit(solution)/shard_map/pack_rows/pallas_call | solution.py:800
  2.1 0.5 %collective-permute-start.2 = (f32[64,1024]{1,0:T(8,128)S(1)}, f32[64,1024]{1,0:T(8,128)S(1)}, u32[]{:S(2)}, u32[]{:S(2)}) collective-permute-start(f32[64,1024]{1,0:T(8,128)S(1)} %get-tuple-element.56), channel_id=1, source_target_pairs={{0,1},{1,0},{2,3},{3,2},{4,5},{5,4},{6,7},{7,6},{8,9},{9,8},{10,11... | collective-permute-start | bytes 786440 | tf_op jit(solution)/shard_map/ppermute | solution.py:84
  2.6 2.6 %collective-permute-start.4 = (f32[64,1024]{1,0:T(8,128)S(1)}, f32[64,1024]{1,0:T(8,128)S(1)}, u32[]{:S(2)}, u32[]{:S(2)}) collective-permute-start(f32[64,1024]{1,0:T(8,128)S(1)} %get-tuple-element.60), channel_id=1, source_target_pairs={{0,16},{1,2},{2,1},{3,4},{4,3},{5,6},{6,5},{7,8},{8,7},{9,10},{10,... | collective-permute-start | bytes 786440 | tf_op jit(solution)/shard_map/ppermute | solution.py:84
  5.2 0.0 copy-done.2
  5.2 0.0 copy-done
  5.2 1.5 %pack_columns.1 = (f32[64,256]{1,0:T(8,128)S(1)}, f32[32,256]{1,0:T(8,128)S(1)}, f32[64,256]{1,0:T(8,128)S(1)}, f32[2,64,128]{2,1,0:T(8,128)S(1)}, f32[2,64,128]...) custom-call(f32[48,64,256]{2,1,0:T(8,128)S(1)} %bitcast.4, s32[48,64,256]{2,1,0:T(8,128)S(1)} %bitcast.9, ...), custom_call_target="tpu_custom_call" | custom-call | bytes 12582912 | tf_op jit(solution)/shard_map/pack_columns/pallas_call | solution.py:812
  6.7 0.2 collective-permute-start
  6.9 1.6 %collective-permute-start.5 = (f32[96,256]{1,0:T(8,128)S(1)}, f32[96,256]{1,0:T(8,128)S(1)}, u32[]{:S(2)}, u32[]{:S(2)}) collective-permute-start(f32[96,256]{1,0:T(8,128)S(1)} %get-tuple-element.62.z1), channel_id=1, source_target_pairs={{0,4},{1,5},{2,6},{3,7},{4,0},{5,1},{6,2},{7,3},{8,12},{9,13},{10,... | collective-permute-start | bytes 294920 | tf_op jit(solution)/shard_map/ppermute | solution.py:84
  8.5 0.2 collective-permute-start.6
  8.6 0.0 collective-permute-done.2.e1
  8.6 1.5 %collective-permute-start.3 = (f32[64,256]{1,0:T(8,128)S(1)}, f32[64,256]{1,0:T(8,128)S(1)}, u32[]{:S(2)}, u32[]{:S(2)}) collective-permute-start(f32[64,256]{1,0:T(8,128)S(1)} %get-tuple-element.58), channel_id=1, source_target_pairs={{0,3},{1,2},{2,1},{3,0},{4,7},{5,6},{6,5},{7,4},{8,11},{9,10},{10,... | collective-permute-start | bytes 196616 | tf_op jit(solution)/shard_map/ppermute | solution.py:84
  10.1 0.0 collective-permute-done.x1
  10.1 0.5 %collective-permute-start.1 = (f32[32,256]{1,0:T(8,128)S(1)}, f32[32,256]{1,0:T(8,128)S(1)}, u32[]{:S(2)}, u32[]{:S(2)}) collective-permute-start(f32[32,256]{1,0:T(8,128)S(1)} %get-tuple-element.55), channel_id=1, source_target_pairs={{0,2},{1,3},{2,0},{3,1},{4,6},{5,7},{6,4},{7,5},{8,10},{9,11},{10,... | collective-permute-start | bytes 98312 | tf_op jit(solution)/shard_map/ppermute | solution.py:84
  10.6 0.0 copy-start.1
  10.6 4.3 %inner.1 = (f32[48,64,256]{2,1,0:T(8,128)S(1)}, f32[48,64,256]{2,1,0:T(8,128)S(1)}, f32[48,64,256]{2,1,0:T(8,128)S(1)}, f32[48,64,256]{2,1,0:T(8,128)S(1)}, f32[...) custom-call(s32[48,64,256]{2,1,0:T(8,128)S(1)} %bitcast.10, ...), custom_call_target="tpu_custom_call" | custom-call | bytes 25165824 | tf_op jit(solution)/shard_map/inner/pallas_call | solution.py:839
  14.9 0.0 collective-permute-done.5.y1
  14.9 0.0 collective-permute-done.6.y2
  14.9 0.0 collective-permute-done.1.x2
  14.9 0.0 collective-permute-done.4.e2
  14.9 0.0 collective-permute-done.3.x3
  14.9 0.0 copy-done.1
  14.9 1.0 %tin_edges.1 = (f32[64,8,32,128]{3,2,1,0:T(8,128)S(1)}, f32[64,1024]{1,0:T(8,128)S(1)}, f32[64,1024]{1,0:T(8,128)S(1)}, f32[16,1024]{1,0:T(8,128)S(1)}) custom-call(f32[64,8,32,128]{3,2,1,0:T(8,128)S(1)} %get-tuple-element.49.padded_in, s32[64,16,1024]{2,1,0:T(8,128)S(1)} %copy-done.1, ...), custom_call_target="tpu_custom_call", output_to_operand_aliasing={{0}: (0, {})} | custom-call | bytes 4194304 | tf_op jit(solution)/shard_map/tin_edges/pallas_call | solution.py:657
  16.0 0.1 collective-permute-start.9
  16.1 1.6 %collective-permute-start.11 = (f32[64,1024]{1,0:T(8,128)S(1)}, f32[64,1024]{1,0:T(8,128)S(1)}, u32[]{:S(2)}, u32[]{:S(2)}) collective-permute-start(f32[64,1024]{1,0:T(8,128)S(1)} %get-tuple-element.81), channel_id=1, source_target_pairs={{0,16},{1,2},{2,1},{3,4},{4,3},{5,6},{6,5},{7,8},{8,7},{9,10},{10,... | collective-permute-start | bytes 786440 | tf_op jit(solution)/shard_map/ppermute | solution.py:84
  17.6 2.0 %floor_edges.1 = (f32[64,256]{1,0:T(8,128)S(1)}, f32[32,256]{1,0:T(8,128)S(1)}, f32[64,256]{1,0:T(8,128)S(1)}, f32[48,64,256]{2,1,0:T(8,128)S(1)}, f32[2,64,128]...) custom-call(f32[16,1024]{1,0:T(8,128)S(1)} %get-tuple-element.68.b_p, ...), custom_call_target="tpu_custom_call" | custom-call | bytes 10485760 | tf_op jit(solution)/shard_map/floor_edges/pallas_call | solution.py:683
  19.6 0.2 collective-permute-start.7
  19.8 0.0 collective-permute-done.9.e1
  19.8 2.4 %collective-permute-start.10 = (f32[64,256]{1,0:T(8,128)S(1)}, f32[64,256]{1,0:T(8,128)S(1)}, u32[]{:S(2)}, u32[]{:S(2)}) collective-permute-start(f32[64,256]{1,0:T(8,128)S(1)} %get-tuple-element.79), channel_id=1, source_target_pairs={{0,3},{1,2},{2,1},{3,0},{4,7},{5,6},{6,5},{7,4},{8,11},{9,10},{10,... | collective-permute-start | bytes 196616 | tf_op jit(solution)/shard_map/ppermute | solution.py:84
  22.3 0.7 %collective-permute-start.12 = (f32[48,256]{1,0:T(8,128)S(1)}, f32[48,256]{1,0:T(8,128)S(1)}, u32[]{:S(2)}, u32[]{:S(2)}) collective-permute-start(f32[48,256]{1,0:T(8,128)S(1)} %get-tuple-element.87.z1), channel_id=1, source_target_pairs={{0,4},{1,5},{2,6},{3,7},{4,0},{5,1},{6,2},{7,3},{8,12},{9,13},{10,... | collective-permute-start | bytes 147464 | tf_op jit(solution)/shard_map/ppermute | solution.py:84
  23.0 0.0 collective-permute-start.13
  23.0 0.0 collective-permute-done.7.x1
  23.0 1.5 %collective-permute-start.8 = (f32[32,256]{1,0:T(8,128)S(1)}, f32[32,256]{1,0:T(8,128)S(1)}, u32[]{:S(2)}, u32[]{:S(2)}) collective-permute-start(f32[32,256]{1,0:T(8,128)S(1)} %get-tuple-element.76), channel_id=1, source_target_pairs={{0,2},{1,3},{2,0},{3,1},{4,6},{5,7},{6,4},{7,5},{8,10},{9,11},{10,... | collective-permute-start | bytes 98312 | tf_op jit(solution)/shard_map/ppermute | solution.py:84
  24.5 3.1 %tin_first.1 = (f32[64,8,32,128]{3,2,1,0:T(8,128)S(1)}, f32[64,8,32,128]{3,2,1,0:T(8,128)S(1)}) custom-call(f32[64,8,32,128]{3,2,1,0:T(8,128)S(1)} %get-tuple-element.65.padded_in, s32[64,16,1024]{2,1,0:T(8,128)S(1)} %copy-done.1, f32[64,256]{1,0:T(8,128)S(1)} %collective-permute-done.x1, ...), custom_call_target="tpu_custom_call", output_to_operand_aliasing={{0}: (0, {})} | custom-call | bytes 20971520 | tf_op jit(solution)/shard_map/tin_first/pallas_call | solution.py:724
  27.6 0.0 collective-permute-done.12.y1
  27.6 0.0 collective-permute-done.13.y2
  27.6 0.0 collective-permute-done.8.x2
  27.6 0.0 collective-permute-done.11.e2
  27.6 0.0 collective-permute-done.10.x3
  27.7 7.2 %last_sweep.1 = (f32[64,8,32,128]{3,2,1,0:T(8,128)S(1)}, f32[64,16,1024]{2,1,0:T(8,128)}, f32[48,64,256]{2,1,0:T(8,128)}) custom-call(f32[64,8,32,128]{3,2,1,0:T(8,128)S(1)} %get-tuple-element.66.padded_in, s32[64,16,1024]{2,1,0:T(8,128)S(1)} %copy-done.1, f32[16,1024]{1,0:T(8,128)S(1)} %get-tuple-element.67.plane, ...), custom_call_target="tpu_custom_call", output_to_operand_aliasing={{0}: (0, {})} | custom-call | bytes 37748736 | tf_op jit(solution)/shard_map/last_sweep/pallas_call | solution.py:777
Async XLA Ops:
  0.6 4.5 %copy-start.2 = (s32[1,48,64,256]{3,2,1,0:T(8,128)S(1)}, s32[1,48,64,256]{3,2,1,0:T(8,128)}, u32[]{:S(2)}) copy-start(s32[1,48,64,256]{3,2,1,0:T(8,128)} %ids.1) | copy-start | bytes 9437188
  0.6 4.5 %copy-start = (f32[1,48,64,256]{3,2,1,0:T(8,128)S(1)}, f32[1,48,64,256]{3,2,1,0:T(8,128)}, u32[]{:S(2)}) copy-start(f32[1,48,64,256]{3,2,1,0:T(8,128)} %floor.1) | copy-start | bytes 9437188
  2.1 6.5 %collective-permute-start.2 = (f32[64,1024]{1,0:T(8,128)S(1)}, f32[64,1024]{1,0:T(8,128)S(1)}, u32[]{:S(2)}, u32[]{:S(2)}) collective-permute-start(f32[64,1024]{1,0:T(8,128)S(1)} %get-tuple-element.56), channel_id=1, source_target_pairs={{0,1},{1,0},{2,3},{3,2},{4,5},{5,4},{6,7},{7,6},{8,9},{9,8},{10,11... | collective-permute-start | bytes 786440 | tf_op jit(solution)/shard_map/ppermute | solution.py:84
  2.6 12.3 %collective-permute-start.4 = (f32[64,1024]{1,0:T(8,128)S(1)}, f32[64,1024]{1,0:T(8,128)S(1)}, u32[]{:S(2)}, u32[]{:S(2)}) collective-permute-start(f32[64,1024]{1,0:T(8,128)S(1)} %get-tuple-element.60), channel_id=1, source_target_pairs={{0,16},{1,2},{2,1},{3,4},{4,3},{5,6},{6,5},{7,8},{8,7},{9,10},{10,... | collective-permute-start | bytes 786440 | tf_op jit(solution)/shard_map/ppermute | solution.py:84
  6.7 3.4 %collective-permute-start = (f32[64,256]{1,0:T(8,128)S(1)}, f32[64,256]{1,0:T(8,128)S(1)}, u32[]{:S(2)}, u32[]{:S(2)}) collective-permute-start(f32[64,256]{1,0:T(8,128)S(1)} %get-tuple-element.52), channel_id=1, source_target_pairs={{0,1},{1,0},{2,3},{3,2},{4,5},{5,4},{6,7},{7,6},{8,9},{9,8},{10,11... | collective-permute-start | bytes 196616 | tf_op jit(solution)/shard_map/ppermute | solution.py:84
  6.9 8.0 %collective-permute-start.5 = (f32[96,256]{1,0:T(8,128)S(1)}, f32[96,256]{1,0:T(8,128)S(1)}, u32[]{:S(2)}, u32[]{:S(2)}) collective-permute-start(f32[96,256]{1,0:T(8,128)S(1)} %get-tuple-element.62.z1), channel_id=1, source_target_pairs={{0,4},{1,5},{2,6},{3,7},{4,0},{5,1},{6,2},{7,3},{8,12},{9,13},{10,... | collective-permute-start | bytes 294920 | tf_op jit(solution)/shard_map/ppermute | solution.py:84
  8.5 6.4 %collective-permute-start.6 = (f32[96,256]{1,0:T(8,128)S(1)}, f32[96,256]{1,0:T(8,128)S(1)}, u32[]{:S(2)}, u32[]{:S(2)}) collective-permute-start(f32[96,256]{1,0:T(8,128)S(1)} %get-tuple-element.63.z2), channel_id=1, source_target_pairs={{0,1},{1,0},{2,3},{3,2},{4,8},{5,9},{6,10},{7,11},{8,4},{9,5},{10,... | collective-permute-start | bytes 294920 | tf_op jit(solution)/shard_map/ppermute | solution.py:84
  8.6 6.3 %collective-permute-start.3 = (f32[64,256]{1,0:T(8,128)S(1)}, f32[64,256]{1,0:T(8,128)S(1)}, u32[]{:S(2)}, u32[]{:S(2)}) collective-permute-start(f32[64,256]{1,0:T(8,128)S(1)} %get-tuple-element.58), channel_id=1, source_target_pairs={{0,3},{1,2},{2,1},{3,0},{4,7},{5,6},{6,5},{7,4},{8,11},{9,10},{10,... | collective-permute-start | bytes 196616 | tf_op jit(solution)/shard_map/ppermute | solution.py:84
  10.1 4.8 %collective-permute-start.1 = (f32[32,256]{1,0:T(8,128)S(1)}, f32[32,256]{1,0:T(8,128)S(1)}, u32[]{:S(2)}, u32[]{:S(2)}) collective-permute-start(f32[32,256]{1,0:T(8,128)S(1)} %get-tuple-element.55), channel_id=1, source_target_pairs={{0,2},{1,3},{2,0},{3,1},{4,6},{5,7},{6,4},{7,5},{8,10},{9,11},{10,... | collective-permute-start | bytes 98312 | tf_op jit(solution)/shard_map/ppermute | solution.py:84
  10.6 4.3 %copy-start.1 = (s32[64,16,1024]{2,1,0:T(8,128)S(1)}, s32[64,16,1024]{2,1,0:T(8,128)}, u32[]{:S(2)}) copy-start(s32[64,16,1024]{2,1,0:T(8,128)} %f.7) | copy-start | bytes 12582916
  16.0 3.8 %collective-permute-start.9 = (f32[64,1024]{1,0:T(8,128)S(1)}, f32[64,1024]{1,0:T(8,128)S(1)}, u32[]{:S(2)}, u32[]{:S(2)}) collective-permute-start(f32[64,1024]{1,0:T(8,128)S(1)} %get-tuple-element.77), channel_id=1, source_target_pairs={{0,1},{1,0},{2,3},{3,2},{4,5},{5,4},{6,7},{7,6},{8,9},{9,8},{10,11... | collective-permute-start | bytes 786440 | tf_op jit(solution)/shard_map/ppermute | solution.py:84
  16.1 11.6 %collective-permute-start.11 = (f32[64,1024]{1,0:T(8,128)S(1)}, f32[64,1024]{1,0:T(8,128)S(1)}, u32[]{:S(2)}, u32[]{:S(2)}) collective-permute-start(f32[64,1024]{1,0:T(8,128)S(1)} %get-tuple-element.81), channel_id=1, source_target_pairs={{0,16},{1,2},{2,1},{3,4},{4,3},{5,6},{6,5},{7,8},{8,7},{9,10},{10,... | collective-permute-start | bytes 786440 | tf_op jit(solution)/shard_map/ppermute | solution.py:84
  19.6 3.4 %collective-permute-start.7 = (f32[64,256]{1,0:T(8,128)S(1)}, f32[64,256]{1,0:T(8,128)S(1)}, u32[]{:S(2)}, u32[]{:S(2)}) collective-permute-start(f32[64,256]{1,0:T(8,128)S(1)} %get-tuple-element.73), channel_id=1, source_target_pairs={{0,1},{1,0},{2,3},{3,2},{4,5},{5,4},{6,7},{7,6},{8,9},{9,8},{10,11... | collective-permute-start | bytes 196616 | tf_op jit(solution)/shard_map/ppermute | solution.py:84
  19.8 7.8 %collective-permute-start.10 = (f32[64,256]{1,0:T(8,128)S(1)}, f32[64,256]{1,0:T(8,128)S(1)}, u32[]{:S(2)}, u32[]{:S(2)}) collective-permute-start(f32[64,256]{1,0:T(8,128)S(1)} %get-tuple-element.79), channel_id=1, source_target_pairs={{0,3},{1,2},{2,1},{3,0},{4,7},{5,6},{6,5},{7,4},{8,11},{9,10},{10,... | collective-permute-start | bytes 196616 | tf_op jit(solution)/shard_map/ppermute | solution.py:84
  22.3 5.4 %collective-permute-start.12 = (f32[48,256]{1,0:T(8,128)S(1)}, f32[48,256]{1,0:T(8,128)S(1)}, u32[]{:S(2)}, u32[]{:S(2)}) collective-permute-start(f32[48,256]{1,0:T(8,128)S(1)} %get-tuple-element.87.z1), channel_id=1, source_target_pairs={{0,4},{1,5},{2,6},{3,7},{4,0},{5,1},{6,2},{7,3},{8,12},{9,13},{10,... | collective-permute-start | bytes 147464 | tf_op jit(solution)/shard_map/ppermute | solution.py:84
  23.0 4.6 %collective-permute-start.13 = (f32[48,256]{1,0:T(8,128)S(1)}, f32[48,256]{1,0:T(8,128)S(1)}, u32[]{:S(2)}, u32[]{:S(2)}) collective-permute-start(f32[48,256]{1,0:T(8,128)S(1)} %get-tuple-element.88.z2), channel_id=1, source_target_pairs={{0,1},{1,0},{2,3},{3,2},{4,8},{5,9},{6,10},{7,11},{8,4},{9,5},{10,... | collective-permute-start | bytes 147464 | tf_op jit(solution)/shard_map/ppermute | solution.py:84
  23.0 4.6 %collective-permute-start.8 = (f32[32,256]{1,0:T(8,128)S(1)}, f32[32,256]{1,0:T(8,128)S(1)}, u32[]{:S(2)}, u32[]{:S(2)}) collective-permute-start(f32[32,256]{1,0:T(8,128)S(1)} %get-tuple-element.76), channel_id=1, source_target_pairs={{0,2},{1,3},{2,0},{3,1},{4,6},{5,7},{6,4},{7,5},{8,10},{9,11},{10,... | collective-permute-start | bytes 98312 | tf_op jit(solution)/shard_map/ppermute | solution.py:84

commit v6 on v5

--- a/solution.py
+++ b/solution.py
@@ -197,21 +197,22 @@
     own_m[...] = jnp.zeros_like(own_m)
 
     def chunk(c, _):
-        start = c * step
-        for t in range(cx // SUBL):
-            rs = slice(t * SUBL, (t + 1) * SUBL)
-
-            def edges(ref):
-                return lambda offset: (
-                    ref[start + offset, rs, :LANES],
-                    ref[start + offset, rs, width - LANES :],
-                )
-
-            keep_columns(own, 0, start, step, rs, edges(g))
-            keep_columns(own_m, shift, start, step, rs, edges(m))
+        for block in range(BODY // step):
+            start = c * BODY + block * step
+            for t in range(cx // SUBL):
+                rs = slice(t * SUBL, (t + 1) * SUBL)
+
+                def edges(ref):
+                    return lambda offset: (
+                        ref[start + offset, rs, :LANES],
+                        ref[start + offset, rs, width - LANES :],
+                    )
+
+                keep_columns(own, 0, start, step, rs, edges(g))
+                keep_columns(own_m, shift, start, step, rs, edges(m))
         return 0
 
-    lax.fori_loop(0, nr // step, chunk, 0)
+    lax.fori_loop(0, nr // BODY, chunk, 0)
     is_k = lax.broadcasted_iota(jnp.int32, (cx, LANES), 1) >= shift
     for s in range(2):
         codes = pltpu.roll(own_m[s], s, 1)
@@ -231,7 +232,7 @@
         halves[i, :, :] = jnp.broadcast_to(0.5 * cond_v[0:1, i : i + 1], (SUBL, LANES))
 
 
-def inner_kernel(m, g, halves, u, f, out, ce, cw, cn, cz, urows, frows, padded, kv, fzv, sem):
+def inner_kernel(m, g, halves, u, f, out, ce, cw, cn, cz, urows, frows, padded, kv, fzv, fxv, sem):
     nr, cx, width = m.shape
     nx = u.shape[1]
     picks = [
@@ -258,10 +259,12 @@
             value = jnp.where(ids == i, values[i], value)
         return value
 
+    kv[...] = jnp.zeros_like(kv)
+    fxv[...] = jnp.zeros_like(fxv)
     for t in range(tiles):
         rs = slice(t * SUBL, (t + 1) * SUBL)
-        for at in spans:
-            kv[0, rs, at] = lookup(m[0, rs, at])
+        for j, at in enumerate(spans):
+            kv[0, j, rs, :] = lookup(m[0, rs, at])
     fzv[...] = jnp.zeros_like(fzv)
     turn = lambda vs, by, axis: [pltpu.roll(v, by, axis) for v in vs]
 
@@ -276,14 +279,13 @@
         def tile(t):
             rs = slice(t * SUBL, (t + 1) * SUBL)
             gs = [g[z, rs, at] for at in spans]
-            ks = [kv[here, rs, at] for at in spans]
-            return gs, ks, turn(gs, SUBL - 1, 0), turn(ks, SUBL - 1, 0)
+            ks = [kv[here, j, rs, :] for j in range(wide)]
+            return gs, ks, turn(gs, SUBL - 1, 0)
 
         now = tile(0)
-        prev = [zero] * wide
         for t in range(tiles):
             rs = slice(t * SUBL, (t + 1) * SUBL)
-            gs, ks, g_up, k_up = now
+            gs, ks, g_up = now
             if t + 1 < tiles:
                 now = tile(t + 1)
             ge, gw = turn(gs, LANES - 1, 1), turn(gs, 1, 1)
@@ -293,13 +295,13 @@
                 k_next, v_next = lookup(m[above, rs, at]), g[above, rs, at]
                 if last:
                     k_next, v_next = scale * k_next, scale * v_next
-                kv[there, rs, at] = k_next
+                kv[there, j, rs, :] = k_next
                 below = k + k_next
+                north = k + kv[here, j, t * SUBL + 1 : (t + 1) * SUBL + 1, :]
                 if t + 1 < tiles:
-                    north = k + jnp.where(r_last, now[3][j], k_up[j])
                     xp = jnp.where(r_last, now[2][j], g_up[j])
                 else:
-                    north, xp = jnp.where(r_last, 0.0, k + k_up[j]), g_up[j]
+                    north, xp = jnp.where(r_last, 0.0, north), g_up[j]
                 if j + 1 < wide:
                     east = k + jnp.where(l_last, ke[j + 1], ke[j])
                     yp = jnp.where(l_last, ge[j + 1], ge[j])
@@ -313,9 +315,8 @@
                 ce[z, rs, at], cw[z, rs, at] = east, west
                 cn[z, rs, at], cz[z, rs, at] = north, below
                 fx = north * (xp - v)
-                turned = pltpu.roll(fx, 1, 0)
-                fxm = jnp.where(r_first, prev[j], turned)
-                prev[j] = turned
+                fxv[offset % 4, j, (t + 1) * SUBL : (t + 2) * SUBL, :] = fx
+                fxm = fxv[offset % 4, j, (t + 1) * SUBL - 1 : (t + 2) * SUBL - 1, :]
                 fz = below * (v_next - v)
                 side = east * (yp - v) + west * (ym - v)
                 out[z, rs, at] = v + ((fx - fxm) + side + (fz - fzv[rs, at]))
@@ -364,7 +365,7 @@
 
 
 def floor_kernel(
-    g, ce, cw, cn, cz, plane, x1, x2, x3, z1, z2, y1, y2, own, kc, kr, out, ov, fzv, tcol, trow, bv, sem
+    g, ce, cw, cn, cz, plane, x1, x2, x3, z1, z2, y1, y2, own, kc, kr, out, ov, fxv, fzv, tcol, trow, bv, sem
 ):
     nr, cx, width = g.shape
     tiles, wide = cx // SUBL, width // LANES
@@ -396,7 +397,6 @@
 
         low, high = row_of(0), row_of(1)
         gs, ups = tile(0)
-        prev = [-v for v in low]
         for t in range(tiles):
             rs = slice(t * SUBL, (t + 1) * SUBL)
             if t + 1 < tiles:
@@ -410,9 +410,10 @@
                     fx = cn[z, rs, at] * (jnp.where(r_last, un[j], ups[j]) - v)
                 else:
                     fx = jnp.where(r_last, high[j], cn[z, rs, at] * (ups[j] - v))
-                turned = pltpu.roll(fx, 1, 0)
-                fxm = jnp.where(r_first, prev[j], turned)
-                prev[j] = turned
+                fxv[offset % 4, j, (t + 1) * SUBL : (t + 2) * SUBL, :] = fx
+                fxm = fxv[offset % 4, j, (t + 1) * SUBL - 1 : (t + 2) * SUBL - 1, :]
+                if t == 0:
+                    fxm = jnp.where(r_first, -low[j], fxm)
                 yp = jnp.where(l_last, east[j + 1], east[j]) if j + 1 < wide else east[j]
                 ym = jnp.where(l_first, west[j - 1], west[j]) if j > 0 else west[j]
                 side = ce[z, rs, at] * (yp - v) + cw[z, rs, at] * (ym - v)
@@ -471,15 +472,14 @@
     tiles, wide = cx // SUBL, width // LANES
     spans = [slice(j * LANES, (j + 1) * LANES) for j in range(wide)]
     step = SUBL
-    chunks = nr // step
     own[...] = jnp.zeros_like(own)
 
     zero = jnp.zeros((SUBL, LANES), F32)
 
-    def chunk(c, _):
-        start = pl.multiple_of(c * step, SUBL)
-
-        touch = jnp.where(c == 0, HR, 0.0)
+    def block(start, first):
+
+        if first is not None:
+            touch = jnp.where(first, HR, 0.0)
         ends = [[zero] * wide, [zero] * wide]
         for offset in range(step):
             z = start + offset
@@ -489,7 +489,7 @@
                 sides = pltpu.roll(tcol[offset % 2, rs, :], back, 1)
                 for j, at in enumerate(spans):
                     v = part[z, rs, at]
-                    if offset == 0:
+                    if offset == 0 and first is not None:
                         v = v + touch * (bv[rs, at] - g[z, rs, at])
                     if j == 0:
                         v = v + jnp.where(l_first, sides, 0.0)
@@ -512,9 +512,13 @@
         for at, low, high in zip(spans, *ends):
             o1[pl.ds(start, step), at] = jnp.where(godd, low, high)
             o2[pl.ds(start, step), at] = jnp.where(godd, high, low)
+
+    def chunk(c, _):
+        for i in range(BODY // step):
+            block(pl.multiple_of(c * BODY + i * step, SUBL), None if i else c == 0)
         return 0
 
-    lax.fori_loop(0, chunks, chunk, 0)
+    lax.fori_loop(0, nr // BODY, chunk, 0)
     own[1, :, :] = pltpu.roll(own[1], 1, 1)
 
 
@@ -785,6 +789,7 @@
             pltpu.VMEM(g.shape, F32),
             pltpu.VMEM(plane.shape, F32),
             pltpu.SemaphoreType.DMA((zt // SUBL,)),
+            pltpu.VMEM((4, g.shape[2] // LANES, g.shape[1] + SUBL, LANES), F32),
         ]
         + floor_scratch(g.shape),
         compiler_params=params(10),
@@ -847,8 +852,9 @@
         in_specs=[VMEM] * 3 + [ANY] * 2,
         out_specs=[VMEM] * 8,
         scratch_shapes=[
-            pltpu.VMEM((2, cx, width), F32),
+            pltpu.VMEM((2, width // LANES, cx + SUBL, LANES), F32),
             pltpu.VMEM((cx, width), F32),
+            pltpu.VMEM((4, width // LANES, cx + SUBL, LANES), F32),
             pltpu.SemaphoreType.DMA((6 + ny // LANES,)),
         ],
         compiler_params=params(2),
@@ -865,7 +871,7 @@
     )
     w1 = swap(w1, "e1")
     d1, w3 = lax.optimization_barrier((d1, w3))
-    w1, w2 = lax.optimization_barrier((w1, w2))
+    w1, z2 = lax.optimization_barrier((w1, z2))
     w2, w3 = swap(w2, "x2"), swap(w3, "x3")
     y1, y2 = swap(z1, "z1"), swap(z2, "z2")
     u1 = tin_first(padded, f, x1, x2, x3, e1, e2, g, rates)

time: 35 us -> 34.4 us (0.983)
  the two profiles are of different devices: /device:TPU:0 before, /device:TPU:8 now
where the time goes in v6:
time: 34.4 us; the launch traced here: 33.8 us
  Pallas kernels  19.8 us (58%)
  starting transfers between devices  12.1 us (35%)
  waiting for transfers between devices  1 us (3%)
  between operations  0.77 us (2%)
    ppermute x14, starting transfers between devices, swap(): return lax.ppermute(value, ('grp', 'len'), pairs)  12.1 us
    pallas_call x1, Pallas kernels, last_sweep(): pl.pallas_call(kernel, out_shape=[shape(padded.shape), far(f.shape), far(...  7.09 us
    pallas_call x1, Pallas kernels, local(): pl.pallas_call(inner_kernel, out_shape=[shape(g.shape)] * 5 + [shape((4,...  4.11 us
    pallas_call x1, Pallas kernels, tin_first(): pl.pallas_call(kernel, out_shape=[shape(padded.shape)] * 2, in_specs=[VME...  3.09 us
    pallas_call x1, Pallas kernels, floor_edges(): pl.pallas_call(floor_edge_kernel, out_shape=[shape(v.shape) for v in (x1,...  1.8 us
    pallas_call x1, Pallas kernels, local(): pl.pallas_call(pack_rows_kernel, out_shape=[shape((zt, ny))] * 2 + [shape...  1.42 us
    pallas_call x1, Pallas kernels, local(): pl.pallas_call(pack_columns_kernel, out_shape=[shape((cx, 2 * LANES)), sh...  1.29 us
    pallas_call x1, Pallas kernels, tin_edges(): pl.pallas_call(tin_edge_kernel, out_shape=[shape(padded.shape), shape(e1....  1.05 us
  transfers between devices with their start and end apart: 14, of which 1 were waited for; matrix products, arithmetic and copies ran while one was open for 0% of the time, Pallas kernels for 30%

profile of v6, /device:TPU:8, one launch (start us, length us, event | category | flops | bytes accessed | tf_op | source)
XLA Modules:
  0.0 33.8 jit_solution(6441167059168102891)
XLA Ops:
  0.6 0.0 copy-start.2
  0.6 0.0 copy-start
  0.6 1.4 %pack_rows.1 = (f32[64,1024]{1,0:T(8,128)S(1)}, f32[64,1024]{1,0:T(8,128)S(1)}, f32[96,256]{1,0:T(8,128)S(1)}, f32[96,256]{1,0:T(8,128)S(1)}) custom-call(f32[64,16,1024]{2,1,0:T(8,128)} %u.5, f32[1,48,64,256]{3,2,1,0:T(8,128)} %floor.1, s32[1,48,64,256]{3,2,1,0:T(8,128)} %ids.1), custom_call_target="tpu_custom_call" | custom-call | bytes 6291456 | tf_op jit(solution)/shard_map/pack_rows/pallas_call | solution.py:805
  2.1 0.1 collective-permute-start.2
  2.2 1.5 %collective-permute-start.4 = (f32[64,1024]{1,0:T(8,128)S(1)}, f32[64,1024]{1,0:T(8,128)S(1)}, u32[]{:S(2)}, u32[]{:S(2)}) collective-permute-start(f32[64,1024]{1,0:T(8,128)S(1)} %get-tuple-element.60), channel_id=1, source_target_pairs={{0,16},{1,2},{2,1},{3,4},{4,3},{5,6},{6,5},{7,8},{8,7},{9,10},{10,... | collective-permute-start | bytes 786440 | tf_op jit(solution)/shard_map/ppermute | solution.py:84
  3.7 0.0 copy-done.2
  3.7 0.1 copy-done
  3.8 1.3 %pack_columns.1 = (f32[64,256]{1,0:T(8,128)S(1)}, f32[32,256]{1,0:T(8,128)S(1)}, f32[64,256]{1,0:T(8,128)S(1)}, f32[2,64,128]{2,1,0:T(8,128)S(1)}, f32[2,64,128]...) custom-call(f32[48,64,256]{2,1,0:T(8,128)S(1)} %bitcast.4, s32[48,64,256]{2,1,0:T(8,128)S(1)} %bitcast.9, ...), custom_call_target="tpu_custom_call" | custom-call | bytes 12582912 | tf_op jit(solution)/shard_map/pack_columns/pallas_call | solution.py:817
  5.1 0.1 collective-permute-start
  5.2 0.5 %collective-permute-start.5 = (f32[96,256]{1,0:T(8,128)S(1)}, f32[96,256]{1,0:T(8,128)S(1)}, u32[]{:S(2)}, u32[]{:S(2)}) collective-permute-start(f32[96,256]{1,0:T(8,128)S(1)} %get-tuple-element.62.z1), channel_id=1, source_target_pairs={{0,4},{1,5},{2,6},{3,7},{4,0},{5,1},{6,2},{7,3},{8,12},{9,13},{10,... | collective-permute-start | bytes 294920 | tf_op jit(solution)/shard_map/ppermute | solution.py:84
  5.7 2.7 %collective-permute-start.6 = (f32[96,256]{1,0:T(8,128)S(1)}, f32[96,256]{1,0:T(8,128)S(1)}, u32[]{:S(2)}, u32[]{:S(2)}) collective-permute-start(f32[96,256]{1,0:T(8,128)S(1)} %get-tuple-element.63.z2), channel_id=1, source_target_pairs={{0,1},{1,0},{2,3},{3,2},{4,8},{5,9},{6,10},{7,11},{8,4},{9,5},{10,... | collective-permute-start | bytes 294920 | tf_op jit(solution)/shard_map/ppermute | solution.py:84
  8.4 0.0 collective-permute-done.2.e1
  8.4 1.0 %collective-permute-start.3 = (f32[64,256]{1,0:T(8,128)S(1)}, f32[64,256]{1,0:T(8,128)S(1)}, u32[]{:S(2)}, u32[]{:S(2)}) collective-permute-start(f32[64,256]{1,0:T(8,128)S(1)} %get-tuple-element.58), channel_id=1, source_target_pairs={{0,3},{1,2},{2,1},{3,0},{4,7},{5,6},{6,5},{7,4},{8,11},{9,10},{10,... | collective-permute-start | bytes 196616 | tf_op jit(solution)/shard_map/ppermute | solution.py:84
  9.4 0.0 collective-permute-done.x1
  9.4 0.6 %collective-permute-start.1 = (f32[32,256]{1,0:T(8,128)S(1)}, f32[32,256]{1,0:T(8,128)S(1)}, u32[]{:S(2)}, u32[]{:S(2)}) collective-permute-start(f32[32,256]{1,0:T(8,128)S(1)} %get-tuple-element.55), channel_id=1, source_target_pairs={{0,2},{1,3},{2,0},{3,1},{4,6},{5,7},{6,4},{7,5},{8,10},{9,11},{10,... | collective-permute-start | bytes 98312 | tf_op jit(solution)/shard_map/ppermute | solution.py:84
  10.0 0.0 copy-start.1
  10.0 4.1 %inner.1 = (f32[48,64,256]{2,1,0:T(8,128)S(1)}, f32[48,64,256]{2,1,0:T(8,128)S(1)}, f32[48,64,256]{2,1,0:T(8,128)S(1)}, f32[48,64,256]{2,1,0:T(8,128)S(1)}, f32[...) custom-call(s32[48,64,256]{2,1,0:T(8,128)S(1)} %bitcast.10, ...), custom_call_target="tpu_custom_call" | custom-call | bytes 25165824 | tf_op jit(solution)/shard_map/inner/pallas_call | solution.py:844
  14.1 0.0 collective-permute-done.5.y1
  14.1 0.0 collective-permute-done.6.y2
  14.1 0.0 collective-permute-done.1.x2
  14.1 0.0 collective-permute-done.4.e2
  14.1 0.0 collective-permute-done.3.x3
  14.2 0.0 copy-done.1
  14.2 1.0 %tin_edges.1 = (f32[64,8,32,128]{3,2,1,0:T(8,128)S(1)}, f32[64,1024]{1,0:T(8,128)S(1)}, f32[64,1024]{1,0:T(8,128)S(1)}, f32[16,1024]{1,0:T(8,128)S(1)}) custom-call(f32[64,8,32,128]{3,2,1,0:T(8,128)S(1)} %get-tuple-element.49.padded_in, s32[64,16,1024]{2,1,0:T(8,128)S(1)} %copy-done.1, ...), custom_call_target="tpu_custom_call", output_to_operand_aliasing={{0}: (0, {})} | custom-call | bytes 4194304 | tf_op jit(solution)/shard_map/tin_edges/pallas_call | solution.py:661
  15.2 0.3 collective-permute-start.9
  15.6 0.2 collective-permute-start.11
  15.8 1.8 %floor_edges.1 = (f32[64,256]{1,0:T(8,128)S(1)}, f32[32,256]{1,0:T(8,128)S(1)}, f32[64,256]{1,0:T(8,128)S(1)}, f32[48,64,256]{2,1,0:T(8,128)S(1)}, f32[2,64,128]...) custom-call(f32[16,1024]{1,0:T(8,128)S(1)} %get-tuple-element.68.b_p, ...), custom_call_target="tpu_custom_call" | custom-call | bytes 10485760 | tf_op jit(solution)/shard_map/floor_edges/pallas_call | solution.py:687
  17.6 1.5 %collective-permute-start.7 = (f32[64,256]{1,0:T(8,128)S(1)}, f32[64,256]{1,0:T(8,128)S(1)}, u32[]{:S(2)}, u32[]{:S(2)}) collective-permute-start(f32[64,256]{1,0:T(8,128)S(1)} %get-tuple-element.73), channel_id=1, source_target_pairs={{0,1},{1,0},{2,3},{3,2},{4,5},{5,4},{6,7},{7,6},{8,9},{9,8},{10,11... | collective-permute-start | bytes 196616 | tf_op jit(solution)/shard_map/ppermute | solution.py:84
  19.1 0.0 collective-permute-done.9.e1
  19.1 0.4 %collective-permute-start.10 = (f32[64,256]{1,0:T(8,128)S(1)}, f32[64,256]{1,0:T(8,128)S(1)}, u32[]{:S(2)}, u32[]{:S(2)}) collective-permute-start(f32[64,256]{1,0:T(8,128)S(1)} %get-tuple-element.79), channel_id=1, source_target_pairs={{0,3},{1,2},{2,1},{3,0},{4,7},{5,6},{6,5},{7,4},{8,11},{9,10},{10,... | collective-permute-start | bytes 196616 | tf_op jit(solution)/shard_map/ppermute | solution.py:84
  19.5 1.2 %collective-permute-start.12 = (f32[48,256]{1,0:T(8,128)S(1)}, f32[48,256]{1,0:T(8,128)S(1)}, u32[]{:S(2)}, u32[]{:S(2)}) collective-permute-start(f32[48,256]{1,0:T(8,128)S(1)} %get-tuple-element.87.z1), channel_id=1, source_target_pairs={{0,4},{1,5},{2,6},{3,7},{4,0},{5,1},{6,2},{7,3},{8,12},{9,13},{10,... | collective-permute-start | bytes 147464 | tf_op jit(solution)/shard_map/ppermute | solution.py:84
  20.7 0.0 collective-permute-done.7.x1
  20.7 1.3 %collective-permute-start.13 = (f32[48,256]{1,0:T(8,128)S(1)}, f32[48,256]{1,0:T(8,128)S(1)}, u32[]{:S(2)}, u32[]{:S(2)}) collective-permute-start(f32[48,256]{1,0:T(8,128)S(1)} %get-tuple-element.88.z2), channel_id=1, source_target_pairs={{0,1},{1,0},{2,3},{3,2},{4,8},{5,9},{6,10},{7,11},{8,4},{9,5},{10,... | collective-permute-start | bytes 147464 | tf_op jit(solution)/shard_map/ppermute | solution.py:84
  22.0 0.6 %collective-permute-start.8 = (f32[32,256]{1,0:T(8,128)S(1)}, f32[32,256]{1,0:T(8,128)S(1)}, u32[]{:S(2)}, u32[]{:S(2)}) collective-permute-start(f32[32,256]{1,0:T(8,128)S(1)} %get-tuple-element.76), channel_id=1, source_target_pairs={{0,2},{1,3},{2,0},{3,1},{4,6},{5,7},{6,4},{7,5},{8,10},{9,11},{10,... | collective-permute-start | bytes 98312 | tf_op jit(solution)/shard_map/ppermute | solution.py:84
  22.6 3.1 %tin_first.1 = (f32[64,8,32,128]{3,2,1,0:T(8,128)S(1)}, f32[64,8,32,128]{3,2,1,0:T(8,128)S(1)}) custom-call(f32[64,8,32,128]{3,2,1,0:T(8,128)S(1)} %get-tuple-element.65.padded_in, s32[64,16,1024]{2,1,0:T(8,128)S(1)} %copy-done.1, f32[64,256]{1,0:T(8,128)S(1)} %collective-permute-done.x1, ...), custom_call_target="tpu_custom_call", output_to_operand_aliasing={{0}: (0, {})} | custom-call | bytes 20971520 | tf_op jit(solution)/shard_map/tin_first/pallas_call | solution.py:728
  25.7 1.0 %collective-permute-done.8.x2 = f32[32,256]{1,0:T(8,128)S(1)} collective-permute-done((f32[32,256]{1,0:T(8,128)S(1)}, f32[32,256]{1,0:T(8,128)S(1)}, u32[]{:S(2)}, u32[]{:S(2)}) %collective-permute-start.8) | collective-permute-done | bytes 32800 | tf_op jit(solution)/shard_map/ppermute | solution.py:84
  26.7 0.0 collective-permute-done.12.y1
  26.7 0.0 collective-permute-done.13.y2
  26.7 0.0 collective-permute-done.11.e2
  26.7 0.0 collective-permute-done.10.x3
  26.7 7.1 %last_sweep.1 = (f32[64,8,32,128]{3,2,1,0:T(8,128)S(1)}, f32[64,16,1024]{2,1,0:T(8,128)}, f32[48,64,256]{2,1,0:T(8,128)}) custom-call(f32[64,8,32,128]{3,2,1,0:T(8,128)S(1)} %get-tuple-element.66.padded_in, s32[64,16,1024]{2,1,0:T(8,128)S(1)} %copy-done.1, f32[16,1024]{1,0:T(8,128)S(1)} %get-tuple-element.67.plane, ...), custom_call_target="tpu_custom_call", output_to_operand_aliasing={{0}: (0, {})} | custom-call | bytes 37748736 | tf_op jit(solution)/shard_map/last_sweep/pallas_call | solution.py:781
Async XLA Ops:
  0.6 3.0 %copy-start.2 = (s32[1,48,64,256]{3,2,1,0:T(8,128)S(1)}, s32[1,48,64,256]{3,2,1,0:T(8,128)}, u32[]{:S(2)}) copy-start(s32[1,48,64,256]{3,2,1,0:T(8,128)} %ids.1) | copy-start | bytes 9437188
  0.6 3.1 %copy-start = (f32[1,48,64,256]{3,2,1,0:T(8,128)S(1)}, f32[1,48,64,256]{3,2,1,0:T(8,128)}, u32[]{:S(2)}) copy-start(f32[1,48,64,256]{3,2,1,0:T(8,128)} %floor.1) | copy-start | bytes 9437188
  2.1 6.3 %collective-permute-start.2 = (f32[64,1024]{1,0:T(8,128)S(1)}, f32[64,1024]{1,0:T(8,128)S(1)}, u32[]{:S(2)}, u32[]{:S(2)}) collective-permute-start(f32[64,1024]{1,0:T(8,128)S(1)} %get-tuple-element.56), channel_id=1, source_target_pairs={{0,1},{1,0},{2,3},{3,2},{4,5},{5,4},{6,7},{7,6},{8,9},{9,8},{10,11... | collective-permute-start | bytes 786440 | tf_op jit(solution)/shard_map/ppermute | solution.py:84
  2.2 12.0 %collective-permute-start.4 = (f32[64,1024]{1,0:T(8,128)S(1)}, f32[64,1024]{1,0:T(8,128)S(1)}, u32[]{:S(2)}, u32[]{:S(2)}) collective-permute-start(f32[64,1024]{1,0:T(8,128)S(1)} %get-tuple-element.60), channel_id=1, source_target_pairs={{0,16},{1,2},{2,1},{3,4},{4,3},{5,6},{6,5},{7,8},{8,7},{9,10},{10,... | collective-permute-start | bytes 786440 | tf_op jit(solution)/shard_map/ppermute | solution.py:84
  5.1 4.3 %collective-permute-start = (f32[64,256]{1,0:T(8,128)S(1)}, f32[64,256]{1,0:T(8,128)S(1)}, u32[]{:S(2)}, u32[]{:S(2)}) collective-permute-start(f32[64,256]{1,0:T(8,128)S(1)} %get-tuple-element.52), channel_id=1, source_target_pairs={{0,1},{1,0},{2,3},{3,2},{4,5},{5,4},{6,7},{7,6},{8,9},{9,8},{10,11... | collective-permute-start | bytes 196616 | tf_op jit(solution)/shard_map/ppermute | solution.py:84
  5.2 8.9 %collective-permute-start.5 = (f32[96,256]{1,0:T(8,128)S(1)}, f32[96,256]{1,0:T(8,128)S(1)}, u32[]{:S(2)}, u32[]{:S(2)}) collective-permute-start(f32[96,256]{1,0:T(8,128)S(1)} %get-tuple-element.62.z1), channel_id=1, source_target_pairs={{0,4},{1,5},{2,6},{3,7},{4,0},{5,1},{6,2},{7,3},{8,12},{9,13},{10,... | collective-permute-start | bytes 294920 | tf_op jit(solution)/shard_map/ppermute | solution.py:84
  5.7 8.4 %collective-permute-start.6 = (f32[96,256]{1,0:T(8,128)S(1)}, f32[96,256]{1,0:T(8,128)S(1)}, u32[]{:S(2)}, u32[]{:S(2)}) collective-permute-start(f32[96,256]{1,0:T(8,128)S(1)} %get-tuple-element.63.z2), channel_id=1, source_target_pairs={{0,1},{1,0},{2,3},{3,2},{4,8},{5,9},{6,10},{7,11},{8,4},{9,5},{10,... | collective-permute-start | bytes 294920 | tf_op jit(solution)/shard_map/ppermute | solution.py:84
  8.4 5.8 %collective-permute-start.3 = (f32[64,256]{1,0:T(8,128)S(1)}, f32[64,256]{1,0:T(8,128)S(1)}, u32[]{:S(2)}, u32[]{:S(2)}) collective-permute-start(f32[64,256]{1,0:T(8,128)S(1)} %get-tuple-element.58), channel_id=1, source_target_pairs={{0,3},{1,2},{2,1},{3,0},{4,7},{5,6},{6,5},{7,4},{8,11},{9,10},{10,... | collective-permute-start | bytes 196616 | tf_op jit(solution)/shard_map/ppermute | solution.py:84
  9.4 4.7 %collective-permute-start.1 = (f32[32,256]{1,0:T(8,128)S(1)}, f32[32,256]{1,0:T(8,128)S(1)}, u32[]{:S(2)}, u32[]{:S(2)}) collective-permute-start(f32[32,256]{1,0:T(8,128)S(1)} %get-tuple-element.55), channel_id=1, source_target_pairs={{0,2},{1,3},{2,0},{3,1},{4,6},{5,7},{6,4},{7,5},{8,10},{9,11},{10,... | collective-permute-start | bytes 98312 | tf_op jit(solution)/shard_map/ppermute | solution.py:84
  10.0 4.2 %copy-start.1 = (s32[64,16,1024]{2,1,0:T(8,128)S(1)}, s32[64,16,1024]{2,1,0:T(8,128)}, u32[]{:S(2)}) copy-start(s32[64,16,1024]{2,1,0:T(8,128)} %f.7) | copy-start | bytes 12582916
  15.2 3.9 %collective-permute-start.9 = (f32[64,1024]{1,0:T(8,128)S(1)}, f32[64,1024]{1,0:T(8,128)S(1)}, u32[]{:S(2)}, u32[]{:S(2)}) collective-permute-start(f32[64,1024]{1,0:T(8,128)S(1)} %get-tuple-element.77), channel_id=1, source_target_pairs={{0,1},{1,0},{2,3},{3,2},{4,5},{5,4},{6,7},{7,6},{8,9},{9,8},{10,11... | collective-permute-start | bytes 786440 | tf_op jit(solution)/shard_map/ppermute | solution.py:84
  15.6 11.1 %collective-permute-start.11 = (f32[64,1024]{1,0:T(8,128)S(1)}, f32[64,1024]{1,0:T(8,128)S(1)}, u32[]{:S(2)}, u32[]{:S(2)}) collective-permute-start(f32[64,1024]{1,0:T(8,128)S(1)} %get-tuple-element.81), channel_id=1, source_target_pairs={{0,16},{1,2},{2,1},{3,4},{4,3},{5,6},{6,5},{7,8},{8,7},{9,10},{10,... | collective-permute-start | bytes 786440 | tf_op jit(solution)/shard_map/ppermute | solution.py:84
  17.6 3.1 %collective-permute-start.7 = (f32[64,256]{1,0:T(8,128)S(1)}, f32[64,256]{1,0:T(8,128)S(1)}, u32[]{:S(2)}, u32[]{:S(2)}) collective-permute-start(f32[64,256]{1,0:T(8,128)S(1)} %get-tuple-element.73), channel_id=1, source_target_pairs={{0,1},{1,0},{2,3},{3,2},{4,5},{5,4},{6,7},{7,6},{8,9},{9,8},{10,11... | collective-permute-start | bytes 196616 | tf_op jit(solution)/shard_map/ppermute | solution.py:84
  19.1 7.6 %collective-permute-start.10 = (f32[64,256]{1,0:T(8,128)S(1)}, f32[64,256]{1,0:T(8,128)S(1)}, u32[]{:S(2)}, u32[]{:S(2)}) collective-permute-start(f32[64,256]{1,0:T(8,128)S(1)} %get-tuple-element.79), channel_id=1, source_target_pairs={{0,3},{1,2},{2,1},{3,0},{4,7},{5,6},{6,5},{7,4},{8,11},{9,10},{10,... | collective-permute-start | bytes 196616 | tf_op jit(solution)/shard_map/ppermute | solution.py:84
  19.5 7.2 %collective-permute-start.12 = (f32[48,256]{1,0:T(8,128)S(1)}, f32[48,256]{1,0:T(8,128)S(1)}, u32[]{:S(2)}, u32[]{:S(2)}) collective-permute-start(f32[48,256]{1,0:T(8,128)S(1)} %get-tuple-element.87.z1), channel_id=1, source_target_pairs={{0,4},{1,5},{2,6},{3,7},{4,0},{5,1},{6,2},{7,3},{8,12},{9,13},{10,... | collective-permute-start | bytes 147464 | tf_op jit(solution)/shard_map/ppermute | solution.py:84
  20.7 6.0 %collective-permute-start.13 = (f32[48,256]{1,0:T(8,128)S(1)}, f32[48,256]{1,0:T(8,128)S(1)}, u32[]{:S(2)}, u32[]{:S(2)}) collective-permute-start(f32[48,256]{1,0:T(8,128)S(1)} %get-tuple-element.88.z2), channel_id=1, source_target_pairs={{0,1},{1,0},{2,3},{3,2},{4,8},{5,9},{6,10},{7,11},{8,4},{9,5},{10,... | collective-permute-start | bytes 147464 | tf_op jit(solution)/shard_map/ppermute | solution.py:84
  22.0 4.7 %collective-permute-start.8 = (f32[32,256]{1,0:T(8,128)S(1)}, f32[32,256]{1,0:T(8,128)S(1)}, u32[]{:S(2)}, u32[]{:S(2)}) collective-permute-start(f32[32,256]{1,0:T(8,128)S(1)} %get-tuple-element.76), channel_id=1, source_target_pairs={{0,2},{1,3},{2,0},{3,1},{4,6},{5,7},{6,4},{7,5},{8,10},{9,11},{10,... | collective-permute-start | bytes 98312 | tf_op jit(solution)/shard_map/ppermute | solution.py:84

commit v7 on v6

--- a/solution.py
+++ b/solution.py
@@ -652,7 +652,10 @@
             o2[here, at] = jnp.where(lonely, 0.0, jnp.where(odd, high, low))
         return 0
 
-    lax.fori_loop(0, blocks, block, 0)
+    def pair(i, _):
+        return block(2 * i + 1, block(2 * i, 0))
+
+    lax.fori_loop(0, blocks // 2, pair, 0)
 
 
 def tin_edges(*arrays):
@@ -871,7 +874,7 @@
     )
     w1 = swap(w1, "e1")
     d1, w3 = lax.optimization_barrier((d1, w3))
-    w1, z2 = lax.optimization_barrier((w1, z2))
+    w1, z1, z2 = lax.optimization_barrier((w1, z1, z2))
     w2, w3 = swap(w2, "x2"), swap(w3, "x3")
     y1, y2 = swap(z1, "z1"), swap(z2, "z2")
     u1 = tin_first(padded, f, x1, x2, x3, e1, e2, g, rates)

time: 34.4 us -> 34.1 us (level)
  transfers between devices with their start and end apart: 14 -> 14, of which waited for: 1 -> 2; matrix products, arithmetic and copies ran while one was open for 0% -> 0% of each run, Pallas kernels for 30% -> 31%
where the time goes in v7:
time: 34.1 us; the launch traced here: 33.5 us
  Pallas kernels  19.5 us (57%)
  starting transfers between devices  12 us (35%)
  waiting for transfers between devices  1.01 us (3%)
  between operations  0.77 us (2%)
    ppermute x14, starting transfers between devices, swap(): return lax.ppermute(value, ('grp', 'len'), pairs)  12 us
    pallas_call x1, Pallas kernels, last_sweep(): pl.pallas_call(kernel, out_shape=[shape(padded.shape), far(f.shape), far(...  7.09 us
    pallas_call x1, Pallas kernels, local(): pl.pallas_call(inner_kernel, out_shape=[shape(g.shape)] * 5 + [shape((4,...  4.11 us
    pallas_call x1, Pallas kernels, tin_first(): pl.pallas_call(kernel, out_shape=[shape(padded.shape)] * 2, in_specs=[VME...  3.09 us
    pallas_call x1, Pallas kernels, floor_edges(): pl.pallas_call(floor_edge_kernel, out_shape=[shape(v.shape) for v in (x1,...  1.8 us
    pallas_call x1, Pallas kernels, local(): pl.pallas_call(pack_rows_kernel, out_shape=[shape((zt, ny))] * 2 + [shape...  1.42 us
    pallas_call x1, Pallas kernels, local(): pl.pallas_call(pack_columns_kernel, out_shape=[shape((cx, 2 * LANES)), sh...  1.29 us
    ppermute x14, waiting for transfers between devices, swap(): return lax.ppermute(value, ('grp', 'len'), pairs)  1.01 us
  transfers between devices with their start and end apart: 14, of which 2 were waited for; matrix products, arithmetic and copies ran while one was open for 0% of the time, Pallas kernels for 31%

profile of v7, /device:TPU:8, one launch (start us, length us, event | category | flops | bytes accessed | tf_op | source)
XLA Modules:
  0.0 33.5 jit_solution(16499210350001576050)
XLA Ops:
  0.6 0.0 copy-start.2
  0.6 0.0 copy-start
  0.6 1.4 %pack_rows.1 = (f32[64,1024]{1,0:T(8,128)S(1)}, f32[64,1024]{1,0:T(8,128)S(1)}, f32[96,256]{1,0:T(8,128)S(1)}, f32[96,256]{1,0:T(8,128)S(1)}) custom-call(f32[64,16,1024]{2,1,0:T(8,128)} %u.5, f32[1,48,64,256]{3,2,1,0:T(8,128)} %floor.1, s32[1,48,64,256]{3,2,1,0:T(8,128)} %ids.1), custom_call_target="tpu_custom_call" | custom-call | bytes 6291456 | tf_op jit(solution)/shard_map/pack_rows/pallas_call | solution.py:808
  2.1 0.1 collective-permute-start.2
  2.2 1.5 %collective-permute-start.4 = (f32[64,1024]{1,0:T(8,128)S(1)}, f32[64,1024]{1,0:T(8,128)S(1)}, u32[]{:S(2)}, u32[]{:S(2)}) collective-permute-start(f32[64,1024]{1,0:T(8,128)S(1)} %get-tuple-element.61), channel_id=1, source_target_pairs={{0,16},{1,2},{2,1},{3,4},{4,3},{5,6},{6,5},{7,8},{8,7},{9,10},{10,... | collective-permute-start | bytes 786440 | tf_op jit(solution)/shard_map/ppermute | solution.py:84
  3.7 0.0 copy-done.2
  3.7 0.1 copy-done
  3.8 1.3 %pack_columns.1 = (f32[64,256]{1,0:T(8,128)S(1)}, f32[32,256]{1,0:T(8,128)S(1)}, f32[64,256]{1,0:T(8,128)S(1)}, f32[2,64,128]{2,1,0:T(8,128)S(1)}, f32[2,64,128]...) custom-call(f32[48,64,256]{2,1,0:T(8,128)S(1)} %bitcast.4, s32[48,64,256]{2,1,0:T(8,128)S(1)} %bitcast.9, ...), custom_call_target="tpu_custom_call" | custom-call | bytes 12582912 | tf_op jit(solution)/shard_map/pack_columns/pallas_call | solution.py:820
  5.1 0.1 collective-permute-start
  5.2 0.5 %collective-permute-start.5 = (f32[96,256]{1,0:T(8,128)S(1)}, f32[96,256]{1,0:T(8,128)S(1)}, u32[]{:S(2)}, u32[]{:S(2)}) collective-permute-start(f32[96,256]{1,0:T(8,128)S(1)} %get-tuple-element.63.z1), channel_id=1, source_target_pairs={{0,4},{1,5},{2,6},{3,7},{4,0},{5,1},{6,2},{7,3},{8,12},{9,13},{10,... | collective-permute-start | bytes 294920 | tf_op jit(solution)/shard_map/ppermute | solution.py:84
  5.7 2.7 %collective-permute-start.6 = (f32[96,256]{1,0:T(8,128)S(1)}, f32[96,256]{1,0:T(8,128)S(1)}, u32[]{:S(2)}, u32[]{:S(2)}) collective-permute-start(f32[96,256]{1,0:T(8,128)S(1)} %get-tuple-element.64.z2), channel_id=1, source_target_pairs={{0,1},{1,0},{2,3},{3,2},{4,8},{5,9},{6,10},{7,11},{8,4},{9,5},{10,... | collective-permute-start | bytes 294920 | tf_op jit(solution)/shard_map/ppermute | solution.py:84
  8.4 0.0 collective-permute-done.2.e1
  8.4 1.0 %collective-permute-start.3 = (f32[64,256]{1,0:T(8,128)S(1)}, f32[64,256]{1,0:T(8,128)S(1)}, u32[]{:S(2)}, u32[]{:S(2)}) collective-permute-start(f32[64,256]{1,0:T(8,128)S(1)} %get-tuple-element.59), channel_id=1, source_target_pairs={{0,3},{1,2},{2,1},{3,0},{4,7},{5,6},{6,5},{7,4},{8,11},{9,10},{10,... | collective-permute-start | bytes 196616 | tf_op jit(solution)/shard_map/ppermute | solution.py:84
  9.4 0.0 collective-permute-done.x1
  9.4 0.6 %collective-permute-start.1 = (f32[32,256]{1,0:T(8,128)S(1)}, f32[32,256]{1,0:T(8,128)S(1)}, u32[]{:S(2)}, u32[]{:S(2)}) collective-permute-start(f32[32,256]{1,0:T(8,128)S(1)} %get-tuple-element.56), channel_id=1, source_target_pairs={{0,2},{1,3},{2,0},{3,1},{4,6},{5,7},{6,4},{7,5},{8,10},{9,11},{10,... | collective-permute-start | bytes 98312 | tf_op jit(solution)/shard_map/ppermute | solution.py:84
  10.0 0.0 copy-start.1
  10.0 4.1 %inner.1 = (f32[48,64,256]{2,1,0:T(8,128)S(1)}, f32[48,64,256]{2,1,0:T(8,128)S(1)}, f32[48,64,256]{2,1,0:T(8,128)S(1)}, f32[48,64,256]{2,1,0:T(8,128)S(1)}, f32[...) custom-call(s32[48,64,256]{2,1,0:T(8,128)S(1)} %bitcast.10, ...), custom_call_target="tpu_custom_call" | custom-call | bytes 25165824 | tf_op jit(solution)/shard_map/inner/pallas_call | solution.py:847
  14.1 0.0 collective-permute-done.5.y1
  14.1 0.0 collective-permute-done.6.y2
  14.1 0.0 collective-permute-done.1.x2
  14.1 0.0 collective-permute-done.4.e2
  14.1 0.0 collective-permute-done.3.x3
  14.2 0.0 copy-done.1
  14.2 0.7 %tin_edges.1 = (f32[64,8,32,128]{3,2,1,0:T(8,128)S(1)}, f32[64,1024]{1,0:T(8,128)S(1)}, f32[64,1024]{1,0:T(8,128)S(1)}, f32[16,1024]{1,0:T(8,128)S(1)}) custom-call(f32[64,8,32,128]{3,2,1,0:T(8,128)S(1)} %get-tuple-element.50.padded_in, s32[64,16,1024]{2,1,0:T(8,128)S(1)} %copy-done.1, ...), custom_call_target="tpu_custom_call", output_to_operand_aliasing={{0}: (0, {})} | custom-call | bytes 4194304 | tf_op jit(solution)/shard_map/tin_edges/pallas_call | solution.py:664
  14.9 0.3 collective-permute-start.9
  15.2 0.2 collective-permute-start.11
  15.5 1.8 %floor_edges.1 = (f32[64,256]{1,0:T(8,128)S(1)}, f32[32,256]{1,0:T(8,128)S(1)}, f32[64,256]{1,0:T(8,128)S(1)}, f32[48,64,256]{2,1,0:T(8,128)S(1)}, f32[2,64,128]...) custom-call(f32[16,1024]{1,0:T(8,128)S(1)} %get-tuple-element.69.b_p, ...), custom_call_target="tpu_custom_call" | custom-call | bytes 10485760 | tf_op jit(solution)/shard_map/floor_edges/pallas_call | solution.py:690
  17.3 1.5 %collective-permute-start.7 = (f32[64,256]{1,0:T(8,128)S(1)}, f32[64,256]{1,0:T(8,128)S(1)}, u32[]{:S(2)}, u32[]{:S(2)}) collective-permute-start(f32[64,256]{1,0:T(8,128)S(1)} %get-tuple-element.74), channel_id=1, source_target_pairs={{0,1},{1,0},{2,3},{3,2},{4,5},{5,4},{6,7},{7,6},{8,9},{9,8},{10,11... | collective-permute-start | bytes 196616 | tf_op jit(solution)/shard_map/ppermute | solution.py:84
  18.8 0.0 collective-permute-done.9.e1
  18.8 0.4 %collective-permute-start.10 = (f32[64,256]{1,0:T(8,128)S(1)}, f32[64,256]{1,0:T(8,128)S(1)}, u32[]{:S(2)}, u32[]{:S(2)}) collective-permute-start(f32[64,256]{1,0:T(8,128)S(1)} %get-tuple-element.81), channel_id=1, source_target_pairs={{0,3},{1,2},{2,1},{3,0},{4,7},{5,6},{6,5},{7,4},{8,11},{9,10},{10,... | collective-permute-start | bytes 196616 | tf_op jit(solution)/shard_map/ppermute | solution.py:84
  19.2 0.5 %collective-permute-done.7.x1 = f32[64,256]{1,0:T(8,128)S(1)} collective-permute-done((f32[64,256]{1,0:T(8,128)S(1)}, f32[64,256]{1,0:T(8,128)S(1)}, u32[]{:S(2)}, u32[]{:S(2)}) %collective-permute-start.7) | collective-permute-done | bytes 65568 | tf_op jit(solution)/shard_map/ppermute | solution.py:84
  19.7 0.8 %collective-permute-start.12 = (f32[48,256]{1,0:T(8,128)S(1)}, f32[48,256]{1,0:T(8,128)S(1)}, u32[]{:S(2)}, u32[]{:S(2)}) collective-permute-start(f32[48,256]{1,0:T(8,128)S(1)} %get-tuple-element.89.z1), channel_id=1, source_target_pairs={{0,4},{1,5},{2,6},{3,7},{4,0},{5,1},{6,2},{7,3},{8,12},{9,13},{10,... | collective-permute-start | bytes 147464 | tf_op jit(solution)/shard_map/ppermute | solution.py:84
  20.4 1.3 %collective-permute-start.13 = (f32[48,256]{1,0:T(8,128)S(1)}, f32[48,256]{1,0:T(8,128)S(1)}, u32[]{:S(2)}, u32[]{:S(2)}) collective-permute-start(f32[48,256]{1,0:T(8,128)S(1)} %get-tuple-element.90.z2), channel_id=1, source_target_pairs={{0,1},{1,0},{2,3},{3,2},{4,8},{5,9},{6,10},{7,11},{8,4},{9,5},{10,... | collective-permute-start | bytes 147464 | tf_op jit(solution)/shard_map/ppermute | solution.py:84
  21.7 1.1 %collective-permute-start.8 = (f32[32,256]{1,0:T(8,128)S(1)}, f32[32,256]{1,0:T(8,128)S(1)}, u32[]{:S(2)}, u32[]{:S(2)}) collective-permute-start(f32[32,256]{1,0:T(8,128)S(1)} %get-tuple-element.78), channel_id=1, source_target_pairs={{0,2},{1,3},{2,0},{3,1},{4,6},{5,7},{6,4},{7,5},{8,10},{9,11},{10,... | collective-permute-start | bytes 98312 | tf_op jit(solution)/shard_map/ppermute | solution.py:84
  22.8 3.1 %tin_first.1 = (f32[64,8,32,128]{3,2,1,0:T(8,128)S(1)}, f32[64,8,32,128]{3,2,1,0:T(8,128)S(1)}) custom-call(f32[64,8,32,128]{3,2,1,0:T(8,128)S(1)} %get-tuple-element.66.padded_in, s32[64,16,1024]{2,1,0:T(8,128)S(1)} %copy-done.1, f32[64,256]{1,0:T(8,128)S(1)} %collective-permute-done.x1, ...), custom_call_target="tpu_custom_call", output_to_operand_aliasing={{0}: (0, {})} | custom-call | bytes 20971520 | tf_op jit(solution)/shard_map/tin_first/pallas_call | solution.py:731
  25.9 0.5 %collective-permute-done.8.x2 = f32[32,256]{1,0:T(8,128)S(1)} collective-permute-done((f32[32,256]{1,0:T(8,128)S(1)}, f32[32,256]{1,0:T(8,128)S(1)}, u32[]{:S(2)}, u32[]{:S(2)}) %collective-permute-start.8) | collective-permute-done | bytes 32800 | tf_op jit(solution)/shard_map/ppermute | solution.py:84
  26.4 0.0 collective-permute-done.12.y1
  26.4 0.0 collective-permute-done.13.y2
  26.4 0.0 collective-permute-done.11.e2
  26.4 0.0 collective-permute-done.10.x3
  26.4 7.1 %last_sweep.1 = (f32[64,8,32,128]{3,2,1,0:T(8,128)S(1)}, f32[64,16,1024]{2,1,0:T(8,128)}, f32[48,64,256]{2,1,0:T(8,128)}) custom-call(f32[64,8,32,128]{3,2,1,0:T(8,128)S(1)} %get-tuple-element.67.padded_in, s32[64,16,1024]{2,1,0:T(8,128)S(1)} %copy-done.1, f32[16,1024]{1,0:T(8,128)S(1)} %get-tuple-element.68.plane, ...), custom_call_target="tpu_custom_call", output_to_operand_aliasing={{0}: (0, {})} | custom-call | bytes 37748736 | tf_op jit(solution)/shard_map/last_sweep/pallas_call | solution.py:784
Async XLA Ops:
  0.6 3.0 %copy-start.2 = (s32[1,48,64,256]{3,2,1,0:T(8,128)S(1)}, s32[1,48,64,256]{3,2,1,0:T(8,128)}, u32[]{:S(2)}) copy-start(s32[1,48,64,256]{3,2,1,0:T(8,128)} %ids.1) | copy-start | bytes 9437188
  0.6 3.1 %copy-start = (f32[1,48,64,256]{3,2,1,0:T(8,128)S(1)}, f32[1,48,64,256]{3,2,1,0:T(8,128)}, u32[]{:S(2)}) copy-start(f32[1,48,64,256]{3,2,1,0:T(8,128)} %floor.1) | copy-start | bytes 9437188
  2.1 6.3 %collective-permute-start.2 = (f32[64,1024]{1,0:T(8,128)S(1)}, f32[64,1024]{1,0:T(8,128)S(1)}, u32[]{:S(2)}, u32[]{:S(2)}) collective-permute-start(f32[64,1024]{1,0:T(8,128)S(1)} %get-tuple-element.57), channel_id=1, source_target_pairs={{0,1},{1,0},{2,3},{3,2},{4,5},{5,4},{6,7},{7,6},{8,9},{9,8},{10,11... | collective-permute-start | bytes 786440 | tf_op jit(solution)/shard_map/ppermute | solution.py:84
  2.2 12.0 %collective-permute-start.4 = (f32[64,1024]{1,0:T(8,128)S(1)}, f32[64,1024]{1,0:T(8,128)S(1)}, u32[]{:S(2)}, u32[]{:S(2)}) collective-permute-start(f32[64,1024]{1,0:T(8,128)S(1)} %get-tuple-element.61), channel_id=1, source_target_pairs={{0,16},{1,2},{2,1},{3,4},{4,3},{5,6},{6,5},{7,8},{8,7},{9,10},{10,... | collective-permute-start | bytes 786440 | tf_op jit(solution)/shard_map/ppermute | solution.py:84
  5.1 4.3 %collective-permute-start = (f32[64,256]{1,0:T(8,128)S(1)}, f32[64,256]{1,0:T(8,128)S(1)}, u32[]{:S(2)}, u32[]{:S(2)}) collective-permute-start(f32[64,256]{1,0:T(8,128)S(1)} %get-tuple-element.53), channel_id=1, source_target_pairs={{0,1},{1,0},{2,3},{3,2},{4,5},{5,4},{6,7},{7,6},{8,9},{9,8},{10,11... | collective-permute-start | bytes 196616 | tf_op jit(solution)/shard_map/ppermute | solution.py:84
  5.2 8.9 %collective-permute-start.5 = (f32[96,256]{1,0:T(8,128)S(1)}, f32[96,256]{1,0:T(8,128)S(1)}, u32[]{:S(2)}, u32[]{:S(2)}) collective-permute-start(f32[96,256]{1,0:T(8,128)S(1)} %get-tuple-element.63.z1), channel_id=1, source_target_pairs={{0,4},{1,5},{2,6},{3,7},{4,0},{5,1},{6,2},{7,3},{8,12},{9,13},{10,... | collective-permute-start | bytes 294920 | tf_op jit(solution)/shard_map/ppermute | solution.py:84
  5.7 8.4 %collective-permute-start.6 = (f32[96,256]{1,0:T(8,128)S(1)}, f32[96,256]{1,0:T(8,128)S(1)}, u32[]{:S(2)}, u32[]{:S(2)}) collective-permute-start(f32[96,256]{1,0:T(8,128)S(1)} %get-tuple-element.64.z2), channel_id=1, source_target_pairs={{0,1},{1,0},{2,3},{3,2},{4,8},{5,9},{6,10},{7,11},{8,4},{9,5},{10,... | collective-permute-start | bytes 294920 | tf_op jit(solution)/shard_map/ppermute | solution.py:84
  8.4 5.8 %collective-permute-start.3 = (f32[64,256]{1,0:T(8,128)S(1)}, f32[64,256]{1,0:T(8,128)S(1)}, u32[]{:S(2)}, u32[]{:S(2)}) collective-permute-start(f32[64,256]{1,0:T(8,128)S(1)} %get-tuple-element.59), channel_id=1, source_target_pairs={{0,3},{1,2},{2,1},{3,0},{4,7},{5,6},{6,5},{7,4},{8,11},{9,10},{10,... | collective-permute-start | bytes 196616 | tf_op jit(solution)/shard_map/ppermute | solution.py:84
  9.4 4.7 %collective-permute-start.1 = (f32[32,256]{1,0:T(8,128)S(1)}, f32[32,256]{1,0:T(8,128)S(1)}, u32[]{:S(2)}, u32[]{:S(2)}) collective-permute-start(f32[32,256]{1,0:T(8,128)S(1)} %get-tuple-element.56), channel_id=1, source_target_pairs={{0,2},{1,3},{2,0},{3,1},{4,6},{5,7},{6,4},{7,5},{8,10},{9,11},{10,... | collective-permute-start | bytes 98312 | tf_op jit(solution)/shard_map/ppermute | solution.py:84
  10.0 4.2 %copy-start.1 = (s32[64,16,1024]{2,1,0:T(8,128)S(1)}, s32[64,16,1024]{2,1,0:T(8,128)}, u32[]{:S(2)}) copy-start(s32[64,16,1024]{2,1,0:T(8,128)} %f.7) | copy-start | bytes 12582916
  14.9 3.9 %collective-permute-start.9 = (f32[64,1024]{1,0:T(8,128)S(1)}, f32[64,1024]{1,0:T(8,128)S(1)}, u32[]{:S(2)}, u32[]{:S(2)}) collective-permute-start(f32[64,1024]{1,0:T(8,128)S(1)} %get-tuple-element.79), channel_id=1, source_target_pairs={{0,1},{1,0},{2,3},{3,2},{4,5},{5,4},{6,7},{7,6},{8,9},{9,8},{10,11... | collective-permute-start | bytes 786440 | tf_op jit(solution)/shard_map/ppermute | solution.py:84
  15.2 11.1 %collective-permute-start.11 = (f32[64,1024]{1,0:T(8,128)S(1)}, f32[64,1024]{1,0:T(8,128)S(1)}, u32[]{:S(2)}, u32[]{:S(2)}) collective-permute-start(f32[64,1024]{1,0:T(8,128)S(1)} %get-tuple-element.83), channel_id=1, source_target_pairs={{0,16},{1,2},{2,1},{3,4},{4,3},{5,6},{6,5},{7,8},{8,7},{9,10},{10,... | collective-permute-start | bytes 786440 | tf_op jit(solution)/shard_map/ppermute | solution.py:84
  17.3 2.4 %collective-permute-start.7 = (f32[64,256]{1,0:T(8,128)S(1)}, f32[64,256]{1,0:T(8,128)S(1)}, u32[]{:S(2)}, u32[]{:S(2)}) collective-permute-start(f32[64,256]{1,0:T(8,128)S(1)} %get-tuple-element.74), channel_id=1, source_target_pairs={{0,1},{1,0},{2,3},{3,2},{4,5},{5,4},{6,7},{7,6},{8,9},{9,8},{10,11... | collective-permute-start | bytes 196616 | tf_op jit(solution)/shard_map/ppermute | solution.py:84
  18.8 7.6 %collective-permute-start.10 = (f32[64,256]{1,0:T(8,128)S(1)}, f32[64,256]{1,0:T(8,128)S(1)}, u32[]{:S(2)}, u32[]{:S(2)}) collective-permute-start(f32[64,256]{1,0:T(8,128)S(1)} %get-tuple-element.81), channel_id=1, source_target_pairs={{0,3},{1,2},{2,1},{3,0},{4,7},{5,6},{6,5},{7,4},{8,11},{9,10},{10,... | collective-permute-start | bytes 196616 | tf_op jit(solution)/shard_map/ppermute | solution.py:84
  19.7 6.7 %collective-permute-start.12 = (f32[48,256]{1,0:T(8,128)S(1)}, f32[48,256]{1,0:T(8,128)S(1)}, u32[]{:S(2)}, u32[]{:S(2)}) collective-permute-start(f32[48,256]{1,0:T(8,128)S(1)} %get-tuple-element.89.z1), channel_id=1, source_target_pairs={{0,4},{1,5},{2,6},{3,7},{4,0},{5,1},{6,2},{7,3},{8,12},{9,13},{10,... | collective-permute-start | bytes 147464 | tf_op jit(solution)/shard_map/ppermute | solution.py:84
  20.4 6.0 %collective-permute-start.13 = (f32[48,256]{1,0:T(8,128)S(1)}, f32[48,256]{1,0:T(8,128)S(1)}, u32[]{:S(2)}, u32[]{:S(2)}) collective-permute-start(f32[48,256]{1,0:T(8,128)S(1)} %get-tuple-element.90.z2), channel_id=1, source_target_pairs={{0,1},{1,0},{2,3},{3,2},{4,8},{5,9},{6,10},{7,11},{8,4},{9,5},{10,... | collective-permute-start | bytes 147464 | tf_op jit(solution)/shard_map/ppermute | solution.py:84
  21.7 4.7 %collective-permute-start.8 = (f32[32,256]{1,0:T(8,128)S(1)}, f32[32,256]{1,0:T(8,128)S(1)}, u32[]{:S(2)}, u32[]{:S(2)}) collective-permute-start(f32[32,256]{1,0:T(8,128)S(1)} %get-tuple-element.78), channel_id=1, source_target_pairs={{0,2},{1,3},{2,0},{3,1},{4,6},{5,7},{6,4},{7,5},{8,10},{9,11},{10,... | collective-permute-start | bytes 98312 | tf_op jit(solution)/shard_map/ppermute | solution.py:84
